TPU v7x, 256 devices: a whole 4x4x8 slice. The times are simulated.
256 devices in a mesh: dp: 8 (over y, core), fsdp: 32 (over x, z).
Axes of the slice: x: 4, y: 4, z: 8, core: 2. Of those that a mesh axis runs over, the one named last changes fastest.
Arguments:
- activations: bfloat16 [81920, 8192], P(('dp', 'fsdp')), may hold values from -16 to 16
- cotangent: bfloat16 [81920, 512], P(('dp', 'fsdp')), may hold values from -6 to 6
- kv_weight: bfloat16 [8192, 512], P('fsdp'), may hold values from -0.25 to 0.25
- error_buffer: float32 [8, 8192, 512], P('dp', 'fsdp'), may hold values from -6 to 6
- q_start: float32 [64, 512], replicated, may hold values from -6 to 6
Outputs:
- input_grad: bfloat16 [81920, 8192], P(('dp', 'fsdp'))
- error_next: float32 [8, 8192, 512], P('dp', 'fsdp')
- compressed: float32 [8192, 512], P('fsdp')
- q_next: float32 [64, 512], replicated
All inputs are finite; a program needn't handle non-finite values.
Results may differ from a plain program's by a relative error of at most 0.0004.
Values may be sent and summed in bfloat16 or wider, within the bound.
No kernel may reach another device: no remote copies, remote signals or barrier semaphores. Data moves between devices by JAX's collectives and lax.ppermute only.
A program may use at most 128 MiB of HBM per device.

v0:
```python
import jax
import jax.numpy as jnp
from jax import lax
from jax.sharding import PartitionSpec as P

loss_scale = 256.0


def local(activations, cotangent, kv_weight, error_buffer, q_start):
    highest = lax.Precision.HIGHEST
    input_grad = jnp.einsum(
        "tk,dk->td",
        cotangent,
        lax.all_gather(kv_weight, "fsdp", axis=0, tiled=True),
        preferred_element_type=jnp.float32,
    ).astype(jnp.bfloat16)
    gradient = lax.psum_scatter(
        jnp.einsum("td,tk->dk", activations, cotangent, preferred_element_type=jnp.float32),
        "fsdp",
        scatter_dimension=0,
        tiled=True,
    )
    merged = gradient / loss_scale + error_buffer[0]
    local_p = jnp.einsum("rk,dk->rd", q_start, merged, precision=highest)
    summed = lax.psum(local_p, "dp")
    gram_matrix = lax.psum(jnp.dot(summed, summed.T, precision=highest), "fsdp")
    factor_low = jnp.linalg.cholesky(gram_matrix)
    p_basis = lax.linalg.triangular_solve(factor_low, summed, left_side=True, lower=True)
    q_total = lax.psum(jnp.dot(p_basis, merged, precision=highest), ("dp", "fsdp"))
    q_next = q_total / lax.axis_size("dp")
    compressed = jnp.dot(p_basis.T, q_next, precision=highest)
    error_next = (merged - compressed)[None]
    return (input_grad, error_next, compressed, q_next)


def solution(mesh):
    return jax.shard_map(
        local,
        mesh=mesh,
        in_specs=(
            P(("dp", "fsdp"), None),
            P(("dp", "fsdp"), None),
            P("fsdp", None),
            P("dp", "fsdp", None),
            P(),
        ),
        out_specs=(P(("dp", "fsdp"), None), P("dp", "fsdp", None), P("fsdp", None), P()),
        check_vma=False,
    )
```

profile of v0, /device:TPU:1, one launch (start us, length us, event | category | flops | bytes accessed | tf_op | source)
XLA Modules:
  0.0 734.4 jit_solution(8424335010536417234)
XLA Ops:
  7.2 0.0 reduce-scatter.2.cloned.1.call-start
  7.2 0.9 copy-done
  8.1 10.8 %fusion.5 = f32[8192,512]{1,0:T(8,128)} fusion(bf16[320,8192]{1,0:T(8,128)(2,1)} %param.5, bf16[320,512]{1,0:T(8,128)(2,1)S(1)} %copy-done), kind=kOutput, calls=%fused_computation.16 | convolution fusion | flops 2684354560 | bytes 22347776 | tf_op jit(solution)/shard_map/td,tk->dk/dot_general | solution.py:18
  19.0 0.0 all-reduce.3.cloned.1.call-start
  19.0 244.6 %reduce-scatter.2.cloned.1.call-done = f32[256,512]{1,0:T(8,128)} async-done(((f32[8192,512]{1,0:T(8,128)}), f32[256,512]{1,0:T(8,128)}) %reduce-scatter.2.cloned.1.call-update) | async-done | bytes 524304 | tf_op jit(solution)/shard_map/reduce_scatter | solution.py:17
  263.6 2.3 convolution_bitcast_fusion
  265.9 0.0 all-gather.2.cloned.1.call-start
  266.0 0.7 all-gather.2.cloned.1.call-update
  266.6 0.0 all-reduce.5.cloned.1.call-start
  266.7 64.1 %all-reduce.3.cloned.1.call-done = f32[64,256]{1,0:T(8,128)} async-done(((f32[64,256]{1,0:T(8,128)}), f32[64,256]{1,0:T(8,128)}) %all-reduce.3.cloned.1.call-update) | async-done | bytes 65552 | tf_op jit(solution)/shard_map/psum | solution.py:25
  330.8 1.1 fusion.6
  331.9 116.6 %psum.22 = f32[64,64]{0,1:T(8,128)S(1)} all-reduce(f32[64,64]{0,1:T(8,128)S(1)} %fusion.6), channel_id=1, replica_groups=mesh['dp'=8,'fsdp'=32] {'fsdp'}, use_global_device_ids=true, to_apply=%region_2.0 | all-reduce | flops 4096 | bytes 32768 | tf_op jit(solution)/shard_map/psum | solution.py:26
  448.5 0.1 copy.10
  448.6 5.8 cholesky.16
  454.5 0.6 compare_reduce_fusion
  455.1 0.7 fusion
  455.8 4.9 custom-call.6
  460.7 1.1 fusion.1
  461.8 2.2 fusion.4
  464.0 10.7 %convolution_convert_fusion = bf16[320,8192]{1,0:T(8,128)(2,1)} fusion(bf16[320,512]{1,0:T(8,128)(2,1)S(1)} %copy-done, bf16[8192,512]{1,0:T(8,128)(2,1)} %all-gather.2.cloned.1.call-done), kind=kOutput, calls=%fused_computation | convolution fusion | flops 2686976000 | bytes 13959168 | tf_op jit(solution)/shard_map/tk,dk->td/dot_general | solution.py:11
  474.7 250.6 %all-reduce.5.cloned.1.call-done = f32[64,512]{1,0:T(8,128)} async-done(((f32[64,512]{1,0:T(8,128)}), f32[64,512]{1,0:T(8,128)}) %all-reduce.5.cloned.1.call-update) | async-done | bytes 131088 | tf_op jit(solution)/shard_map/psum | solution.py:29
  725.4 0.9 broadcast_multiply_fusion
  726.3 0.6 fusion.7
  726.9 1.0 subtract_bitcast_fusion
  (17 shorter events, 0.1 us)
Async XLA Ops:
  7.2 1.0 copy-start
  7.2 256.4 %reduce-scatter.2.cloned.1.call-start = ((), (), s32[]{:S(2)}) async-start(), calls=%async_computation.2 | async-start | bytes 17301504 | tf_op jit(solution)/shard_map/reduce_scatter | solution.py:17
  18.9 244.7 %copy-start.1 = (f32[1,256,512]{2,1,0:T(8,128)S(1)}, f32[1,256,512]{2,1,0:T(8,128)}, u32[]{:S(2)}) copy-start(f32[1,256,512]{2,1,0:T(8,128)} %param.8) | copy-start | bytes 1572868
  18.9 244.7 %copy-start.5 = (f32[64,512]{1,0:T(8,128)S(1)}, f32[64,512]{1,0:T(8,128)}, u32[]{:S(2)}) copy-start(f32[64,512]{1,0:T(8,128)} %param.9) | copy-start | bytes 393220
  19.0 311.9 %all-reduce.3.cloned.1.call-start = ((), (), s32[]{:S(2)}) async-start(), calls=%async_computation.3 | async-start | bytes 131072 | tf_op jit(solution)/shard_map/psum | solution.py:25
  265.9 198.1 %all-gather.2.cloned.1.call-start = ((), (), s32[]{:S(2)}) async-start(), calls=%async_computation.1 | async-start | bytes 8650752 | tf_op jit(solution)/shard_map/all_gather | solution.py:14
  266.6 458.7 %all-reduce.5.cloned.1.call-start = ((), (), s32[]{:S(2)}) async-start(), calls=%async_computation.4 | async-start | bytes 262144 | tf_op jit(solution)/shard_map/psum | solution.py:29
  464.0 262.9 %copy-start.2 = (f32[256,512]{1,0:T(8,128)S(1)}, f32[256,512]{1,0:T(8,128)}, u32[]{:S(2)}) copy-start(f32[256,512]{1,0:T(8,128)} %reduce-scatter.2.cloned.1.call-done) | copy-start | bytes 1572868
  726.3 1.6 copy-start.4
  726.9 1.0 copy-start.3
Sparse Core Ops, SparseCore 0:
  19.1 244.4 reduce-scatter.1
  266.5 64.2 all-reduce.2
  333.8 99.8 all-gather.1
  464.1 261.1 all-reduce.4
where the time goes:
time: 735 us; the launch traced here: 734 us
  waiting for transfers between devices  560 us (76%)
  blocking collectives  117 us (16%)
  matrix products  28.8 us (4%)
  other arithmetic  13.9 us (2%)
  between operations  13.9 us (2%)
    psum x1, waiting for transfers between devices, local(): lax.psum(jnp.dot(p_basis, merged, precision=highest), ('dp', 'fsdp'))  251 us
    reduce_scatter x1, waiting for transfers between devices, local(): lax.psum_scatter(jnp.einsum('td,tk->dk', activations, cotangent, preferre...  245 us
    psum x1, blocking collectives, local(): gram_matrix = lax.psum(jnp.dot(summed, summed.T, precision=highest), 'fsdp')  117 us
    psum x1, waiting for transfers between devices, local(): summed = lax.psum(local_p, 'dp')  64.1 us
  transfers between devices with their start and end apart: 4, of which 3 were waited for; matrix products, arithmetic and copies ran while one was open for 4% of the time, Pallas kernels for 0%

commit v1 on v0

v1 whole, which is shorter than its diff:
```python
import jax
import jax.numpy as jnp
from jax import lax
from jax.experimental import pallas as pl
from jax.experimental.pallas import tpu as pltpu
from jax.sharding import Mesh, PartitionSpec as P

LOSS_SCALE = 256.0
HIGHEST = lax.Precision.HIGHEST
F32 = jnp.float32
BF16 = jnp.bfloat16
NY, NC, NX, NZ = 4, 2, 4, 8
NT = (((1,), (1,)), ((), ()))
TN = (((0,), (0,)), ((), ()))


def swap(value, axis, size, k):
    return lax.ppermute(value, axis, [(i, i ^ k) for i in range(size)])


def swaps(value, axis, size):
    return [value] + [swap(value, axis, size, k) for k in range(1, size)]


def tree(parts):
    while len(parts) > 1:
        parts = [parts[i] + parts[i + 1] for i in range(0, len(parts), 2)]
    return parts[0]


def project_kernel(place, cot, *rest):
    pieces, out, rows, arrived = rest[:NC * NX], rest[NC * NX], rest[NC * NX + 1], rest[NC * NX + 2]
    sub = pieces[0].shape[1]
    block = NC * sub

    def fetch(k, c):
        start = pl.multiple_of((place[1] ^ c) * sub, sub)
        return pltpu.make_async_copy(
            pieces[NC * k + c], rows.at[k, :, pl.ds(start, sub), :], arrived.at[NC * k + c]
        )

    @pl.when(pl.program_id(0) == 0)
    def _():
        for k in range(NX):
            for c in range(NC):
                fetch(k, c).start()

    for k in range(NX):
        @pl.when(pl.program_id(0) == k)
        def _():
            for c in range(NC):
                fetch(k, c).wait()
            for z in range(NZ):
                out[:, z * block:(z + 1) * block] = lax.dot_general(
                    cot[...], rows[k, z], NT, preferred_element_type=F32
                ).astype(BF16)


def project(place, cot, pieces):
    tokens, width = cot.shape
    sub = pieces[0].shape[1]
    columns = NZ * NC * sub
    return pl.pallas_call(
        project_kernel,
        out_shape=jax.ShapeDtypeStruct((tokens, NX * columns), BF16),
        grid_spec=pltpu.PrefetchScalarGridSpec(
            num_scalar_prefetch=1,
            grid=(NX,),
            in_specs=[pl.BlockSpec((tokens, width), lambda k, place: (0, 0))]
            + [pl.BlockSpec(memory_space=pl.ANY)] * (NC * NX),
            out_specs=pl.BlockSpec((tokens, columns), lambda k, place: (0, k ^ place[0])),
            scratch_shapes=[pltpu.VMEM((NX, NZ, NC * sub, width), BF16), pltpu.SemaphoreType.DMA((NC * NX,))],
        ),
        cost_estimate=pl.CostEstimate(
            flops=2 * tokens * width * NX * columns,
            bytes_accessed=2 * (tokens + width) * NX * columns,
            transcendentals=0,
        ),
        compiler_params=pltpu.CompilerParams(vmem_limit_bytes=40 * 1024 * 1024),
        name="project",
    )(place, cot, *pieces)


def right_kernel(place, _, gradient, error, p_total, merged_out, keep, give):
    half = keep.shape[0]
    merged = gradient[...] * (1.0 / LOSS_SCALE) + error[...]
    merged_out[...] = merged
    p = p_total[...]
    right = jnp.dot(p, merged, precision=HIGHEST, preferred_element_type=F32)
    gram = lax.dot_general(p, p, NT, precision=HIGHEST, preferred_element_type=F32) * (1.0 / (NY * NC))
    sums = jnp.concatenate([right, gram], axis=1)
    first = place[1] == 0
    keep[...] = jnp.where(first, sums[:half], sums[half:])
    give[...] = jnp.where(first, sums[half:], sums[:half])


def right_terms(place, after, gradient, error, p_total):
    rank, width = p_total.shape[0], gradient.shape[1]
    half = jax.ShapeDtypeStruct((rank // NC, width + rank), F32)
    return pl.pallas_call(
        right_kernel,
        out_shape=(jax.ShapeDtypeStruct(gradient.shape, F32), half, half),
        in_specs=[pl.BlockSpec(memory_space=pltpu.SMEM), pl.BlockSpec(memory_space=pltpu.HBM)]
        + [pl.BlockSpec(memory_space=pltpu.VMEM)] * 3,
        compiler_params=pltpu.CompilerParams(vmem_limit_bytes=32 * 1024 * 1024),
        name="right_terms",
    )(place, after, gradient, error, p_total)


def finish_kernel(place, mine, other, p_total, merged, error_out, compressed_out, q_out):
    rank, width = p_total.shape[0], merged.shape[1]
    first = place[1] == 0
    sums = jnp.concatenate([jnp.where(first, mine[...], other[...]), jnp.where(first, other[...], mine[...])], axis=0)
    gram = sums[:, width:]
    row = lax.broadcasted_iota(jnp.int32, (rank, 2 * rank), 0)
    col = lax.broadcasted_iota(jnp.int32, (rank, 2 * rank), 1)
    work = jnp.concatenate([gram, jnp.zeros_like(gram)], axis=1)
    work = jnp.where(col == row + rank, 1.0, work)
    scale = jnp.zeros((rank, 1), F32)
    row1 = lax.broadcasted_iota(jnp.int32, (rank, 1), 0)
    for k in range(rank):
        pivot = work[k:k + 1, k:k + 1]
        ratio = jnp.where(row1 > k, work[:, k:k + 1] * (1.0 / pivot), 0.0)
        scale = jnp.where(row1 == k, lax.rsqrt(pivot), scale)
        work = work - ratio * work[k:k + 1, :]
    inverse = work[:, rank:] * scale
    q_next = jnp.dot(inverse, sums[:, :width], precision=HIGHEST, preferred_element_type=F32) * (1.0 / (NY * NC))
    p_basis = jnp.dot(inverse, p_total[...], precision=HIGHEST, preferred_element_type=F32)
    compressed = lax.dot_general(p_basis, q_next, TN, precision=HIGHEST, preferred_element_type=F32)
    q_out[...] = q_next
    compressed_out[...] = compressed
    error_out[...] = merged[...] - compressed


def finish(place, mine, other, p_total, merged):
    rank = p_total.shape[0]
    return pl.pallas_call(
        finish_kernel,
        out_shape=(
            jax.ShapeDtypeStruct(merged.shape, F32),
            jax.ShapeDtypeStruct(merged.shape, F32),
            jax.ShapeDtypeStruct((rank, merged.shape[1]), F32),
        ),
        in_specs=[pl.BlockSpec(memory_space=pltpu.SMEM)] + [pl.BlockSpec(memory_space=pltpu.VMEM)] * 4,
        compiler_params=pltpu.CompilerParams(vmem_limit_bytes=32 * 1024 * 1024),
        name="finish",
    )(place, mine, other, p_total, merged)


def thirds(value):
    parts = []
    for _ in range(3):
        part = lax.reduce_precision(value, 8, 7)
        parts.append(part.astype(BF16))
        value = value - part
    return jnp.concatenate(parts, axis=0)


def local(activations, cotangent, kv_weight, error_buffer, q_start):
    y, c, x, z = (lax.axis_index(a) for a in "ycxz")
    place = jnp.stack([x, c]).astype(jnp.int32)
    rank = q_start.shape[0]
    tokens = cotangent.shape[0]
    error = error_buffer[0]

    with jax.named_scope("exchange"):
        sub = kv_weight.shape[0] // NC
        mine = lax.dynamic_slice_in_dim(kv_weight, c * sub, sub, axis=0)
        line = lax.all_gather(mine, "z", axis=0)
        cot_x = jnp.zeros((NX * tokens, cotangent.shape[1]), BF16)
        for k, piece in enumerate(swaps(cotangent, "x", NX)):
            cot_x = lax.dynamic_update_slice_in_dim(cot_x, piece, (x ^ k) * tokens, axis=0)
        act_x = lax.all_to_all(activations, "x", 1, 0, tiled=True)

    with jax.named_scope("gradient"):
        part = jnp.einsum("td,tk->dk", act_x, cot_x, preferred_element_type=F32)
        part, line, act_x, cot_x = lax.optimization_barrier((part, line, act_x, cot_x))
        gradient = lax.psum_scatter(part, "z", scatter_dimension=0, tiled=True)

    with jax.named_scope("weight"):
        pieces = []
        for piece in swaps(line, "x", NX):
            pieces += [piece, swap(piece, "c", NC, 1)]
        input_grad = project(place, cotangent, pieces)

    with jax.named_scope("left"):
        q_cot = jnp.einsum("rk,tk->rt", q_start, cot_x.astype(F32), precision=HIGHEST)
        p_part = jnp.dot(thirds(q_cot), act_x, preferred_element_type=F32)
        p_part = p_part[:rank] + p_part[rank:2 * rank] + p_part[2 * rank:]
        p_part = lax.all_to_all(p_part, "z", 1, 0, tiled=True).reshape(NZ, rank, -1)
        p_own = jnp.einsum("rk,dk->rd", q_start, error, precision=HIGHEST)
        p_total = tree([p_part[i] for i in range(NZ)]) * (1.0 / LOSS_SCALE) + p_own
        p_total = tree(swaps(p_total, "c", NC))
        p_total = tree(swaps(p_total, "y", NY))

    with jax.named_scope("sums"):
        merged, keep, give = right_terms(place, input_grad[:16, :128], gradient, error, p_total)
        keep = keep + swap(give, "c", NC, 1)
        keep = tree(swaps(keep, "y", NY))
        keep = tree(swaps(keep, "x", NX))
        keep = keep + swap(keep, "z", NZ, 1)
        keep = tree([keep] + [swap(keep, "z", NZ, k) for k in (2, 4, 6)])
        other = swap(keep, "c", NC, 1)

    with jax.named_scope("finish"):
        error_next, compressed, q_next = finish(place, keep, other, p_total, merged)
    return (input_grad, error_next[None], compressed, q_next)


def solution(mesh):
    fine = Mesh(mesh.devices.reshape(NY, NC, NX, NZ), ("y", "c", "x", "z"))
    dp, fsdp = ("y", "c"), ("x", "z")
    return jax.shard_map(
        local,
        mesh=fine,
        in_specs=(P(dp + fsdp, None), P(dp + fsdp, None), P(fsdp, None), P(dp, fsdp, None), P()),
        out_specs=(P(dp + fsdp, None), P(dp, fsdp, None), P(fsdp, None), P()),
        check_vma=False,
    )
```

time: 735 us -> 238 us (0.32)
  waiting for transfers between devices: 560 us -> 118 us
  blocking collectives: 117 us -> 0 us
  starting transfers between devices: 0.16 us -> 62.2 us
  Pallas kernels: 0 us -> 16.1 us
  other arithmetic: 13.9 us -> 0.27 us
  matrix products: 28.8 us -> 16.8 us
  local copies, waits for them, and re-layouts: 1.02 us -> 10.4 us
    psum x2 -> x0, waiting for transfers between devices: 315 us -> none  [the longest x1 251 us: local(): lax.psum(jnp.dot(p_basis, merged, precision=highest), ('dp', 'fsdp'))]
    reduce_scatter x1, waiting for transfers between devices: 245 us -> 0.01 us  [local(): gradient = lax.psum_scatter(part, 'z', scatter_dimension=0, tiled=True)]
    ppermute x0 -> x26, waiting for transfers between devices: none -> 118 us  [swap(): return lax.ppermute(value, axis, [(i, i ^ k) for i in range(size)])]
    psum x1 -> x0, blocking collectives: 117 us -> none  [local(): gram_matrix = lax.psum(jnp.dot(summed, summed.T, precision=highest), 'fsdp')]
    ppermute x0 -> x26, starting transfers between devices: none -> 46.4 us  [swap(): return lax.ppermute(value, axis, [(i, i ^ k) for i in range(size)])]
    pallas_call x0 -> x3, Pallas kernels: none -> 16.1 us  [the longest x1 8.33 us: finish(): pl.pallas_call(finish_kernel, out_shape=(jax.ShapeDtypeStruct(merged.shap...]
    all_to_all x0 -> x2, starting transfers between devices: none -> 15.7 us  [the longest x1 10.5 us: local(): p_part = lax.all_to_all(p_part, 'z', 1, 0, tiled=True).reshape(NZ, rank, -1)]
    another operation x5 -> x1, other arithmetic: 12.1 us -> 0.07 us  [local(): place = jnp.stack([x, c]).astype(jnp.int32)]
  transfers between devices with their start and end apart: 4 -> 30, of which waited for: 3 -> 17; matrix products, arithmetic and copies ran while one was open for 4% -> 8% of each run, Pallas kernels for 0% -> 3%
where the time goes in v1:
time: 238 us
  waiting for transfers between devices  118 us (50%)
  starting transfers between devices  62.2 us (26%)
  matrix products  16.8 us (7%)
  Pallas kernels  16.1 us (7%)
  between operations  14.3 us (6%)
  local copies, waits for them, and re-layouts  10.4 us (4%)
    ppermute x26, waiting for transfers between devices, swap(): return lax.ppermute(value, axis, [(i, i ^ k) for i in range(size)])  118 us
    ppermute x26, starting transfers between devices, swap(): return lax.ppermute(value, axis, [(i, i ^ k) for i in range(size)])  46.4 us
    all_to_all x1, starting transfers between devices, local(): p_part = lax.all_to_all(p_part, 'z', 1, 0, tiled=True).reshape(NZ, rank, -1)  10.5 us
    dot_general x1, matrix products, local(): part = jnp.einsum('td,tk->dk', act_x, cot_x, preferred_element_type=F32)  8.74 us
    pallas_call x1, Pallas kernels, finish(): pl.pallas_call(finish_kernel, out_shape=(jax.ShapeDtypeStruct(merged.shap...  8.33 us
    pallas_call x1, Pallas kernels, project(): pl.pallas_call(project_kernel, out_shape=jax.ShapeDtypeStruct((tokens, NX...  6.76 us
    all_to_all x1, local copies, waits for them, and re-layouts, local(): act_x = lax.all_to_all(activations, 'x', 1, 0, tiled=True)  5.74 us
    all_to_all x1, starting transfers between devices, local(): act_x = lax.all_to_all(activations, 'x', 1, 0, tiled=True)  5.21 us
  transfers between devices with their start and end apart: 30, of which 17 were waited for; matrix products, arithmetic and copies ran while one was open for 8% of the time, Pallas kernels for 3%

profile of v1, /device:TPU:1, one launch (start us, length us, event | category | flops | bytes accessed | tf_op | source)
XLA Modules:
  0.0 237.8 jit_solution(9769533872662259756)
XLA Ops:
  7.2 5.7 %copy.23 = bf16[40,4,8,2048]{3,2,0,1:T(8,128)(2,1)} copy(bf16[40,4,8,2048]{3,2,1,0:T(8,128)(2,1)} %bitcast.40) | data formatting | bytes 10485760 | tf_op jit(solution)/shard_map/exchange/all_to_all | solution.py:173
  12.9 5.2 %all-to-all-start = ((bf16[320,4,2048]{2,0,1:T(8,128)(2,1)}), bf16[320,4,2048]{2,0,1:T(8,128)(2,1)}, u32[]{:S(2)}, u32[]{:S(2)}) async-start(bf16[320,4,2048]{2,0,1:T(8,128)(2,1)} %bitcast.39), calls=%async_computation | async-start | bytes 10485760 | tf_op jit(solution)/shard_map/exchange/all_to_all | solution.py:173
  21.1 2.5 %collective-permute-start.1 = (bf16[320,512]{1,0:T(8,128)(2,1)S(1)}, bf16[320,512]{1,0:T(8,128)(2,1)S(1)}, u32[]{:S(2)}, u32[]{:S(2)}) collective-permute-start(bf16[320,512]{1,0:T(8,128)(2,1)S(1)} %copy-done.2), channel_id=1, source_target_pairs={{0,16},{8,24},{16,0},{24,8},{1,17},{9,25},{17,1},{25,9},{2,18},{10... | collective-permute-start | bytes 983048 | tf_op jit(solution)/shard_map/exchange/ppermute | solution.py:18
  23.7 58.1 %collective-permute-done = bf16[320,512]{1,0:T(8,128)(2,1)S(1)} collective-permute-done((bf16[320,512]{1,0:T(8,128)(2,1)S(1)}, bf16[320,512]{1,0:T(8,128)(2,1)S(1)}, u32[]{:S(2)}, u32[]{:S(2)}) %collective-permute-start) | collective-permute-done | bytes 327712 | tf_op jit(solution)/shard_map/exchange/ppermute | solution.py:18
  81.8 8.4 %collective-permute-done.1 = bf16[320,512]{1,0:T(8,128)(2,1)S(1)} collective-permute-done((bf16[320,512]{1,0:T(8,128)(2,1)S(1)}, bf16[320,512]{1,0:T(8,128)(2,1)S(1)}, u32[]{:S(2)}, u32[]{:S(2)}) %collective-permute-start.1) | collective-permute-done | bytes 327712 | tf_op jit(solution)/shard_map/exchange/ppermute | solution.py:18
  90.3 8.7 %convolution_bitcast_fusion = f32[2048,512]{1,0:T(8,128)} fusion(bf16[1280,512]{1,0:T(8,128)(2,1)S(1)} %constant_dynamic-update-slice_fusion, bf16[1280,2048]{1,0:T(8,128)(2,1)} %bitcast.3), kind=kOutput, calls=%fused_computation.1 | convolution fusion | flops 2684354560 | bytes 10747904 | tf_op jit(solution)/shard_map/gradient/td,tk->dk/dot_general | solution.py:176
  103.5 2.6 %reduce-precision_convert_fusion.1 = (bf16[64,1280]{1,0:T(8,128)(2,1)S(1)}, bf16[64,1280]{1,0:T(8,128)(2,1)S(1)}, bf16[64,1280]{1,0:T(8,128)(2,1)S(1)}) fusion(bf16[1280,512]{1,0:T(8,128)(2,1)} %copy-done.5, f32[64,512]{1,0:T(8,128)S(1)} %copy-done.6), kind=kOutput, calls=%fused_computation.16 | convolution fusion | flops 503971840 | bytes 1933312 | tf_op jit(solution)/shard_map/left/rk,tk->rt/dot_general | solution.py:187
  106.1 3.7 %fusion = f32[192,2048]{1,0:T(8,128)S(1)} fusion(bf16[1280,2048]{1,0:T(8,128)(2,1)} %bitcast.3, bf16[64,1280]{1,0:T(8,128)(2,1)S(1)} %get-tuple-element.25, bf16[64,1280]{1,0:T(8,128)(2,1)S(1)} %get-tuple-element.26, bf16[64,1280]{1,0:T(8,128)(2,1)S(1)} %get-tuple-element.24), kind=kOutput, calls=%fused_computation.7 | convolution fusion | flops 1008107520 | bytes 7307264 | tf_op jit(solution)/shard_map/left/dot_general | solution.py:188
  110.8 10.5 %all-to-all-start.1 = ((f32[64,8,256]{2,0,1:T(8,128)}), f32[64,8,256]{2,0,1:T(8,128)}, u32[]{:S(2)}, u32[]{:S(2)}) async-start(f32[64,8,256]{2,0,1:T(8,128)} %bitcast.41), calls=%async_computation.2 | async-start | bytes 1048576 | tf_op jit(solution)/shard_map/left/all_to_all | solution.py:190
  121.3 2.7 %collective-permute-start.3 = (bf16[8,128,512]{2,1,0:T(8,128)(2,1)S(1)}, bf16[8,128,512]{2,1,0:T(8,128)(2,1)}, u32[]{:S(2)}, u32[]{:S(2)}) collective-permute-start(bf16[8,128,512]{2,1,0:T(8,128)(2,1)S(1)} %bitcast.37), channel_id=1, source_target_pairs={{0,32},{32,0},{1,33},{33,1},{2,34},{34,2},{3,35},{35,3},{4,36},{36... | collective-permute-start | bytes 3145736 | tf_op jit(solution)/shard_map/weight/ppermute | solution.py:18
  124.0 23.9 %collective-permute-done.8.rest_6_ = bf16[8,128,512]{2,1,0:T(8,128)(2,1)S(1)} collective-permute-done((bf16[8,128,512]{2,1,0:T(8,128)(2,1)S(1)}, bf16[8,128,512]{2,1,0:T(8,128)(2,1)S(1)}, u32[]{:S(2)}, u32[]{:S(2)}) %collective-permute-start.8) | collective-permute-done | bytes 1048608 | tf_op jit(solution)/shard_map/weight/ppermute | solution.py:18
  152.0 2.7 %collective-permute-done.10 = f32[64,256]{1,0:T(8,128)S(1)} collective-permute-done((f32[64,256]{1,0:T(8,128)S(1)}, f32[64,256]{1,0:T(8,128)S(1)}, u32[]{:S(2)}, u32[]{:S(2)}) %collective-permute-start.10) | collective-permute-done | bytes 65568 | tf_op jit(solution)/shard_map/left/ppermute | solution.py:18
  154.7 5.3 %collective-permute-start.13 = (f32[64,256]{1,0:T(8,128)S(1)}, f32[64,256]{1,0:T(8,128)S(1)}, u32[]{:S(2)}, u32[]{:S(2)}) collective-permute-start(f32[64,256]{1,0:T(8,128)S(1)} %add.114), channel_id=1, source_target_pairs={{0,192},{64,128},{128,64},{192,0},{1,193},{65,129},{129,65},{193,1... | collective-permute-start | bytes 196616 | tf_op jit(solution)/shard_map/left/ppermute | solution.py:18
  160.0 2.4 %collective-permute-done.13 = f32[64,256]{1,0:T(8,128)S(1)} collective-permute-done((f32[64,256]{1,0:T(8,128)S(1)}, f32[64,256]{1,0:T(8,128)S(1)}, u32[]{:S(2)}, u32[]{:S(2)}) %collective-permute-start.13) | collective-permute-done | bytes 65568 | tf_op jit(solution)/shard_map/left/ppermute | solution.py:18
  163.9 3.2 %collective-permute-done.12 = f32[64,256]{1,0:T(8,128)S(1)} collective-permute-done((f32[64,256]{1,0:T(8,128)S(1)}, f32[64,256]{1,0:T(8,128)S(1)}, u32[]{:S(2)}, u32[]{:S(2)}) %collective-permute-start.12) | collective-permute-done | bytes 65568 | tf_op jit(solution)/shard_map/left/ppermute | solution.py:18
  167.6 2.6 %collective-permute-done.11 = f32[64,256]{1,0:T(8,128)S(1)} collective-permute-done((f32[64,256]{1,0:T(8,128)S(1)}, f32[64,256]{1,0:T(8,128)S(1)}, u32[]{:S(2)}, u32[]{:S(2)}) %collective-permute-start.11) | collective-permute-done | bytes 65568 | tf_op jit(solution)/shard_map/left/ppermute | solution.py:18
  170.3 6.8 %project.1 = bf16[320,8192]{1,0:T(8,128)(2,1)} custom-call(s32[2]{0:T(128)S(1)} %pad_add_fusion.place, bf16[320,512]{1,0:T(8,128)(2,1)S(1)} %copy-done.2, bf16[8,128,512]{2,1,0:T(8,128)(2,1)S(1)} %bitcast.38, bf16[8,128,512]{2,1,0:T(8,128)(2,1)} %collective-permute-done.3.rest_1_, bf16[8,128,512]{2,1,0:T(8,128)(2,1)} %collective-permute-done.4.rest_2_, ...), custom_call_target="tpu_custom_call" | custom-call | flops 2684354560 | bytes 13631488 | tf_op jit(solution)/shard_map/weight/project/pallas_call | solution.py:63
  179.8 3.0 %collective-permute-start.14 = (f32[32,576]{1,0:T(8,128)S(1)}, f32[32,576]{1,0:T(8,128)S(1)}, u32[]{:S(2)}, u32[]{:S(2)}) collective-permute-start(f32[32,576]{1,0:T(8,128)S(1)} %get-tuple-element.19), channel_id=1, source_target_pairs={{0,32},{32,0},{1,33},{33,1},{2,34},{34,2},{3,35},{35,3},{4,36},{36... | collective-permute-start | bytes 221192 | tf_op jit(solution)/shard_map/sums/ppermute | solution.py:18
  183.8 2.8 %collective-permute-start.17 = (f32[32,576]{1,0:T(8,128)S(1)}, f32[32,576]{1,0:T(8,128)S(1)}, u32[]{:S(2)}, u32[]{:S(2)}) collective-permute-start(f32[32,576]{1,0:T(8,128)S(1)} %add.118), channel_id=1, source_target_pairs={{0,192},{64,128},{128,64},{192,0},{1,193},{65,129},{129,65},{193,1... | collective-permute-start | bytes 221192 | tf_op jit(solution)/shard_map/sums/ppermute | solution.py:18
  187.2 2.3 collective-permute-done.17
  201.0 6.0 %collective-permute-start.24 = (f32[32,576]{1,0:T(8,128)S(1)}, f32[32,576]{1,0:T(8,128)S(1)}, u32[]{:S(2)}, u32[]{:S(2)}) collective-permute-start(f32[32,576]{1,0:T(8,128)S(1)} %add.125), channel_id=1, source_target_pairs={{0,6},{1,7},{2,4},{3,5},{4,2},{5,3},{6,0},{7,1},{8,14},{9,15},{10,... | collective-permute-start | bytes 221192 | tf_op jit(solution)/shard_map/sums/ppermute | solution.py:18
  209.3 5.8 %collective-permute-done.23 = f32[32,576]{1,0:T(8,128)S(1)} collective-permute-done((f32[32,576]{1,0:T(8,128)S(1)}, f32[32,576]{1,0:T(8,128)S(1)}, u32[]{:S(2)}, u32[]{:S(2)}) %collective-permute-start.23) | collective-permute-done | bytes 73760 | tf_op jit(solution)/shard_map/sums/ppermute | solution.py:18
  215.1 6.6 %collective-permute-start.25 = (f32[32,576]{1,0:T(8,128)S(1)}, f32[32,576]{1,0:T(8,128)S(1)}, u32[]{:S(2)}, u32[]{:S(2)}) collective-permute-start(f32[32,576]{1,0:T(8,128)S(1)} %add_add_fusion.mine), channel_id=1, source_target_pairs={{0,32},{32,0},{1,33},{33,1},{2,34},{34,2},{3,35},{35,3},{4,36},{36... | collective-permute-start | bytes 221192 | tf_op jit(solution)/shard_map/sums/ppermute | solution.py:18
  222.6 8.3 %finish.1 = (f32[256,512]{1,0:T(8,128)}, f32[256,512]{1,0:T(8,128)}, f32[64,512]{1,0:T(8,128)}) custom-call(s32[2]{0:T(128)S(1)} %pad_add_fusion.place, f32[32,576]{1,0:T(8,128)S(1)} %add_add_fusion.mine, f32[32,576]{1,0:T(8,128)S(1)} %collective-permute-done.25.other, f32[64,256]{1,0:T(8,128)S(1)} %add_add_fusion.3.p_total, ...), custom_call_target="tpu_custom_call" | custom-call | tf_op jit(solution)/shard_map/finish/finish/pallas_call | solution.py:137
  (77 shorter events, 33.7 us)
Async XLA Ops:
  12.9 77.3 %all-to-all-start = ((bf16[320,4,2048]{2,0,1:T(8,128)(2,1)}), bf16[320,4,2048]{2,0,1:T(8,128)(2,1)}, u32[]{:S(2)}, u32[]{:S(2)}) async-start(bf16[320,4,2048]{2,0,1:T(8,128)(2,1)} %bitcast.39), calls=%async_computation | async-start | bytes 10485760 | tf_op jit(solution)/shard_map/exchange/all_to_all | solution.py:173
  18.1 80.9 %all-gather.3.cloned.1.call-start = ((), (), s32[]{:S(2)}) async-start(), calls=%async_computation.4 | async-start | bytes 1179648 | tf_op jit(solution)/shard_map/exchange/all_gather | solution.py:169
  18.9 158.8 %reduce-scatter.2.cloned.1.call-start = ((), (), s32[]{:S(2)}) async-start(), calls=%async_computation.3 | async-start | bytes 4718592 | tf_op jit(solution)/shard_map/gradient/reduce_scatter | solution.py:178
  19.0 62.8 %collective-permute-start = (bf16[320,512]{1,0:T(8,128)(2,1)S(1)}, bf16[320,512]{1,0:T(8,128)(2,1)S(1)}, u32[]{:S(2)}, u32[]{:S(2)}) collective-permute-start(bf16[320,512]{1,0:T(8,128)(2,1)S(1)} %copy-done.2), channel_id=1, source_target_pairs={{0,8},{8,0},{16,24},{24,16},{1,9},{9,1},{17,25},{25,17},{2,10},{10... | collective-permute-start | bytes 983048 | tf_op jit(solution)/shard_map/exchange/ppermute | solution.py:18
  21.1 69.1 %collective-permute-start.1 = (bf16[320,512]{1,0:T(8,128)(2,1)S(1)}, bf16[320,512]{1,0:T(8,128)(2,1)S(1)}, u32[]{:S(2)}, u32[]{:S(2)}) collective-permute-start(bf16[320,512]{1,0:T(8,128)(2,1)S(1)} %copy-done.2), channel_id=1, source_target_pairs={{0,16},{8,24},{16,0},{24,8},{1,17},{9,25},{17,1},{25,9},{2,18},{10... | collective-permute-start | bytes 983048 | tf_op jit(solution)/shard_map/exchange/ppermute | solution.py:18
  23.5 66.7 %collective-permute-start.2 = (bf16[320,512]{1,0:T(8,128)(2,1)S(1)}, bf16[320,512]{1,0:T(8,128)(2,1)S(1)}, u32[]{:S(2)}, u32[]{:S(2)}) collective-permute-start(bf16[320,512]{1,0:T(8,128)(2,1)S(1)} %copy-done.2), channel_id=1, source_target_pairs={{0,24},{8,16},{16,8},{24,0},{1,25},{9,17},{17,9},{25,1},{2,26},{10... | collective-permute-start | bytes 983048 | tf_op jit(solution)/shard_map/exchange/ppermute | solution.py:18
  100.2 47.6 %collective-permute-start.8 = (bf16[8,128,512]{2,1,0:T(8,128)(2,1)S(1)}, bf16[8,128,512]{2,1,0:T(8,128)(2,1)S(1)}, u32[]{:S(2)}, u32[]{:S(2)}) collective-permute-start(bf16[8,128,512]{2,1,0:T(8,128)(2,1)S(1)} %bitcast.34), channel_id=1, source_target_pairs={{0,24},{8,16},{16,8},{24,0},{1,25},{9,17},{17,9},{25,1},{2,26},{10... | collective-permute-start | bytes 3145736 | tf_op jit(solution)/shard_map/weight/ppermute | solution.py:18
  101.1 48.4 %collective-permute-start.6 = (bf16[8,128,512]{2,1,0:T(8,128)(2,1)S(1)}, bf16[8,128,512]{2,1,0:T(8,128)(2,1)}, u32[]{:S(2)}, u32[]{:S(2)}) collective-permute-start(bf16[8,128,512]{2,1,0:T(8,128)(2,1)S(1)} %bitcast.35), channel_id=1, source_target_pairs={{0,16},{8,24},{16,0},{24,8},{1,17},{9,25},{17,1},{25,9},{2,18},{10... | collective-permute-start | bytes 3145736 | tf_op jit(solution)/shard_map/weight/ppermute | solution.py:18
  102.4 47.1 %collective-permute-start.4 = (bf16[8,128,512]{2,1,0:T(8,128)(2,1)S(1)}, bf16[8,128,512]{2,1,0:T(8,128)(2,1)}, u32[]{:S(2)}, u32[]{:S(2)}) collective-permute-start(bf16[8,128,512]{2,1,0:T(8,128)(2,1)S(1)} %bitcast.36), channel_id=1, source_target_pairs={{0,8},{8,0},{16,24},{24,16},{1,9},{9,1},{17,25},{25,17},{2,10},{10... | collective-permute-start | bytes 3145736 | tf_op jit(solution)/shard_map/weight/ppermute | solution.py:18
  110.8 39.4 %all-to-all-start.1 = ((f32[64,8,256]{2,0,1:T(8,128)}), f32[64,8,256]{2,0,1:T(8,128)}, u32[]{:S(2)}, u32[]{:S(2)}) async-start(f32[64,8,256]{2,0,1:T(8,128)} %bitcast.41), calls=%async_computation.2 | async-start | bytes 1048576 | tf_op jit(solution)/shard_map/left/all_to_all | solution.py:190
  121.3 48.9 %collective-permute-start.3 = (bf16[8,128,512]{2,1,0:T(8,128)(2,1)S(1)}, bf16[8,128,512]{2,1,0:T(8,128)(2,1)}, u32[]{:S(2)}, u32[]{:S(2)}) collective-permute-start(bf16[8,128,512]{2,1,0:T(8,128)(2,1)S(1)} %bitcast.37), channel_id=1, source_target_pairs={{0,32},{32,0},{1,33},{33,1},{2,34},{34,2},{3,35},{35,3},{4,36},{36... | collective-permute-start | bytes 3145736 | tf_op jit(solution)/shard_map/weight/ppermute | solution.py:18
  147.8 22.4 %collective-permute-start.9 = (bf16[8,128,512]{2,1,0:T(8,128)(2,1)S(1)}, bf16[8,128,512]{2,1,0:T(8,128)(2,1)}, u32[]{:S(2)}, u32[]{:S(2)}) collective-permute-start(bf16[8,128,512]{2,1,0:T(8,128)(2,1)S(1)} %collective-permute-done.8.rest_6_), channel_id=1, source_target_pairs={{0,32},{32,0},{1,33},{33,1},{2,34},{34,2},{3,35},{35,3},{4,36},{36... | collective-permute-start | bytes 3145736 | tf_op jit(solution)/shard_map/weight/ppermute | solution.py:18
  149.5 20.8 %collective-permute-start.7 = (bf16[8,128,512]{2,1,0:T(8,128)(2,1)}, bf16[8,128,512]{2,1,0:T(8,128)(2,1)}, u32[]{:S(2)}, u32[]{:S(2)}) collective-permute-start(bf16[8,128,512]{2,1,0:T(8,128)(2,1)} %collective-permute-done.6.rest_4_), channel_id=1, source_target_pairs={{0,32},{32,0},{1,33},{33,1},{2,34},{34,2},{3,35},{35,3},{4,36},{36... | collective-permute-start | bytes 3145736 | tf_op jit(solution)/shard_map/weight/ppermute | solution.py:18
  149.5 20.8 %collective-permute-start.5 = (bf16[8,128,512]{2,1,0:T(8,128)(2,1)}, bf16[8,128,512]{2,1,0:T(8,128)(2,1)}, u32[]{:S(2)}, u32[]{:S(2)}) collective-permute-start(bf16[8,128,512]{2,1,0:T(8,128)(2,1)} %collective-permute-done.4.rest_2_), channel_id=1, source_target_pairs={{0,32},{32,0},{1,33},{33,1},{2,34},{34,2},{3,35},{35,3},{4,36},{36... | collective-permute-start | bytes 3145736 | tf_op jit(solution)/shard_map/weight/ppermute | solution.py:18
  154.7 7.7 %collective-permute-start.13 = (f32[64,256]{1,0:T(8,128)S(1)}, f32[64,256]{1,0:T(8,128)S(1)}, u32[]{:S(2)}, u32[]{:S(2)}) collective-permute-start(f32[64,256]{1,0:T(8,128)S(1)} %add.114), channel_id=1, source_target_pairs={{0,192},{64,128},{128,64},{192,0},{1,193},{65,129},{129,65},{193,1... | collective-permute-start | bytes 196616 | tf_op jit(solution)/shard_map/left/ppermute | solution.py:18
  183.8 5.7 %collective-permute-start.17 = (f32[32,576]{1,0:T(8,128)S(1)}, f32[32,576]{1,0:T(8,128)S(1)}, u32[]{:S(2)}, u32[]{:S(2)}) collective-permute-start(f32[32,576]{1,0:T(8,128)S(1)} %add.118), channel_id=1, source_target_pairs={{0,192},{64,128},{128,64},{192,0},{1,193},{65,129},{129,65},{193,1... | collective-permute-start | bytes 221192 | tf_op jit(solution)/shard_map/sums/ppermute | solution.py:18
  186.5 4.8 %collective-permute-start.16 = (f32[32,576]{1,0:T(8,128)S(1)}, f32[32,576]{1,0:T(8,128)S(1)}, u32[]{:S(2)}, u32[]{:S(2)}) collective-permute-start(f32[32,576]{1,0:T(8,128)S(1)} %add.118), channel_id=1, source_target_pairs={{0,128},{64,192},{128,0},{192,64},{1,129},{65,193},{129,1},{193,65... | collective-permute-start | bytes 221192 | tf_op jit(solution)/shard_map/sums/ppermute | solution.py:18
  186.5 4.8 %collective-permute-start.15 = (f32[32,576]{1,0:T(8,128)S(1)}, f32[32,576]{1,0:T(8,128)S(1)}, u32[]{:S(2)}, u32[]{:S(2)}) collective-permute-start(f32[32,576]{1,0:T(8,128)S(1)} %add.118), channel_id=1, source_target_pairs={{0,64},{64,0},{128,192},{192,128},{1,65},{65,1},{129,193},{193,129... | collective-permute-start | bytes 221192 | tf_op jit(solution)/shard_map/sums/ppermute | solution.py:18
  192.3 4.8 %collective-permute-start.19 = (f32[32,576]{1,0:T(8,128)S(1)}, f32[32,576]{1,0:T(8,128)S(1)}, u32[]{:S(2)}, u32[]{:S(2)}) collective-permute-start(f32[32,576]{1,0:T(8,128)S(1)} %add_add_fusion.2), channel_id=1, source_target_pairs={{0,16},{8,24},{16,0},{24,8},{1,17},{9,25},{17,1},{25,9},{2,18},{10... | collective-permute-start | bytes 221192 | tf_op jit(solution)/shard_map/sums/ppermute | solution.py:18
  192.6 4.8 %collective-permute-start.18 = (f32[32,576]{1,0:T(8,128)S(1)}, f32[32,576]{1,0:T(8,128)S(1)}, u32[]{:S(2)}, u32[]{:S(2)}) collective-permute-start(f32[32,576]{1,0:T(8,128)S(1)} %add_add_fusion.2), channel_id=1, source_target_pairs={{0,8},{8,0},{16,24},{24,16},{1,9},{9,1},{17,25},{25,17},{2,10},{10... | collective-permute-start | bytes 221192 | tf_op jit(solution)/shard_map/sums/ppermute | solution.py:18
  201.0 8.3 %collective-permute-start.24 = (f32[32,576]{1,0:T(8,128)S(1)}, f32[32,576]{1,0:T(8,128)S(1)}, u32[]{:S(2)}, u32[]{:S(2)}) collective-permute-start(f32[32,576]{1,0:T(8,128)S(1)} %add.125), channel_id=1, source_target_pairs={{0,6},{1,7},{2,4},{3,5},{4,2},{5,3},{6,0},{7,1},{8,14},{9,15},{10,... | collective-permute-start | bytes 221192 | tf_op jit(solution)/shard_map/sums/ppermute | solution.py:18
  207.0 8.1 %collective-permute-start.23 = (f32[32,576]{1,0:T(8,128)S(1)}, f32[32,576]{1,0:T(8,128)S(1)}, u32[]{:S(2)}, u32[]{:S(2)}) collective-permute-start(f32[32,576]{1,0:T(8,128)S(1)} %add.125), channel_id=1, source_target_pairs={{0,4},{1,5},{2,6},{3,7},{4,0},{5,1},{6,2},{7,3},{8,12},{9,13},{10,... | collective-permute-start | bytes 221192 | tf_op jit(solution)/shard_map/sums/ppermute | solution.py:18
  208.0 7.1 %collective-permute-start.22 = (f32[32,576]{1,0:T(8,128)S(1)}, f32[32,576]{1,0:T(8,128)S(1)}, u32[]{:S(2)}, u32[]{:S(2)}) collective-permute-start(f32[32,576]{1,0:T(8,128)S(1)} %add.125), channel_id=1, source_target_pairs={{0,2},{1,3},{2,0},{3,1},{4,6},{5,7},{6,4},{7,5},{8,10},{9,11},{10,... | collective-permute-start | bytes 221192 | tf_op jit(solution)/shard_map/sums/ppermute | solution.py:18
  215.1 7.5 %collective-permute-start.25 = (f32[32,576]{1,0:T(8,128)S(1)}, f32[32,576]{1,0:T(8,128)S(1)}, u32[]{:S(2)}, u32[]{:S(2)}) collective-permute-start(f32[32,576]{1,0:T(8,128)S(1)} %add_add_fusion.mine), channel_id=1, source_target_pairs={{0,32},{32,0},{1,33},{33,1},{2,34},{34,2},{3,35},{35,3},{4,36},{36... | collective-permute-start | bytes 221192 | tf_op jit(solution)/shard_map/sums/ppermute | solution.py:18
  (13 other events, 95.5 us)
Sparse Core Ops, SparseCore 0:
  21.3 39.2 all-gather.2
  99.2 70.8 reduce-scatter.1

commit v2 on v1

v2 whole, which is shorter than its diff:
```python
import jax
import jax.numpy as jnp
from jax import lax
from jax.experimental import pallas as pl
from jax.experimental.pallas import tpu as pltpu
from jax.sharding import Mesh, PartitionSpec as P

LOSS_SCALE = 256.0
HIGHEST = lax.Precision.HIGHEST
F32 = jnp.float32
BF16 = jnp.bfloat16
NY, NC, NX, NZ = 4, 2, 4, 8
NT = (((1,), (1,)), ((), ()))
TN = (((0,), (0,)), ((), ()))


def swap(value, axis, size, k):
    return lax.ppermute(value, axis, [(i, i ^ k) for i in range(size)])


def swaps(value, axis, size):
    return [value] + [swap(value, axis, size, k) for k in range(1, size)]


def tree(parts):
    while len(parts) > 1:
        parts = [parts[i] + parts[i + 1] for i in range(0, len(parts), 2)]
    return parts[0]


def thirds(value):
    parts = []
    for _ in range(3):
        part = value.astype(BF16)
        parts.append(part)
        value = value - part.astype(F32)
    return jnp.concatenate(parts, axis=0)


def join(value):
    rank = value.shape[0] // 3
    return value[:rank] + (value[rank:2 * rank] + value[2 * rank:])


def pack_kernel(act, cot, out, done):
    columns = act.shape[1] // NX
    copies = []
    for i in range(NX):
        copies.append((act.at[:, pl.ds(i * columns, columns)], out.at[i, :, pl.ds(0, columns)]))
        copies.append((cot, out.at[i, :, pl.ds(columns, cot.shape[1])]))
    copies = [pltpu.make_async_copy(src, dst, done.at[i]) for i, (src, dst) in enumerate(copies)]
    for copy in copies:
        copy.start()
    for copy in copies:
        copy.wait()


def pack(activations, cotangent):
    tokens, width = cotangent.shape
    columns = activations.shape[1] // NX
    return pl.pallas_call(
        pack_kernel,
        out_shape=jax.ShapeDtypeStruct((NX, tokens, columns + width), BF16),
        in_specs=[pl.BlockSpec(memory_space=pltpu.HBM)] * 2,
        out_specs=pl.BlockSpec(memory_space=pltpu.HBM),
        scratch_shapes=[pltpu.SemaphoreType.DMA((2 * NX,))],
        name="pack",
    )(activations, cotangent)


def gradient_kernel(q, cot, act, gradient, left, lhs):
    rank, width = q.shape

    @pl.when(pl.program_id(0) == 0)
    def _():
        lhs[:width, :] = cot[...].T
        q_cot = lax.dot_general(
            q[...], cot[...].astype(F32), NT, precision=HIGHEST, preferred_element_type=F32
        )
        lhs[width:, :] = thirds(q_cot)

    both = jnp.dot(lhs[...], act[...], preferred_element_type=F32)
    gradient[0] = both[:width]
    left[0] = join(both[width:])


def gradient_terms(q_start, gathered):
    rank, width = q_start.shape
    tokens = gathered.shape[0]
    columns = gathered.shape[1] - width
    block = columns // NZ
    return pl.pallas_call(
        gradient_kernel,
        out_shape=(
            jax.ShapeDtypeStruct((NZ, width, block), F32),
            jax.ShapeDtypeStruct((NZ, rank, block), F32),
        ),
        grid=(NZ,),
        in_specs=[
            pl.BlockSpec((rank, width), lambda z: (0, 0)),
            pl.BlockSpec((tokens, width), lambda z: (0, columns // width)),
            pl.BlockSpec((tokens, block), lambda z: (0, z)),
        ],
        out_specs=(
            pl.BlockSpec((1, width, block), lambda z: (z, 0, 0)),
            pl.BlockSpec((1, rank, block), lambda z: (z, 0, 0)),
        ),
        scratch_shapes=[pltpu.VMEM((width + 3 * rank, tokens), BF16)],
        cost_estimate=pl.CostEstimate(
            flops=2 * (width + 3 * rank) * tokens * columns,
            bytes_accessed=2 * gathered.size + 4 * (width + rank) * columns,
            transcendentals=0,
        ),
        compiler_params=pltpu.CompilerParams(vmem_limit_bytes=60 * 1024 * 1024),
        name="gradient_terms",
    )(q_start, gathered, gathered)


def project_kernel(place, cot, own, other, out, rows, arrived):
    sub = own.shape[2]
    block = NC * sub

    def fetch(k, c):
        start = pl.multiple_of((place[1] ^ c) * sub, sub)
        return pltpu.make_async_copy(
            (own, other)[c].at[:, k], rows.at[k, :, pl.ds(start, sub), :], arrived.at[NC * k + c]
        )

    @pl.when(pl.program_id(0) == 0)
    def _():
        for k in range(NX):
            for c in range(NC):
                fetch(k, c).start()

    for k in range(NX):
        @pl.when(pl.program_id(0) == k)
        def _():
            for c in range(NC):
                fetch(k, c).wait()
            for z in range(NZ):
                out[:, z * block:(z + 1) * block] = lax.dot_general(
                    cot[...], rows[k, z], NT, preferred_element_type=F32
                ).astype(BF16)


def project(place, cot, own, other):
    tokens, width = cot.shape
    sub = own.shape[2]
    columns = NZ * NC * sub
    return pl.pallas_call(
        project_kernel,
        out_shape=jax.ShapeDtypeStruct((tokens, NX * columns), BF16),
        grid_spec=pltpu.PrefetchScalarGridSpec(
            num_scalar_prefetch=1,
            grid=(NX,),
            in_specs=[pl.BlockSpec((tokens, width), lambda k, place: (0, 0))]
            + [pl.BlockSpec(memory_space=pltpu.HBM)] * 2,
            out_specs=pl.BlockSpec((tokens, columns), lambda k, place: (0, k ^ place[0])),
            scratch_shapes=[pltpu.VMEM((NX, NZ, NC * sub, width), BF16), pltpu.SemaphoreType.DMA((NC * NX,))],
        ),
        cost_estimate=pl.CostEstimate(
            flops=2 * tokens * width * NX * columns,
            bytes_accessed=2 * (tokens + width) * NX * columns,
            transcendentals=0,
        ),
        compiler_params=pltpu.CompilerParams(vmem_limit_bytes=62_000_000),
        name="project",
    )(place, cot, own, other)


def right_kernel(place, _, cot, p_line, act, p_total, error, keep, give, inner):
    step = pl.program_id(0)
    half = keep.shape[0]
    part = join(lax.dot_general(thirds(p_line[0]), act[...], NT, preferred_element_type=F32))

    @pl.when(step == 0)
    def _():
        inner[...] = part

    @pl.when(step > 0)
    def _():
        inner[...] = inner[...] + part

    @pl.when(step == NZ - 1)
    def _():
        p = p_total[...]
        right = join(jnp.dot(thirds(inner[...]), cot[...], preferred_element_type=F32)) * (1.0 / LOSS_SCALE)
        right = right + jnp.dot(p, error[...], precision=HIGHEST, preferred_element_type=F32)
        gram = lax.dot_general(p, p, NT, precision=HIGHEST, preferred_element_type=F32) * (1.0 / (NY * NC))
        sums = jnp.concatenate([right, gram], axis=1)
        first = place[1] == 0
        keep[...] = jnp.where(first, sums[:half], sums[half:])
        give[...] = jnp.where(first, sums[half:], sums[:half])


def right_terms(place, after, gathered, p_line, p_total, error):
    rank, block = p_total.shape
    width = error.shape[1]
    tokens = gathered.shape[0]
    columns = gathered.shape[1] - width
    half = jax.ShapeDtypeStruct((rank // NC, width + rank), F32)
    whole = pl.BlockSpec((rank // NC, width + rank), lambda z, place: (0, 0))
    return pl.pallas_call(
        right_kernel,
        out_shape=(half, half),
        grid_spec=pltpu.PrefetchScalarGridSpec(
            num_scalar_prefetch=1,
            grid=(NZ,),
            in_specs=[
                pl.BlockSpec(memory_space=pltpu.HBM),
                pl.BlockSpec((tokens, width), lambda z, place: (0, columns // width)),
                pl.BlockSpec((1, rank, block), lambda z, place: (z, 0, 0)),
                pl.BlockSpec((tokens, block), lambda z, place: (0, z)),
                pl.BlockSpec((rank, block), lambda z, place: (0, 0)),
                pl.BlockSpec((block, width), lambda z, place: (0, 0)),
            ],
            out_specs=(whole, whole),
            scratch_shapes=[pltpu.VMEM((rank, tokens), F32)],
        ),
        cost_estimate=pl.CostEstimate(
            flops=6 * rank * tokens * (columns + width),
            bytes_accessed=2 * gathered.size,
            transcendentals=0,
        ),
        compiler_params=pltpu.CompilerParams(vmem_limit_bytes=32 * 1024 * 1024),
        name="right_terms",
    )(place, after, gathered, p_line, gathered, p_total, error)


def eliminate(gram):
    rank = gram.shape[0]
    group = 4
    row = lax.broadcasted_iota(jnp.int32, (rank, 2 * rank), 0)
    col = lax.broadcasted_iota(jnp.int32, (rank, 2 * rank), 1)
    work = jnp.where(col == row + rank, 1.0, jnp.concatenate([gram, jnp.zeros_like(gram)], axis=1))
    scale = jnp.zeros_like(work)
    for base in range(0, rank, group):
        at = [base + j for j in range(group)]
        cols = [jnp.broadcast_to(work[:, k:k + 1], work.shape) for k in at]
        rows = [work[k:k + 1, :] for k in at]
        for j, k in enumerate(at):
            pivot = cols[j][k:k + 1, :]
            ratio = jnp.where(row > k, cols[j] * (1.0 / pivot), 0.0)
            scale = jnp.where(row == k, lax.rsqrt(pivot), scale)
            for i in range(j + 1, group):
                cols[i] = cols[i] - ratio * cols[i][k:k + 1, :]
                rows[i] = rows[i] - ratio[at[i]:at[i] + 1, :] * rows[j]
            work = work - ratio * rows[j]
    return (work * scale)[:, rank:]


def finish_kernel(place, mine, other, p_total, gradient, error, error_out, compressed_out, q_out, own, old, arrived):
    width = error.shape[1]
    first = place[1] == 0
    fetches = [
        pltpu.make_async_copy(gradient.at[0], own, arrived.at[0]),
        pltpu.make_async_copy(error, old, arrived.at[1]),
    ]
    for fetch in fetches:
        fetch.start()
    sums = jnp.concatenate([jnp.where(first, mine[...], other[...]), jnp.where(first, other[...], mine[...])], axis=0)
    inverse = eliminate(sums[:, width:])
    q_next = jnp.dot(inverse, sums[:, :width], precision=HIGHEST, preferred_element_type=F32) * (1.0 / (NY * NC))
    p_basis = jnp.dot(inverse, p_total[...], precision=HIGHEST, preferred_element_type=F32)
    compressed = lax.dot_general(p_basis, q_next, TN, precision=HIGHEST, preferred_element_type=F32)
    q_out[...] = q_next
    compressed_out[...] = compressed
    for fetch in fetches:
        fetch.wait()
    error_out[...] = (own[...].T * (1.0 / LOSS_SCALE) + old[...]) - compressed


def finish(place, mine, other, p_total, gradient, error):
    rank = p_total.shape[0]
    return pl.pallas_call(
        finish_kernel,
        out_shape=(
            jax.ShapeDtypeStruct(error.shape, F32),
            jax.ShapeDtypeStruct(error.shape, F32),
            jax.ShapeDtypeStruct((rank, error.shape[1]), F32),
        ),
        in_specs=[pl.BlockSpec(memory_space=pltpu.SMEM)]
        + [pl.BlockSpec(memory_space=pltpu.VMEM)] * 3
        + [pl.BlockSpec(memory_space=pltpu.HBM)] * 2,
        scratch_shapes=[
            pltpu.VMEM(gradient.shape[1:], F32),
            pltpu.VMEM(error.shape, F32),
            pltpu.SemaphoreType.DMA((2,)),
        ],
        compiler_params=pltpu.CompilerParams(vmem_limit_bytes=62_800_000),
        name="finish",
    )(place, mine, other, p_total, gradient, error)


def local(activations, cotangent, kv_weight, error_buffer, q_start):
    c, x = lax.axis_index("c"), lax.axis_index("x")
    place = jnp.stack([x, c]).astype(jnp.int32)
    rank = q_start.shape[0]
    error = error_buffer[0]

    with jax.named_scope("exchange"):
        sub = kv_weight.shape[0] // NC
        mine = lax.dynamic_slice_in_dim(kv_weight, c * sub, sub, axis=0)
        column = jnp.stack(swaps(mine, "x", NX))
        column, packed = lax.optimization_barrier((column, pack(activations, cotangent)))
        weight = lax.all_gather(column, "z", axis=0)
        gathered = lax.all_to_all(packed, "x", 0, 0, tiled=True)
        p_own = jnp.einsum("rk,dk->rd", q_start, error, precision=HIGHEST)
        gathered, p_own = lax.optimization_barrier((gathered, p_own))
        gathered = gathered.reshape(-1, gathered.shape[2])

    with jax.named_scope("gradient"):
        part, p_part = gradient_terms(q_start, gathered)
        gradient = lax.psum_scatter(part, "z", scatter_dimension=0, tiled=True)

    with jax.named_scope("left"):
        p_part = lax.all_to_all(p_part, "z", 0, 0, tiled=True)
        p_total = tree([p_part[i] for i in range(NZ)]) * (1.0 / LOSS_SCALE) + p_own
        p_total = tree(swaps(p_total, "c", NC))
        p_total = tree(swaps(p_total, "y", NY))
        p_line = jnp.broadcast_to(p_total[None], (NZ,) + p_total.shape)
        p_line = lax.all_to_all(p_line, "z", 0, 0, tiled=True)

    with jax.named_scope("weight"):
        input_grad = project(place, cotangent, weight, swap(weight, "c", NC, 1))

    with jax.named_scope("sums"):
        keep, give = right_terms(place, input_grad[:16, :128], gathered, p_line, p_total, error)
        keep = keep + swap(give, "c", NC, 1)
        keep = tree(swaps(keep, "y", NY))
        keep = tree(swaps(keep, "x", NX))
        keep = keep + swap(keep, "z", NZ, 1)
        keep = tree([keep] + [swap(keep, "z", NZ, k) for k in (2, 4, 6)])
        other = swap(keep, "c", NC, 1)

    with jax.named_scope("finish"):
        error_next, compressed, q_next = finish(place, keep, other, p_total, gradient, error)
    return (input_grad, error_next[None], compressed, q_next)


def solution(mesh):
    fine = Mesh(mesh.devices.reshape(NY, NC, NX, NZ), ("y", "c", "x", "z"))
    dp, fsdp = ("y", "c"), ("x", "z")
    return jax.shard_map(
        local,
        mesh=fine,
        in_specs=(P(dp + fsdp, None), P(dp + fsdp, None), P(fsdp, None), P(dp, fsdp, None), P()),
        out_specs=(P(dp + fsdp, None), P(dp, fsdp, None), P(fsdp, None), P()),
        check_vma=False,
    )
```

time: 238 us -> 430 us (1.81)
  Pallas kernels: 16.1 us -> 234 us
  blocking collectives: 0 us -> 29.9 us
  starting transfers between devices: 62.2 us -> 37.6 us
  matrix products: 16.8 us -> 0.61 us
  waiting for transfers between devices: 118 us -> 109 us
  local copies, waits for them, and re-layouts: 10.4 us -> 3.1 us
    pallas_call x2 -> x4, Pallas kernels: 9.37 us -> 226 us  [the longest x1 200 us: pack(): pl.pallas_call(pack_kernel, out_shape=jax.ShapeDtypeStruct((NX, tokens, c...]
    ppermute x26 -> x20, waiting for transfers between devices: 118 us -> 25 us  [swap(): return lax.ppermute(value, axis, [(i, i ^ k) for i in range(size)])]
    all_to_all x2, waiting for transfers between devices: 0.01 us -> 83.6 us  [the longest x1 70.1 us: local(): gathered = lax.all_to_all(packed, 'x', 0, 0, tiled=True)]
    all_to_all x0 -> x1, blocking collectives: none -> 29.9 us  [local(): p_part = lax.all_to_all(p_part, 'z', 0, 0, tiled=True)]
    ppermute x26 -> x20, starting transfers between devices: 46.4 us -> 28.6 us  [swap(): return lax.ppermute(value, axis, [(i, i ^ k) for i in range(size)])]
    dot_general x3 -> x0, matrix products: 15.1 us -> none  [the longest x1 8.74 us: local(): part = jnp.einsum('td,tk->dk', act_x, cot_x, preferred_element_type=F32)]
    all_to_all x2, starting transfers between devices: 15.7 us -> 8.95 us  [the longest x1 5.46 us: local(): gathered = lax.all_to_all(packed, 'x', 0, 0, tiled=True)]
    all_to_all x2 -> x0, local copies, waits for them, and re-layouts: 6.58 us -> none  [the longest x1 5.74 us: local(): act_x = lax.all_to_all(activations, 'x', 1, 0, tiled=True)]
  transfers between devices with their start and end apart: 30 -> 24, of which waited for: 17 -> 15; matrix products, arithmetic and copies ran while one was open for 8% -> 1% of each run, Pallas kernels for 3% -> 53%
where the time goes in v2:
time: 430 us
  Pallas kernels  234 us (54%)
  waiting for transfers between devices  109 us (25%)
  starting transfers between devices  37.6 us (9%)
  blocking collectives  29.9 us (7%)
  between operations  14.3 us (3%)
    pallas_call x1, Pallas kernels, pack(): pl.pallas_call(pack_kernel, out_shape=jax.ShapeDtypeStruct((NX, tokens, c...  200 us
    all_to_all x1, waiting for transfers between devices, local(): gathered = lax.all_to_all(packed, 'x', 0, 0, tiled=True)  70.1 us
    all_to_all x1, blocking collectives, local(): p_part = lax.all_to_all(p_part, 'z', 0, 0, tiled=True)  29.9 us
    ppermute x20, starting transfers between devices, swap(): return lax.ppermute(value, axis, [(i, i ^ k) for i in range(size)])  28.6 us
    ppermute x20, waiting for transfers between devices, swap(): return lax.ppermute(value, axis, [(i, i ^ k) for i in range(size)])  25 us
    all_to_all x1, waiting for transfers between devices, local(): p_line = lax.all_to_all(p_line, 'z', 0, 0, tiled=True)  13.4 us
    pallas_call x1, Pallas kernels, gradient_terms(): pl.pallas_call(gradient_kernel, out_shape=(jax.ShapeDtypeStruct((NZ, widt...  11.9 us
  transfers between devices with their start and end apart: 24, of which 15 were waited for; matrix products, arithmetic and copies ran while one was open for 1% of the time, Pallas kernels for 53%

profile of v2, /device:TPU:1, one launch (start us, length us, event | category | flops | bytes accessed | tf_op | source)
XLA Modules:
  0.0 429.6 jit_solution(17889009685964363410)
XLA Ops:
  8.1 3.4 collective-permute-start.2
  12.2 199.7 %pack.1 = bf16[4,320,2560]{2,1,0:T(8,128)(2,1)} custom-call(bf16[320,8192]{1,0:T(8,128)(2,1)} %act.1, bf16[320,512]{1,0:T(8,128)(2,1)} %cot.3), custom_call_target="tpu_custom_call" | custom-call | tf_op jit(solution)/shard_map/exchange/pack/pallas_call | solution.py:61
  212.9 5.5 %all-to-all-start = ((bf16[4,320,2560]{2,1,0:T(8,128)(2,1)}), bf16[4,320,2560]{2,1,0:T(8,128)(2,1)}, u32[]{:S(2)}, u32[]{:S(2)}) async-start(bf16[4,320,2560]{2,1,0:T(8,128)(2,1)} %pack.1), calls=%async_computation | async-start | bytes 13107200 | tf_op jit(solution)/shard_map/exchange/all_to_all | solution.py:307
  219.0 70.1 %all-to-all-done = bf16[4,320,2560]{2,1,0:T(8,128)(2,1)} async-done(((bf16[4,320,2560]{2,1,0:T(8,128)(2,1)}), bf16[4,320,2560]{2,1,0:T(8,128)(2,1)}, u32[]{:S(2)}, u32[]{:S(2)}) %all-to-all-start) | async-done | bytes 6553632 | tf_op jit(solution)/shard_map/exchange/all_to_all | solution.py:307
  289.2 11.9 %gradient_terms.1 = (f32[8,512,256]{2,1,0:T(8,128)}, f32[8,64,256]{2,1,0:T(8,128)}) custom-call(f32[64,512]{1,0:T(8,128)} %q.1, bf16[1280,2560]{1,0:T(8,128)(2,1)} %bitcast.8.cot.act, bf16[1280,2560]{1,0:T(8,128)(2,1)} %bitcast.8.cot.act), custom_call_target="tpu_custom_call" | custom-call | flops 3690987520 | bytes 11272192 | tf_op jit(solution)/shard_map/gradient/gradient_terms/pallas_call | solution.py:92
  301.2 4.4 %collective-permute-start.3 = (bf16[8,4,128,512]{3,2,1,0:T(8,128)(2,1)}, bf16[8,4,128,512]{3,2,1,0:T(8,128)(2,1)}, u32[]{:S(2)}, u32[]{:S(2)}) collective-permute-start(bf16[8,4,128,512]{3,2,1,0:T(8,128)(2,1)} %bitcast.20), channel_id=1, source_target_pairs={{0,32},{32,0},{1,33},{33,1},{2,34},{34,2},{3,35},{35,3},{4,36},{36... | collective-permute-start | bytes 12582920 | tf_op jit(solution)/shard_map/weight/ppermute | solution.py:18
  305.5 29.9 %all_to_all.15 = f32[8,64,256]{2,1,0:T(8,128)S(1)} all-to-all(f32[8,64,256]{2,1,0:T(8,128)} %get-tuple-element.18), channel_id=1, replica_groups=mesh['y'=4,'c'=2,'x'=4,'z'=8] {'z'}, dimensions={0} | all-to-all | bytes 1048576 | tf_op jit(solution)/shard_map/left/all_to_all | solution.py:317
  337.2 3.0 collective-permute-start.6
  341.9 3.0 collective-permute-done.7
  345.8 3.5 all-to-all-start.2
  349.9 8.2 %project.1 = bf16[320,8192]{1,0:T(8,128)(2,1)} custom-call(s32[2]{0:T(128)} %pad_add_fusion.place, bf16[320,512]{1,0:T(8,128)(2,1)} %cot.3, bf16[8,4,128,512]{3,2,1,0:T(8,128)(2,1)} %bitcast.21, bf16[8,4,128,512]{3,2,1,0:T(8,128)(2,1)} %collective-permute-done.3.other), custom_call_target="tpu_custom_call" | custom-call | flops 2684354560 | bytes 13631488 | tf_op jit(solution)/shard_map/weight/project/pallas_call | solution.py:150
  358.8 13.4 %all-to-all-done.2.p_line = f32[8,64,256]{2,1,0:T(8,128)S(1)} async-done(((f32[8,64,256]{2,1,0:T(8,128)}), f32[8,64,256]{2,1,0:T(8,128)S(1)}, u32[]{:S(2)}, u32[]{:S(2)}) %all-to-all-start.2) | async-done | bytes 524320 | tf_op jit(solution)/shard_map/left/all_to_all | solution.py:322
  372.2 8.4 %right_terms.1 = (f32[32,576]{1,0:T(8,128)S(1)}, f32[32,576]{1,0:T(8,128)S(1)}) custom-call(s32[2]{0:T(128)S(1)} %copy-done.3, bf16[16,128]{1,0:T(8,128)(2,1)S(1)} %slice.36._, bf16[1280,2560]{1,0:T(8,128)(2,1)} %bitcast.8.cot.act, f32[8,64,256]{2,1,0:T(8,128)S(1)} %all-to-all-done.2.p_line, bf16[1280,2560]{1,0:T(8,128)(2,1)} %bitcast.8.cot.act, ...), custom_call_target="tpu_custom_call" | custom-call | flops 1258291200 | bytes 6553600 | tf_op jit(solution)/shard_map/sums/right_terms/pallas_call | solution.py:203
  380.6 2.3 collective-permute-start.8
  386.6 2.5 collective-permute-done.10
  389.1 2.3 collective-permute-done.11
  394.1 2.3 collective-permute-done.13
  396.4 2.3 collective-permute-done.14
  399.5 2.6 collective-permute-done.15
  402.7 2.8 collective-permute-start.18
  405.5 2.3 collective-permute-start.16
  407.9 2.0 collective-permute-done.17
  410.8 3.4 collective-permute-done.16
  417.0 5.7 %finish.1 = (f32[256,512]{1,0:T(8,128)}, f32[256,512]{1,0:T(8,128)}, f32[64,512]{1,0:T(8,128)}) custom-call(s32[2]{0:T(128)} %pad_add_fusion.place, f32[32,576]{1,0:T(8,128)} %copy-done.4, f32[32,576]{1,0:T(8,128)} %copy-done.6, f32[64,256]{1,0:T(8,128)} %copy-done.2, f32[1,512,256]{2,1,0:T(8,128)} %reduce-scatter.2.cloned.1.call-done.gradient, ...), custom_call_target="tpu_custom_call" | custom-call | tf_op jit(solution)/shard_map/finish/finish/pallas_call | solution.py:275
  (61 shorter events, 20.3 us)
Async XLA Ops:
  7.2 294.0 %all-gather.3.cloned.1.call-start = ((), (), s32[]{:S(2)}) async-start(), calls=%async_computation.5 | async-start | bytes 4718592 | tf_op jit(solution)/shard_map/exchange/all_gather | solution.py:306
  8.1 203.8 %collective-permute-start.2 = (bf16[128,512]{1,0:T(8,128)(2,1)S(1)}, bf16[128,512]{1,0:T(8,128)(2,1)S(1)}, u32[]{:S(2)}, u32[]{:S(2)}) collective-permute-start(bf16[128,512]{1,0:T(8,128)(2,1)S(1)} %constant_dynamic-slice_fusion), channel_id=1, source_target_pairs={{0,24},{8,16},{16,8},{24,0},{1,25},{9,17},{17,9},{25,1},{2,26},{10... | collective-permute-start | bytes 393224 | tf_op jit(solution)/shard_map/exchange/ppermute | solution.py:18
  11.5 200.4 %collective-permute-start.1 = (bf16[128,512]{1,0:T(8,128)(2,1)S(1)}, bf16[128,512]{1,0:T(8,128)(2,1)S(1)}, u32[]{:S(2)}, u32[]{:S(2)}) collective-permute-start(bf16[128,512]{1,0:T(8,128)(2,1)S(1)} %constant_dynamic-slice_fusion), channel_id=1, source_target_pairs={{0,16},{8,24},{16,0},{24,8},{1,17},{9,25},{17,1},{25,9},{2,18},{10... | collective-permute-start | bytes 393224 | tf_op jit(solution)/shard_map/exchange/ppermute | solution.py:18
  12.0 199.9 %collective-permute-start = (bf16[128,512]{1,0:T(8,128)(2,1)S(1)}, bf16[128,512]{1,0:T(8,128)(2,1)S(1)}, u32[]{:S(2)}, u32[]{:S(2)}) collective-permute-start(bf16[128,512]{1,0:T(8,128)(2,1)S(1)} %constant_dynamic-slice_fusion), channel_id=1, source_target_pairs={{0,8},{8,0},{16,24},{24,16},{1,9},{9,1},{17,25},{25,17},{2,10},{10... | collective-permute-start | bytes 393224 | tf_op jit(solution)/shard_map/exchange/ppermute | solution.py:18
  212.9 76.3 %all-to-all-start = ((bf16[4,320,2560]{2,1,0:T(8,128)(2,1)}), bf16[4,320,2560]{2,1,0:T(8,128)(2,1)}, u32[]{:S(2)}, u32[]{:S(2)}) async-start(bf16[4,320,2560]{2,1,0:T(8,128)(2,1)} %pack.1), calls=%async_computation | async-start | bytes 13107200 | tf_op jit(solution)/shard_map/exchange/all_to_all | solution.py:307
  218.3 198.1 %reduce-scatter.2.cloned.1.call-start = ((), (), s32[]{:S(2)}) async-start(), calls=%async_computation.4 | async-start | bytes 4718592 | tf_op jit(solution)/shard_map/gradient/reduce_scatter | solution.py:314
  301.2 48.7 %collective-permute-start.3 = (bf16[8,4,128,512]{3,2,1,0:T(8,128)(2,1)}, bf16[8,4,128,512]{3,2,1,0:T(8,128)(2,1)}, u32[]{:S(2)}, u32[]{:S(2)}) collective-permute-start(bf16[8,4,128,512]{3,2,1,0:T(8,128)(2,1)} %bitcast.20), channel_id=1, source_target_pairs={{0,32},{32,0},{1,33},{33,1},{2,34},{34,2},{3,35},{35,3},{4,36},{36... | collective-permute-start | bytes 12582920 | tf_op jit(solution)/shard_map/weight/ppermute | solution.py:18
  335.4 1.7 collective-permute-start.4
  337.2 4.7 %collective-permute-start.6 = (f32[64,256]{1,0:T(8,128)S(1)}, f32[64,256]{1,0:T(8,128)S(1)}, u32[]{:S(2)}, u32[]{:S(2)}) collective-permute-start(f32[64,256]{1,0:T(8,128)S(1)} %add.90), channel_id=1, source_target_pairs={{0,128},{64,192},{128,0},{192,64},{1,129},{65,193},{129,1},{193,65... | collective-permute-start | bytes 196616 | tf_op jit(solution)/shard_map/left/ppermute | solution.py:18
  340.2 4.7 %collective-permute-start.7 = (f32[64,256]{1,0:T(8,128)S(1)}, f32[64,256]{1,0:T(8,128)S(1)}, u32[]{:S(2)}, u32[]{:S(2)}) collective-permute-start(f32[64,256]{1,0:T(8,128)S(1)} %add.90), channel_id=1, source_target_pairs={{0,192},{64,128},{128,64},{192,0},{1,193},{65,129},{129,65},{193,1... | collective-permute-start | bytes 196616 | tf_op jit(solution)/shard_map/left/ppermute | solution.py:18
  341.0 3.9 collective-permute-start.5
  345.8 26.4 %all-to-all-start.2 = ((f32[8,64,256]{2,1,0:T(8,128)}), f32[8,64,256]{2,1,0:T(8,128)S(1)}, u32[]{:S(2)}, u32[]{:S(2)}) async-start(f32[8,64,256]{2,1,0:T(8,128)} %broadcast_in_dim.4), calls=%async_computation.2 | async-start | bytes 1048576 | tf_op jit(solution)/shard_map/left/all_to_all | solution.py:322
  380.6 3.2 collective-permute-start.8
  383.8 5.3 %collective-permute-start.10 = (f32[32,576]{1,0:T(8,128)S(1)}, f32[32,576]{1,0:T(8,128)S(1)}, u32[]{:S(2)}, u32[]{:S(2)}) collective-permute-start(f32[32,576]{1,0:T(8,128)S(1)} %add.94), channel_id=1, source_target_pairs={{0,128},{64,192},{128,0},{192,64},{1,129},{65,193},{129,1},{193,65... | collective-permute-start | bytes 221192 | tf_op jit(solution)/shard_map/sums/ppermute | solution.py:18
  385.1 6.2 %collective-permute-start.11 = (f32[32,576]{1,0:T(8,128)S(1)}, f32[32,576]{1,0:T(8,128)S(1)}, u32[]{:S(2)}, u32[]{:S(2)}) collective-permute-start(f32[32,576]{1,0:T(8,128)S(1)} %add.94), channel_id=1, source_target_pairs={{0,192},{64,128},{128,64},{192,0},{1,193},{65,129},{129,65},{193,1... | collective-permute-start | bytes 221192 | tf_op jit(solution)/shard_map/sums/ppermute | solution.py:18
  386.6 4.8 %collective-permute-start.9 = (f32[32,576]{1,0:T(8,128)S(1)}, f32[32,576]{1,0:T(8,128)S(1)}, u32[]{:S(2)}, u32[]{:S(2)}) collective-permute-start(f32[32,576]{1,0:T(8,128)S(1)} %add.94), channel_id=1, source_target_pairs={{0,64},{64,0},{128,192},{192,128},{1,65},{65,1},{129,193},{193,129... | collective-permute-start | bytes 221192 | tf_op jit(solution)/shard_map/sums/ppermute | solution.py:18
  391.4 5.0 %collective-permute-start.13 = (f32[32,576]{1,0:T(8,128)S(1)}, f32[32,576]{1,0:T(8,128)S(1)}, u32[]{:S(2)}, u32[]{:S(2)}) collective-permute-start(f32[32,576]{1,0:T(8,128)S(1)} %add_add_fusion.2), channel_id=1, source_target_pairs={{0,16},{8,24},{16,0},{24,8},{1,17},{9,25},{17,1},{25,9},{2,18},{10... | collective-permute-start | bytes 221192 | tf_op jit(solution)/shard_map/sums/ppermute | solution.py:18
  391.5 7.2 %collective-permute-start.14 = (f32[32,576]{1,0:T(8,128)S(1)}, f32[32,576]{1,0:T(8,128)S(1)}, u32[]{:S(2)}, u32[]{:S(2)}) collective-permute-start(f32[32,576]{1,0:T(8,128)S(1)} %add_add_fusion.2), channel_id=1, source_target_pairs={{0,24},{8,16},{16,8},{24,0},{1,25},{9,17},{17,9},{25,1},{2,26},{10... | collective-permute-start | bytes 221192 | tf_op jit(solution)/shard_map/sums/ppermute | solution.py:18
  393.4 5.3 %collective-permute-start.12 = (f32[32,576]{1,0:T(8,128)S(1)}, f32[32,576]{1,0:T(8,128)S(1)}, u32[]{:S(2)}, u32[]{:S(2)}) collective-permute-start(f32[32,576]{1,0:T(8,128)S(1)} %add_add_fusion.2), channel_id=1, source_target_pairs={{0,8},{8,0},{16,24},{24,16},{1,9},{9,1},{17,25},{25,17},{2,10},{10... | collective-permute-start | bytes 221192 | tf_op jit(solution)/shard_map/sums/ppermute | solution.py:18
  398.7 3.4 collective-permute-start.15
  402.1 7.8 %collective-permute-start.17 = (f32[32,576]{1,0:T(8,128)S(1)}, f32[32,576]{1,0:T(8,128)S(1)}, u32[]{:S(2)}, u32[]{:S(2)}) collective-permute-start(f32[32,576]{1,0:T(8,128)S(1)} %add.101), channel_id=1, source_target_pairs={{0,4},{1,5},{2,6},{3,7},{4,0},{5,1},{6,2},{7,3},{8,12},{9,13},{10,... | collective-permute-start | bytes 221192 | tf_op jit(solution)/shard_map/sums/ppermute | solution.py:18
  402.7 8.0 %collective-permute-start.18 = (f32[32,576]{1,0:T(8,128)S(1)}, f32[32,576]{1,0:T(8,128)S(1)}, u32[]{:S(2)}, u32[]{:S(2)}) collective-permute-start(f32[32,576]{1,0:T(8,128)S(1)} %add.101), channel_id=1, source_target_pairs={{0,6},{1,7},{2,4},{3,5},{4,2},{5,3},{6,0},{7,1},{8,14},{9,15},{10,... | collective-permute-start | bytes 221192 | tf_op jit(solution)/shard_map/sums/ppermute | solution.py:18
  405.5 8.6 %collective-permute-start.16 = (f32[32,576]{1,0:T(8,128)S(1)}, f32[32,576]{1,0:T(8,128)S(1)}, u32[]{:S(2)}, u32[]{:S(2)}) collective-permute-start(f32[32,576]{1,0:T(8,128)S(1)} %add.101), channel_id=1, source_target_pairs={{0,2},{1,3},{2,0},{3,1},{4,6},{5,7},{6,4},{7,5},{8,10},{9,11},{10,... | collective-permute-start | bytes 221192 | tf_op jit(solution)/shard_map/sums/ppermute | solution.py:18
  414.2 2.2 collective-permute-start.19
  (7 other events, 64.4 us)
Sparse Core Ops, SparseCore 0:
  213.0 58.7 all-gather.2
  301.3 79.5 reduce-scatter.1

commit v3 on v1

v3 whole, which is shorter than its diff:
```python
import functools

import jax
import jax.numpy as jnp
from jax import lax
from jax.experimental import pallas as pl
from jax.experimental.pallas import tpu as pltpu
from jax.sharding import Mesh, PartitionSpec as P

LOSS_SCALE = 256.0
HIGHEST = lax.Precision.HIGHEST
F32 = jnp.float32
BF16 = jnp.bfloat16
NY, NC, NX, NZ = 4, 2, 4, 8
NT = (((1,), (1,)), ((), ()))
TN = (((0,), (0,)), ((), ()))


def swap(value, axis, size, k):
    return lax.ppermute(value, axis, [(i, i ^ k) for i in range(size)])


def swaps(value, axis, size):
    return [value] + [swap(value, axis, size, k) for k in range(1, size)]


def tree(parts):
    while len(parts) > 1:
        parts = [parts[i] + parts[i + 1] for i in range(0, len(parts), 2)]
    return parts[0]


def thirds(value):
    parts = []
    for _ in range(3):
        part = value.astype(BF16)
        parts.append(part)
        value = value - part.astype(F32)
    return jnp.concatenate(parts, axis=0)


def join(value):
    rank = value.shape[0] // 3
    return value[:rank] + (value[rank:2 * rank] + value[2 * rank:])


def load_tokens(refs, rows):
    at = 0
    for ref in refs:
        rows[at:at + ref.shape[0], :] = ref[...]
        at += ref.shape[0]


def gradient_kernel(count, place, *refs):
    cots, acts = refs[:NX], refs[NX:NX + count]
    gradient, lhs, cot_rows, rows = refs[NX + count:]

    @pl.when(pl.program_id(0) == 0)
    def _():
        load_tokens(cots, cot_rows)
        lhs[...] = cot_rows[...].T

    load_tokens(acts, rows)
    gradient[0] = jnp.dot(lhs[...], rows[...], preferred_element_type=F32)


def left_kernel(count, place, q, error, *refs):
    cots, acts = refs[:NX], refs[NX:NX + count]
    left, lhs, cot_rows, rows = refs[NX + count:]
    z = pl.program_id(0)
    block = acts[0].shape[1]

    @pl.when(z == 0)
    def _():
        load_tokens(cots, cot_rows)
        q_cot = lax.dot_general(
            q[...], cot_rows[...].astype(F32), NT, precision=HIGHEST, preferred_element_type=F32
        )
        lhs[...] = thirds(q_cot)

    load_tokens(acts, rows)
    part = join(jnp.dot(lhs[...], rows[...], preferred_element_type=F32)) * (1.0 / LOSS_SCALE)
    left[:, 0] = part.reshape(NY * NC, -1, block)

    @pl.when(z == place[2])
    def _():
        own = lax.dot_general(q[...], error[...], NT, precision=HIGHEST, preferred_element_type=F32)
        left[:, 0] = left[:, 0] + own.reshape(NY * NC, -1, block)


def token_specs(activations, cots, pieces):
    block = activations.shape[1] // (NX * NZ)
    tokens, width = cots[0].shape
    specs = [pl.BlockSpec((tokens, width), lambda z, place: (0, 0))] * NX
    specs.append(pl.BlockSpec((tokens, block), lambda z, place: (0, place[0] * NZ + z)))
    specs += [pl.BlockSpec((piece.shape[0], block), lambda z, place: (0, z)) for piece in pieces]
    return specs


def gradient_terms(place, activations, cots, pieces):
    width = cots[0].shape[1]
    tokens = NX * cots[0].shape[0]
    block = activations.shape[1] // (NX * NZ)
    return pl.pallas_call(
        functools.partial(gradient_kernel, 1 + len(pieces)),
        out_shape=jax.ShapeDtypeStruct((NZ, width, block), F32),
        grid_spec=pltpu.PrefetchScalarGridSpec(
            num_scalar_prefetch=1,
            grid=(NZ,),
            in_specs=token_specs(activations, cots, pieces),
            out_specs=pl.BlockSpec((1, width, block), lambda z, place: (z, 0, 0)),
            scratch_shapes=[pltpu.VMEM(shape, BF16) for shape in ((width, tokens), (tokens, width), (tokens, block))],
        ),
        cost_estimate=pl.CostEstimate(
            flops=2 * width * tokens * block * NZ,
            bytes_accessed=(2 * tokens + 4 * width) * block * NZ,
            transcendentals=0,
        ),
        compiler_params=pltpu.CompilerParams(vmem_limit_bytes=60 * 1024 * 1024),
        name="gradient_terms",
    )(place, *cots, activations, *pieces)


def left_terms(place, q_start, error, activations, cots, pieces):
    rank, width = q_start.shape
    tokens = NX * cots[0].shape[0]
    block = activations.shape[1] // (NX * NZ)
    shares = NY * NC
    return pl.pallas_call(
        functools.partial(left_kernel, 1 + len(pieces)),
        out_shape=jax.ShapeDtypeStruct((shares, NZ, rank // shares, block), F32),
        grid_spec=pltpu.PrefetchScalarGridSpec(
            num_scalar_prefetch=1,
            grid=(NZ,),
            in_specs=[
                pl.BlockSpec((rank, width), lambda z, place: (0, 0)),
                pl.BlockSpec((block, width), lambda z, place: (0, 0)),
            ]
            + token_specs(activations, cots, pieces),
            out_specs=pl.BlockSpec((shares, 1, rank // shares, block), lambda z, place: (0, z, 0, 0)),
            scratch_shapes=[pltpu.VMEM(shape, BF16) for shape in ((3 * rank, tokens), (tokens, width), (tokens, block))],
        ),
        cost_estimate=pl.CostEstimate(
            flops=6 * rank * tokens * block * NZ,
            bytes_accessed=2 * tokens * block * NZ,
            transcendentals=0,
        ),
        compiler_params=pltpu.CompilerParams(vmem_limit_bytes=60 * 1024 * 1024),
        name="left_terms",
    )(place, q_start, error, *cots, activations, *pieces)


def project_kernel(place, cot, own, other, out, rows, arrived):
    sub = own.shape[2]
    block = NC * sub

    def fetch(k, c):
        start = pl.multiple_of((place[1] ^ c) * sub, sub)
        return pltpu.make_async_copy(
            (own, other)[c].at[:, k], rows.at[k, :, pl.ds(start, sub), :], arrived.at[NC * k + c]
        )

    @pl.when(pl.program_id(0) == 0)
    def _():
        for k in range(NX):
            for c in range(NC):
                fetch(k, c).start()

    for k in range(NX):
        @pl.when(pl.program_id(0) == k)
        def _():
            for c in range(NC):
                fetch(k, c).wait()
            for z in range(NZ):
                out[:, z * block:(z + 1) * block] = lax.dot_general(
                    cot[...], rows[k, z], NT, preferred_element_type=F32
                ).astype(BF16)


def project(place, cot, own, other):
    tokens, width = cot.shape
    sub = own.shape[2]
    columns = NZ * NC * sub
    return pl.pallas_call(
        project_kernel,
        out_shape=jax.ShapeDtypeStruct((tokens, NX * columns), BF16),
        grid_spec=pltpu.PrefetchScalarGridSpec(
            num_scalar_prefetch=1,
            grid=(NX,),
            in_specs=[pl.BlockSpec((tokens, width), lambda k, place: (0, 0))]
            + [pl.BlockSpec(memory_space=pltpu.HBM)] * 2,
            out_specs=pl.BlockSpec((tokens, columns), lambda k, place: (0, k ^ place[0])),
            scratch_shapes=[pltpu.VMEM((NX, NZ, NC * sub, width), BF16), pltpu.SemaphoreType.DMA((NC * NX,))],
        ),
        cost_estimate=pl.CostEstimate(
            flops=2 * tokens * width * NX * columns,
            bytes_accessed=2 * (tokens + width) * NX * columns,
            transcendentals=0,
        ),
        compiler_params=pltpu.CompilerParams(vmem_limit_bytes=62_000_000),
        name="project",
    )(place, cot, own, other)


def right_kernel(place, _, gradient, error, p_total, merged_out, keep, give):
    half = keep.shape[0]
    merged = gradient[0].T * (1.0 / LOSS_SCALE) + error[...]
    merged_out[...] = merged
    p = p_total[...]
    right = jnp.dot(p, merged, precision=HIGHEST, preferred_element_type=F32)
    gram = lax.dot_general(p, p, NT, precision=HIGHEST, preferred_element_type=F32) * (1.0 / (NY * NC))
    sums = jnp.concatenate([right, gram], axis=1)
    first = place[1] == 0
    keep[...] = jnp.where(first, sums[:half], sums[half:])
    give[...] = jnp.where(first, sums[half:], sums[:half])


def right_terms(place, after, gradient, error, p_total):
    rank, width = p_total.shape[0], error.shape[1]
    half = jax.ShapeDtypeStruct((rank // NC, width + rank), F32)
    return pl.pallas_call(
        right_kernel,
        out_shape=(jax.ShapeDtypeStruct(error.shape, F32), half, half),
        in_specs=[pl.BlockSpec(memory_space=pltpu.SMEM), pl.BlockSpec(memory_space=pltpu.HBM)]
        + [pl.BlockSpec(memory_space=pltpu.VMEM)] * 3,
        compiler_params=pltpu.CompilerParams(vmem_limit_bytes=32 * 1024 * 1024),
        name="right_terms",
    )(place, after, gradient, error, p_total)


def eliminate(gram):
    rank = gram.shape[0]
    group = 4
    row = lax.broadcasted_iota(jnp.int32, (rank, 2 * rank), 0)
    col = lax.broadcasted_iota(jnp.int32, (rank, 2 * rank), 1)
    work = jnp.where(col == row + rank, 1.0, jnp.concatenate([gram, jnp.zeros_like(gram)], axis=1))
    scale = jnp.zeros_like(work)
    for base in range(0, rank, group):
        at = [base + j for j in range(group)]
        cols = [jnp.broadcast_to(work[:, k:k + 1], work.shape) for k in at]
        rows = [work[k:k + 1, :] for k in at]
        for j, k in enumerate(at):
            pivot = cols[j][k:k + 1, :]
            ratio = jnp.where(row > k, cols[j] * (1.0 / pivot), 0.0)
            scale = jnp.where(row == k, lax.rsqrt(pivot), scale)
            for i in range(j + 1, group):
                cols[i] = cols[i] - ratio * cols[i][k:k + 1, :]
                rows[i] = rows[i] - ratio[at[i]:at[i] + 1, :] * rows[j]
            work = work - ratio * rows[j]
    return (work * scale)[:, rank:]


def finish_kernel(place, mine, other, p_total, merged, error_out, compressed_out, q_out):
    width = merged.shape[1]
    first = place[1] == 0
    sums = jnp.concatenate([jnp.where(first, mine[...], other[...]), jnp.where(first, other[...], mine[...])], axis=0)
    inverse = eliminate(sums[:, width:])
    q_next = jnp.dot(inverse, sums[:, :width], precision=HIGHEST, preferred_element_type=F32) * (1.0 / (NY * NC))
    p_basis = jnp.dot(inverse, p_total[...], precision=HIGHEST, preferred_element_type=F32)
    compressed = lax.dot_general(p_basis, q_next, TN, precision=HIGHEST, preferred_element_type=F32)
    q_out[...] = q_next
    compressed_out[...] = compressed
    error_out[...] = merged[...] - compressed


def finish(place, mine, other, p_total, merged):
    rank = p_total.shape[0]
    return pl.pallas_call(
        finish_kernel,
        out_shape=(
            jax.ShapeDtypeStruct(merged.shape, F32),
            jax.ShapeDtypeStruct(merged.shape, F32),
            jax.ShapeDtypeStruct((rank, merged.shape[1]), F32),
        ),
        in_specs=[pl.BlockSpec(memory_space=pltpu.SMEM)] + [pl.BlockSpec(memory_space=pltpu.VMEM)] * 4,
        compiler_params=pltpu.CompilerParams(vmem_limit_bytes=32 * 1024 * 1024),
        name="finish",
    )(place, mine, other, p_total, merged)


def local(activations, cotangent, kv_weight, error_buffer, q_start):
    c, x, z = (lax.axis_index(a) for a in "cxz")
    place = jnp.stack([x, c, z]).astype(jnp.int32)
    error = error_buffer[0]
    tokens = cotangent.shape[0]
    columns = activations.shape[1] // NX

    with jax.named_scope("exchange"):
        cots, pieces = [cotangent], []
        for k in (2, 1, 3):
            cots.append(swap(cotangent, "x", NX, k))
            for h in range(2):
                piece = lax.dynamic_slice(activations, (h * (tokens // 2), (x ^ k) * columns), (tokens // 2, columns))
                pieces.append(swap(piece, "x", NX, k))
        sub = kv_weight.shape[0] // NC
        mine = lax.dynamic_slice_in_dim(kv_weight, c * sub, sub, axis=0)
        column = jnp.stack(swaps(mine, "x", NX))
        weight = lax.all_gather(column, "z", axis=0)

    with jax.named_scope("gradient"):
        part = gradient_terms(place, activations, cots, pieces)
        part, cots, pieces = lax.optimization_barrier((part, cots, pieces))
        gradient = lax.psum_scatter(part, "z", scatter_dimension=0, tiled=True)

    with jax.named_scope("left"):
        left = left_terms(place, q_start, error, activations, cots, pieces)
        left = tree(list(lax.all_to_all(left, ("y", "c"), 0, 0, tiled=True)))
        left = tree(list(lax.all_to_all(left, "z", 0, 0, tiled=True)))
        left = jnp.broadcast_to(left[None], (NY * NC,) + left.shape)
        p_total = lax.all_to_all(left, ("y", "c"), 0, 0, tiled=True).reshape(q_start.shape[0], -1)

    with jax.named_scope("weight"):
        input_grad = project(place, cotangent, weight, swap(weight, "c", NC, 1))

    with jax.named_scope("sums"):
        merged, keep, give = right_terms(place, input_grad[:16, :128], gradient, error, p_total)
        keep = keep + swap(give, "c", NC, 1)
        keep = tree(swaps(keep, "y", NY))
        keep = tree(swaps(keep, "x", NX))
        keep = keep + swap(keep, "z", NZ, 1)
        keep = tree([keep] + [swap(keep, "z", NZ, k) for k in (2, 4, 6)])
        other = swap(keep, "c", NC, 1)

    with jax.named_scope("finish"):
        error_next, compressed, q_next = finish(place, keep, other, p_total, merged)
    return (input_grad, error_next[None], compressed, q_next)


def solution(mesh):
    fine = Mesh(mesh.devices.reshape(NY, NC, NX, NZ), ("y", "c", "x", "z"))
    dp, fsdp = ("y", "c"), ("x", "z")
    return jax.shard_map(
        local,
        mesh=fine,
        in_specs=(P(dp + fsdp, None), P(dp + fsdp, None), P(fsdp, None), P(dp, fsdp, None), P()),
        out_specs=(P(dp + fsdp, None), P(dp, fsdp, None), P(fsdp, None), P()),
        check_vma=False,
    )
```

time: 238 us -> 236 us (level)
  blocking collectives: 0 us -> 32 us
  Pallas kernels: 16.1 us -> 36.6 us
  waiting for transfers between devices: 118 us -> 97.5 us
  starting transfers between devices: 62.2 us -> 44.9 us
  matrix products: 16.8 us -> 0 us
  local copies, waits for them, and re-layouts: 10.4 us -> 7.89 us
    all_to_all x0 -> x2, blocking collectives: none -> 32 us  [the longest x1 16.3 us: local(): left = tree(list(lax.all_to_all(left, 'z', 0, 0, tiled=True)))]
    pallas_call x1 -> x3, Pallas kernels: 1.03 us -> 23.1 us  [the longest x1 11.6 us: left_terms(): pl.pallas_call(functools.partial(left_kernel, 1 + len(pieces)), out_shape...]
    ppermute x26 -> x25, waiting for transfers between devices: 118 us -> 97.5 us  [swap(): return lax.ppermute(value, axis, [(i, i ^ k) for i in range(size)])]
    dot_general x4 -> x0, matrix products: 16.8 us -> none  [the longest x1 8.74 us: local(): part = jnp.einsum('td,tk->dk', act_x, cot_x, preferred_element_type=F32)]
    all_to_all x2 -> x1, starting transfers between devices: 15.7 us -> 5.73 us  [local(): lax.all_to_all(left, ('y', 'c'), 0, 0, tiled=True)]
    ppermute x26 -> x25, starting transfers between devices: 46.4 us -> 39.1 us  [swap(): return lax.ppermute(value, axis, [(i, i ^ k) for i in range(size)])]
    all_to_all x2 -> x0, local copies, waits for them, and re-layouts: 6.58 us -> none  [the longest x1 5.74 us: local(): act_x = lax.all_to_all(activations, 'x', 1, 0, tiled=True)]
    dynamic_slice x0 -> x1, local copies, waits for them, and re-layouts: none -> 3.86 us  [local(): lax.dynamic_slice(activations, (h * (tokens // 2), (x ^ k) * columns), (t...]
  transfers between devices with their start and end apart: 30 -> 28, of which waited for: 17 -> 17; matrix products, arithmetic and copies ran while one was open for 8% -> 3% of each run, Pallas kernels for 3% -> 13%
where the time goes in v3:
time: 236 us; the launch traced here: 235 us
  waiting for transfers between devices  97.5 us (41%)
  starting transfers between devices  44.9 us (19%)
  Pallas kernels  36.6 us (16%)
  blocking collectives  32 us (14%)
  between operations  14.2 us (6%)
  local copies, waits for them, and re-layouts  7.89 us (3%)
    ppermute x25, waiting for transfers between devices, swap(): return lax.ppermute(value, axis, [(i, i ^ k) for i in range(size)])  97.5 us
    ppermute x25, starting transfers between devices, swap(): return lax.ppermute(value, axis, [(i, i ^ k) for i in range(size)])  39.1 us
    all_to_all x1, blocking collectives, local(): left = tree(list(lax.all_to_all(left, 'z', 0, 0, tiled=True)))  16.3 us
    all_to_all x1, blocking collectives, local(): left = tree(list(lax.all_to_all(left, ('y', 'c'), 0, 0, tiled=True)))  15.8 us
    pallas_call x1, Pallas kernels, left_terms(): pl.pallas_call(functools.partial(left_kernel, 1 + len(pieces)), out_shape...  11.6 us
    pallas_call x1, Pallas kernels, gradient_terms(): pl.pallas_call(functools.partial(gradient_kernel, 1 + len(pieces)), out_s...  10.3 us
    pallas_call x1, Pallas kernels, project(): pl.pallas_call(project_kernel, out_shape=jax.ShapeDtypeStruct((tokens, NX...  8.22 us
    all_to_all x1, starting transfers between devices, local(): lax.all_to_all(left, ('y', 'c'), 0, 0, tiled=True)  5.73 us
  transfers between devices with their start and end apart: 28, of which 17 were waited for; matrix products, arithmetic and copies ran while one was open for 3% of the time, Pallas kernels for 13%

profile of v3, /device:TPU:1, one launch (start us, length us, event | category | flops | bytes accessed | tf_op | source)
XLA Modules:
  0.0 234.7 jit_solution(5816378871882546568)
XLA Ops:
  8.1 3.7 %collective-permute-start.1 = (bf16[128,512]{1,0:T(8,128)(2,1)S(1)}, bf16[128,512]{1,0:T(8,128)(2,1)S(1)}, u32[]{:S(2)}, u32[]{:S(2)}) collective-permute-start(bf16[128,512]{1,0:T(8,128)(2,1)S(1)} %constant_dynamic-slice_fusion.6), channel_id=1, source_target_pairs={{0,16},{8,24},{16,0},{24,8},{1,17},{9,25},{17,1},{25,9},{2,18},{10... | collective-permute-start | bytes 393224 | tf_op jit(solution)/shard_map/exchange/ppermute | solution.py:20
  14.2 3.7 %collective-permute-done = bf16[128,512]{1,0:T(8,128)(2,1)S(1)} collective-permute-done((bf16[128,512]{1,0:T(8,128)(2,1)S(1)}, bf16[128,512]{1,0:T(8,128)(2,1)S(1)}, u32[]{:S(2)}, u32[]{:S(2)}) %collective-permute-start) | collective-permute-done | bytes 131104 | tf_op jit(solution)/shard_map/exchange/ppermute | solution.py:20
  20.6 3.9 %constant_dynamic-slice_fusion = (bf16[160,2048]{1,0:T(8,128)(2,1)S(1)}, bf16[160,2048]{1,0:T(8,128)(2,1)}, bf16[160,2048]{1,0:T(8,128)(2,1)}, bf16[160,2048]{1,...) fusion(bf16[320,8192]{1,0:T(8,128)(2,1)} %refs_4_.3, s32[]{:T(128)S(6)} %select_n.18, ...), kind=kLoop, calls=%fused_computation.20 | loop fusion | bytes 7864332 | tf_op jit(solution)/shard_map/exchange/dynamic_slice | solution.py:293
  31.0 24.0 %collective-permute-done.6.refs_3_ = bf16[320,512]{1,0:T(8,128)(2,1)S(1)} collective-permute-done((bf16[320,512]{1,0:T(8,128)(2,1)S(1)}, bf16[320,512]{1,0:T(8,128)(2,1)S(1)}, u32[]{:S(2)}, u32[]{:S(2)}) %collective-permute-start.6) | collective-permute-done | bytes 327712 | tf_op jit(solution)/shard_map/exchange/ppermute | solution.py:20
  60.8 8.2 %collective-permute-done.11.refs_9_ = bf16[160,2048]{1,0:T(8,128)(2,1)S(1)} collective-permute-done((bf16[160,2048]{1,0:T(8,128)(2,1)}, bf16[160,2048]{1,0:T(8,128)(2,1)S(1)}, u32[]{:S(2)}, u32[]{:S(2)}) %collective-permute-start.11) | collective-permute-done | bytes 655392 | tf_op jit(solution)/shard_map/exchange/ppermute | solution.py:20
  69.0 13.2 %collective-permute-done.9.refs_7_ = bf16[160,2048]{1,0:T(8,128)(2,1)} collective-permute-done((bf16[160,2048]{1,0:T(8,128)(2,1)}, bf16[160,2048]{1,0:T(8,128)(2,1)}, u32[]{:S(2)}, u32[]{:S(2)}) %collective-permute-start.9) | collective-permute-done | bytes 655392 | tf_op jit(solution)/shard_map/exchange/ppermute | solution.py:20
  82.2 12.5 %collective-permute-done.8.refs_6_ = bf16[160,2048]{1,0:T(8,128)(2,1)S(1)} collective-permute-done((bf16[160,2048]{1,0:T(8,128)(2,1)}, bf16[160,2048]{1,0:T(8,128)(2,1)S(1)}, u32[]{:S(2)}, u32[]{:S(2)}) %collective-permute-start.8) | collective-permute-done | bytes 655392 | tf_op jit(solution)/shard_map/exchange/ppermute | solution.py:20
  94.7 14.1 %collective-permute-done.7.refs_5_ = bf16[160,2048]{1,0:T(8,128)(2,1)} collective-permute-done((bf16[160,2048]{1,0:T(8,128)(2,1)}, bf16[160,2048]{1,0:T(8,128)(2,1)}, u32[]{:S(2)}, u32[]{:S(2)}) %collective-permute-start.7) | collective-permute-done | bytes 655392 | tf_op jit(solution)/shard_map/exchange/ppermute | solution.py:20
  108.9 10.3 %gradient_terms.1 = f32[8,512,256]{2,1,0:T(8,128)} custom-call(s32[3]{0:T(128)} %pad_add_fusion.place, bf16[320,512]{1,0:T(8,128)(2,1)} %refs_0_.2, bf16[320,512]{1,0:T(8,128)(2,1)} %copy-done.11, bf16[320,512]{1,0:T(8,128)(2,1)} %copy-done.10, bf16[320,512]{1,0:T(8,128)(2,1)} %copy-done.9, bf16[320,8192]{1,0:T(8,128)(2,1)} %refs_4_.3, ...), custom_call_target="tpu_custom_call" | custom-call | flops 2684354560 | bytes 9437184 | tf_op jit(solution)/shard_map/gradient/gradient_terms/pallas_call | solution.py:104
  119.2 5.5 %collective-permute-start.3 = (bf16[8,4,128,512]{3,2,1,0:T(8,128)(2,1)}, bf16[8,4,128,512]{3,2,1,0:T(8,128)(2,1)}, u32[]{:S(2)}, u32[]{:S(2)}) collective-permute-start(bf16[8,4,128,512]{3,2,1,0:T(8,128)(2,1)} %bitcast.20), channel_id=1, source_target_pairs={{0,32},{32,0},{1,33},{33,1},{2,34},{34,2},{3,35},{35,3},{4,36},{36... | collective-permute-start | bytes 12582920 | tf_op jit(solution)/shard_map/weight/ppermute | solution.py:20
  124.8 11.6 %left_terms.1 = f32[8,8,8,256]{3,2,1,0:T(8,128)} custom-call(s32[3]{0:T(128)} %pad_add_fusion.place, f32[64,512]{1,0:T(8,128)} %q.1, f32[256,512]{1,0:T(8,128)} %bitcast.16, bf16[320,512]{1,0:T(8,128)(2,1)} %refs_0_.2, bf16[320,512]{1,0:T(8,128)(2,1)} %copy-done.11, bf16[320,512]{1,0:T(8,128)(2,1)} %copy-done.10, bf16[320,512]{1,0:T(8,128)(2,1)} %copy-done.9, ...), custom_call_target="tpu_custom_call" | custom-call | flops 1006632960 | bytes 5242880 | tf_op jit(solution)/shard_map/left/left_terms/pallas_call | solution.py:129
  136.4 15.8 %all_to_all.15 = f32[8,8,8,256]{3,2,1,0:T(8,128)S(1)} all-to-all(f32[8,8,8,256]{3,2,1,0:T(8,128)} %left_terms.1), channel_id=1, replica_groups=mesh['y'=4,'c'=2,'x'=4,'z'=8] {'y','c'}, dimensions={0} | all-to-all | bytes 1048576 | tf_op jit(solution)/shard_map/left/all_to_all | solution.py:307
  152.2 16.3 %all_to_all.16 = f32[8,8,256]{2,1,0:T(8,128)S(1)} all-to-all(f32[8,8,256]{2,1,0:T(8,128)S(1)} %fusion.2), channel_id=1, replica_groups=mesh['y'=4,'c'=2,'x'=4,'z'=8] {'z'}, dimensions={0} | all-to-all | bytes 131072 | tf_op jit(solution)/shard_map/left/all_to_all | solution.py:308
  169.1 5.7 %all-to-all-start.2 = ((f32[8,8,256]{2,1,0:T(8,128)}), f32[8,8,256]{2,1,0:T(8,128)S(1)}, u32[]{:S(2)}, u32[]{:S(2)}) async-start(f32[8,8,256]{2,1,0:T(8,128)} %broadcast_in_dim.12), calls=%async_computation.3 | async-start | bytes 131072 | tf_op jit(solution)/shard_map/left/all_to_all | solution.py:310
  174.9 8.2 %project.1 = bf16[320,8192]{1,0:T(8,128)(2,1)} custom-call(s32[3]{0:T(128)} %pad_add_fusion.place, bf16[320,512]{1,0:T(8,128)(2,1)} %refs_0_.2, bf16[8,4,128,512]{3,2,1,0:T(8,128)(2,1)} %bitcast.21, bf16[8,4,128,512]{3,2,1,0:T(8,128)(2,1)} %collective-permute-done.3.other), custom_call_target="tpu_custom_call" | custom-call | flops 2684354560 | bytes 13631488 | tf_op jit(solution)/shard_map/weight/project/pallas_call | solution.py:184
  187.4 2.7 %collective-permute-start.16 = (f32[32,576]{1,0:T(8,128)S(1)}, f32[32,576]{1,0:T(8,128)S(1)}, u32[]{:S(2)}, u32[]{:S(2)}) collective-permute-start(f32[32,576]{1,0:T(8,128)S(1)} %add.127), channel_id=1, source_target_pairs={{0,192},{64,128},{128,64},{192,0},{1,193},{65,129},{129,65},{193,1... | collective-permute-start | bytes 221192 | tf_op jit(solution)/shard_map/sums/ppermute | solution.py:20
  190.7 2.6 %collective-permute-done.16 = f32[32,576]{1,0:T(8,128)S(1)} collective-permute-done((f32[32,576]{1,0:T(8,128)S(1)}, f32[32,576]{1,0:T(8,128)S(1)}, u32[]{:S(2)}, u32[]{:S(2)}) %collective-permute-start.16) | collective-permute-done | bytes 73760 | tf_op jit(solution)/shard_map/sums/ppermute | solution.py:20
  194.9 2.2 collective-permute-start.19
  199.5 2.5 %collective-permute-done.18 = f32[32,576]{1,0:T(8,128)S(1)} collective-permute-done((f32[32,576]{1,0:T(8,128)S(1)}, f32[32,576]{1,0:T(8,128)S(1)}, u32[]{:S(2)}, u32[]{:S(2)}) %collective-permute-start.18) | collective-permute-done | bytes 73760 | tf_op jit(solution)/shard_map/sums/ppermute | solution.py:20
  202.1 3.3 %collective-permute-done.20 = f32[32,576]{1,0:T(8,128)S(1)} collective-permute-done((f32[32,576]{1,0:T(8,128)S(1)}, f32[32,576]{1,0:T(8,128)S(1)}, u32[]{:S(2)}, u32[]{:S(2)}) %collective-permute-start.20) | collective-permute-done | bytes 73760 | tf_op jit(solution)/shard_map/sums/ppermute | solution.py:20
  207.4 2.9 %collective-permute-start.22 = (f32[32,576]{1,0:T(8,128)S(1)}, f32[32,576]{1,0:T(8,128)S(1)}, u32[]{:S(2)}, u32[]{:S(2)}) collective-permute-start(f32[32,576]{1,0:T(8,128)S(1)} %add.134), channel_id=1, source_target_pairs={{0,4},{1,5},{2,6},{3,7},{4,0},{5,1},{6,2},{7,3},{8,12},{9,13},{10,... | collective-permute-start | bytes 221192 | tf_op jit(solution)/shard_map/sums/ppermute | solution.py:20
  211.2 4.0 %collective-permute-done.22 = f32[32,576]{1,0:T(8,128)S(1)} collective-permute-done((f32[32,576]{1,0:T(8,128)S(1)}, f32[32,576]{1,0:T(8,128)S(1)}, u32[]{:S(2)}, u32[]{:S(2)}) %collective-permute-start.22) | collective-permute-done | bytes 73760 | tf_op jit(solution)/shard_map/sums/ppermute | solution.py:20
  216.6 5.1 %collective-permute-start.24 = (f32[32,576]{1,0:T(8,128)S(1)}, f32[32,576]{1,0:T(8,128)S(1)}, u32[]{:S(2)}, u32[]{:S(2)}) collective-permute-start(f32[32,576]{1,0:T(8,128)S(1)} %add_add_fusion.mine), channel_id=1, source_target_pairs={{0,32},{32,0},{1,33},{33,1},{2,34},{34,2},{3,35},{35,3},{4,36},{36... | collective-permute-start | bytes 221192 | tf_op jit(solution)/shard_map/sums/ppermute | solution.py:20
  222.6 5.3 %finish.1 = (f32[256,512]{1,0:T(8,128)}, f32[256,512]{1,0:T(8,128)}, f32[64,512]{1,0:T(8,128)}) custom-call(s32[3]{0:T(128)S(1)} %copy-done.3, f32[32,576]{1,0:T(8,128)S(1)} %add_add_fusion.mine, f32[32,576]{1,0:T(8,128)S(1)} %collective-permute-done.24.other, f32[64,256]{1,0:T(8,128)S(1)} %bitcast.19, f32[256,512]{1,0:T(8,128)S(1)} %get-tuple-element.34.merged), custom_call_target="tpu_custom_call" | custom-call | tf_op jit(solution)/shard_map/finish/finish/pallas_call | solution.py:268
  (79 shorter events, 33.3 us)
Async XLA Ops:
  7.2 112.0 %all-gather.3.cloned.1.call-start = ((), (), s32[]{:S(2)}) async-start(), calls=%async_computation.5 | async-start | bytes 4718592 | tf_op jit(solution)/shard_map/exchange/all_gather | solution.py:298
  8.1 6.0 %collective-permute-start.1 = (bf16[128,512]{1,0:T(8,128)(2,1)S(1)}, bf16[128,512]{1,0:T(8,128)(2,1)S(1)}, u32[]{:S(2)}, u32[]{:S(2)}) collective-permute-start(bf16[128,512]{1,0:T(8,128)(2,1)S(1)} %constant_dynamic-slice_fusion.6), channel_id=1, source_target_pairs={{0,16},{8,24},{16,0},{24,8},{1,17},{9,25},{17,1},{25,9},{2,18},{10... | collective-permute-start | bytes 393224 | tf_op jit(solution)/shard_map/exchange/ppermute | solution.py:20
  11.8 6.0 %collective-permute-start = (bf16[128,512]{1,0:T(8,128)(2,1)S(1)}, bf16[128,512]{1,0:T(8,128)(2,1)S(1)}, u32[]{:S(2)}, u32[]{:S(2)}) collective-permute-start(bf16[128,512]{1,0:T(8,128)(2,1)S(1)} %constant_dynamic-slice_fusion.6), channel_id=1, source_target_pairs={{0,8},{8,0},{16,24},{24,16},{1,9},{9,1},{17,25},{25,17},{2,10},{10... | collective-permute-start | bytes 393224 | tf_op jit(solution)/shard_map/exchange/ppermute | solution.py:20
  12.1 7.5 %collective-permute-start.2 = (bf16[128,512]{1,0:T(8,128)(2,1)S(1)}, bf16[128,512]{1,0:T(8,128)(2,1)S(1)}, u32[]{:S(2)}, u32[]{:S(2)}) collective-permute-start(bf16[128,512]{1,0:T(8,128)(2,1)S(1)} %constant_dynamic-slice_fusion.6), channel_id=1, source_target_pairs={{0,24},{8,16},{16,8},{24,0},{1,25},{9,17},{17,9},{25,1},{2,26},{10... | collective-permute-start | bytes 393224 | tf_op jit(solution)/shard_map/exchange/ppermute | solution.py:20
  20.5 163.3 %reduce-scatter.2.cloned.1.call-start = ((), (), s32[]{:S(2)}) async-start(), calls=%async_computation.4 | async-start | bytes 4718592 | tf_op jit(solution)/shard_map/gradient/reduce_scatter | solution.py:303
  24.4 33.7 %collective-permute-start.12 = (bf16[160,2048]{1,0:T(8,128)(2,1)S(1)}, bf16[160,2048]{1,0:T(8,128)(2,1)S(1)}, u32[]{:S(2)}, u32[]{:S(2)}) collective-permute-start(bf16[160,2048]{1,0:T(8,128)(2,1)S(1)} %get-tuple-element.38), channel_id=1, source_target_pairs={{0,24},{8,16},{16,8},{24,0},{1,25},{9,17},{17,9},{25,1},{2,26},{10... | collective-permute-start | bytes 1966088 | tf_op jit(solution)/shard_map/exchange/ppermute | solution.py:20
  25.0 30.0 %collective-permute-start.6 = (bf16[320,512]{1,0:T(8,128)(2,1)S(1)}, bf16[320,512]{1,0:T(8,128)(2,1)S(1)}, u32[]{:S(2)}, u32[]{:S(2)}) collective-permute-start(bf16[320,512]{1,0:T(8,128)(2,1)S(1)} %copy-done.4), channel_id=1, source_target_pairs={{0,24},{8,16},{16,8},{24,0},{1,25},{9,17},{17,9},{25,1},{2,26},{10... | collective-permute-start | bytes 983048 | tf_op jit(solution)/shard_map/exchange/ppermute | solution.py:20
  27.1 27.9 %collective-permute-start.5 = (bf16[320,512]{1,0:T(8,128)(2,1)S(1)}, bf16[320,512]{1,0:T(8,128)(2,1)S(1)}, u32[]{:S(2)}, u32[]{:S(2)}) collective-permute-start(bf16[320,512]{1,0:T(8,128)(2,1)S(1)} %copy-done.4), channel_id=1, source_target_pairs={{0,8},{8,0},{16,24},{24,16},{1,9},{9,1},{17,25},{25,17},{2,10},{10... | collective-permute-start | bytes 983048 | tf_op jit(solution)/shard_map/exchange/ppermute | solution.py:20
  27.1 29.4 %collective-permute-start.4 = (bf16[320,512]{1,0:T(8,128)(2,1)S(1)}, bf16[320,512]{1,0:T(8,128)(2,1)S(1)}, u32[]{:S(2)}, u32[]{:S(2)}) collective-permute-start(bf16[320,512]{1,0:T(8,128)(2,1)S(1)} %copy-done.4), channel_id=1, source_target_pairs={{0,16},{8,24},{16,0},{24,8},{1,17},{9,25},{17,1},{25,9},{2,18},{10... | collective-permute-start | bytes 983048 | tf_op jit(solution)/shard_map/exchange/ppermute | solution.py:20
  28.8 40.2 %collective-permute-start.11 = (bf16[160,2048]{1,0:T(8,128)(2,1)}, bf16[160,2048]{1,0:T(8,128)(2,1)S(1)}, u32[]{:S(2)}, u32[]{:S(2)}) collective-permute-start(bf16[160,2048]{1,0:T(8,128)(2,1)} %get-tuple-element.39), channel_id=1, source_target_pairs={{0,24},{8,16},{16,8},{24,0},{1,25},{9,17},{17,9},{25,1},{2,26},{10... | collective-permute-start | bytes 1966088 | tf_op jit(solution)/shard_map/exchange/ppermute | solution.py:20
  55.0 14.0 %collective-permute-start.10 = (bf16[160,2048]{1,0:T(8,128)(2,1)}, bf16[160,2048]{1,0:T(8,128)(2,1)S(1)}, u32[]{:S(2)}, u32[]{:S(2)}) collective-permute-start(bf16[160,2048]{1,0:T(8,128)(2,1)} %get-tuple-element.40), channel_id=1, source_target_pairs={{0,8},{8,0},{16,24},{24,16},{1,9},{9,1},{17,25},{25,17},{2,10},{10... | collective-permute-start | bytes 1966088 | tf_op jit(solution)/shard_map/exchange/ppermute | solution.py:20
  55.0 27.2 %collective-permute-start.9 = (bf16[160,2048]{1,0:T(8,128)(2,1)}, bf16[160,2048]{1,0:T(8,128)(2,1)}, u32[]{:S(2)}, u32[]{:S(2)}) collective-permute-start(bf16[160,2048]{1,0:T(8,128)(2,1)} %get-tuple-element.41), channel_id=1, source_target_pairs={{0,8},{8,0},{16,24},{24,16},{1,9},{9,1},{17,25},{25,17},{2,10},{10... | collective-permute-start | bytes 1966088 | tf_op jit(solution)/shard_map/exchange/ppermute | solution.py:20
  57.2 37.5 %collective-permute-start.8 = (bf16[160,2048]{1,0:T(8,128)(2,1)}, bf16[160,2048]{1,0:T(8,128)(2,1)S(1)}, u32[]{:S(2)}, u32[]{:S(2)}) collective-permute-start(bf16[160,2048]{1,0:T(8,128)(2,1)} %get-tuple-element.42), channel_id=1, source_target_pairs={{0,16},{8,24},{16,0},{24,8},{1,17},{9,25},{17,1},{25,9},{2,18},{10... | collective-permute-start | bytes 1966088 | tf_op jit(solution)/shard_map/exchange/ppermute | solution.py:20
  58.1 50.7 %collective-permute-start.7 = (bf16[160,2048]{1,0:T(8,128)(2,1)}, bf16[160,2048]{1,0:T(8,128)(2,1)}, u32[]{:S(2)}, u32[]{:S(2)}) collective-permute-start(bf16[160,2048]{1,0:T(8,128)(2,1)} %get-tuple-element.43), channel_id=1, source_target_pairs={{0,16},{8,24},{16,0},{24,8},{1,17},{9,25},{17,1},{25,9},{2,18},{10... | collective-permute-start | bytes 1966088 | tf_op jit(solution)/shard_map/exchange/ppermute | solution.py:20
  119.2 55.6 %collective-permute-start.3 = (bf16[8,4,128,512]{3,2,1,0:T(8,128)(2,1)}, bf16[8,4,128,512]{3,2,1,0:T(8,128)(2,1)}, u32[]{:S(2)}, u32[]{:S(2)}) collective-permute-start(bf16[8,4,128,512]{3,2,1,0:T(8,128)(2,1)} %bitcast.20), channel_id=1, source_target_pairs={{0,32},{32,0},{1,33},{33,1},{2,34},{34,2},{3,35},{35,3},{4,36},{36... | collective-permute-start | bytes 12582920 | tf_op jit(solution)/shard_map/weight/ppermute | solution.py:20
  169.1 14.7 %all-to-all-start.2 = ((f32[8,8,256]{2,1,0:T(8,128)}), f32[8,8,256]{2,1,0:T(8,128)S(1)}, u32[]{:S(2)}, u32[]{:S(2)}) async-start(f32[8,8,256]{2,1,0:T(8,128)} %broadcast_in_dim.12), calls=%async_computation.3 | async-start | bytes 131072 | tf_op jit(solution)/shard_map/left/all_to_all | solution.py:310
  187.4 6.0 %collective-permute-start.16 = (f32[32,576]{1,0:T(8,128)S(1)}, f32[32,576]{1,0:T(8,128)S(1)}, u32[]{:S(2)}, u32[]{:S(2)}) collective-permute-start(f32[32,576]{1,0:T(8,128)S(1)} %add.127), channel_id=1, source_target_pairs={{0,192},{64,128},{128,64},{192,0},{1,193},{65,129},{129,65},{193,1... | collective-permute-start | bytes 221192 | tf_op jit(solution)/shard_map/sums/ppermute | solution.py:20
  190.1 4.8 %collective-permute-start.15 = (f32[32,576]{1,0:T(8,128)S(1)}, f32[32,576]{1,0:T(8,128)S(1)}, u32[]{:S(2)}, u32[]{:S(2)}) collective-permute-start(f32[32,576]{1,0:T(8,128)S(1)} %add.127), channel_id=1, source_target_pairs={{0,128},{64,192},{128,0},{192,64},{1,129},{65,193},{129,1},{193,65... | collective-permute-start | bytes 221192 | tf_op jit(solution)/shard_map/sums/ppermute | solution.py:20
  194.9 4.6 %collective-permute-start.19 = (f32[32,576]{1,0:T(8,128)S(1)}, f32[32,576]{1,0:T(8,128)S(1)}, u32[]{:S(2)}, u32[]{:S(2)}) collective-permute-start(f32[32,576]{1,0:T(8,128)S(1)} %add_add_fusion.2), channel_id=1, source_target_pairs={{0,24},{8,16},{16,8},{24,0},{1,25},{9,17},{17,9},{25,1},{2,26},{10... | collective-permute-start | bytes 221192 | tf_op jit(solution)/shard_map/sums/ppermute | solution.py:20
  197.1 4.8 %collective-permute-start.18 = (f32[32,576]{1,0:T(8,128)S(1)}, f32[32,576]{1,0:T(8,128)S(1)}, u32[]{:S(2)}, u32[]{:S(2)}) collective-permute-start(f32[32,576]{1,0:T(8,128)S(1)} %add_add_fusion.2), channel_id=1, source_target_pairs={{0,16},{8,24},{16,0},{24,8},{1,17},{9,25},{17,1},{25,9},{2,18},{10... | collective-permute-start | bytes 221192 | tf_op jit(solution)/shard_map/sums/ppermute | solution.py:20
  205.4 5.8 %collective-permute-start.23 = (f32[32,576]{1,0:T(8,128)S(1)}, f32[32,576]{1,0:T(8,128)S(1)}, u32[]{:S(2)}, u32[]{:S(2)}) collective-permute-start(f32[32,576]{1,0:T(8,128)S(1)} %add.134), channel_id=1, source_target_pairs={{0,6},{1,7},{2,4},{3,5},{4,2},{5,3},{6,0},{7,1},{8,14},{9,15},{10,... | collective-permute-start | bytes 221192 | tf_op jit(solution)/shard_map/sums/ppermute | solution.py:20
  207.4 7.7 %collective-permute-start.22 = (f32[32,576]{1,0:T(8,128)S(1)}, f32[32,576]{1,0:T(8,128)S(1)}, u32[]{:S(2)}, u32[]{:S(2)}) collective-permute-start(f32[32,576]{1,0:T(8,128)S(1)} %add.134), channel_id=1, source_target_pairs={{0,4},{1,5},{2,6},{3,7},{4,0},{5,1},{6,2},{7,3},{8,12},{9,13},{10,... | collective-permute-start | bytes 221192 | tf_op jit(solution)/shard_map/sums/ppermute | solution.py:20
  210.3 6.2 %collective-permute-start.21 = (f32[32,576]{1,0:T(8,128)S(1)}, f32[32,576]{1,0:T(8,128)S(1)}, u32[]{:S(2)}, u32[]{:S(2)}) collective-permute-start(f32[32,576]{1,0:T(8,128)S(1)} %add.134), channel_id=1, source_target_pairs={{0,2},{1,3},{2,0},{3,1},{4,6},{5,7},{6,4},{7,5},{8,10},{9,11},{10,... | collective-permute-start | bytes 221192 | tf_op jit(solution)/shard_map/sums/ppermute | solution.py:20
  216.6 6.0 %collective-permute-start.24 = (f32[32,576]{1,0:T(8,128)S(1)}, f32[32,576]{1,0:T(8,128)S(1)}, u32[]{:S(2)}, u32[]{:S(2)}) collective-permute-start(f32[32,576]{1,0:T(8,128)S(1)} %add_add_fusion.mine), channel_id=1, source_target_pairs={{0,32},{32,0},{1,33},{33,1},{2,34},{34,2},{3,35},{35,3},{4,36},{36... | collective-permute-start | bytes 221192 | tf_op jit(solution)/shard_map/sums/ppermute | solution.py:20
  (16 other events, 251.5 us)
Sparse Core Ops, SparseCore 0:
  20.6 56.7 all-gather.2
  119.3 63.8 reduce-scatter.1

commit v4 on v3

--- a/solution.py
+++ b/solution.py
@@ -44,6 +44,41 @@
     return value[:rank] + (value[rank:2 * rank] + value[2 * rank:])
 
 
+PARTNERS = (2, 1, 3)
+
+
+def pack_kernel(place, act, cot, *outs):
+    rows, columns = outs[0].shape[0], act.shape[1]
+    for j in range(len(PARTNERS)):
+        @pl.when(pl.program_id(0) == j)
+        def _():
+            for h in range(2):
+                outs[2 * j + h][:, :columns] = act[h * rows:(h + 1) * rows, :]
+                outs[2 * j + h][:, columns:] = cot[h * rows:(h + 1) * rows, :]
+
+
+def pack(place, activations, cotangent):
+    tokens, width = cotangent.shape
+    columns = activations.shape[1] // NX
+    shape = (tokens // 2, columns + width)
+    return pl.pallas_call(
+        pack_kernel,
+        out_shape=(jax.ShapeDtypeStruct(shape, BF16),) * (2 * len(PARTNERS)),
+        grid_spec=pltpu.PrefetchScalarGridSpec(
+            num_scalar_prefetch=1,
+            grid=(len(PARTNERS),),
+            in_specs=[
+                pl.BlockSpec((tokens, columns), lambda j, place: (0, place[3 + j])),
+                pl.BlockSpec((tokens, width), lambda j, place: (0, 0)),
+            ],
+            out_specs=[pl.BlockSpec(shape, lambda j, place: (0, 0))] * (2 * len(PARTNERS)),
+        ),
+        cost_estimate=pl.CostEstimate(flops=0, bytes_accessed=8 * tokens * columns * 2, transcendentals=0),
+        compiler_params=pltpu.CompilerParams(vmem_limit_bytes=60 * 1024 * 1024),
+        name="pack",
+    )(place, activations, cotangent)
+
+
 def load_tokens(refs, rows):
     at = 0
     for ref in refs:
@@ -52,8 +87,8 @@
 
 
 def gradient_kernel(count, place, *refs):
-    cots, acts = refs[:NX], refs[NX:NX + count]
-    gradient, lhs, cot_rows, rows = refs[NX + count:]
+    cots, acts = refs[:count], refs[count:2 * count]
+    gradient, lhs, cot_rows, rows = refs[2 * count:]
 
     @pl.when(pl.program_id(0) == 0)
     def _():
@@ -61,12 +96,14 @@
         lhs[...] = cot_rows[...].T
 
     load_tokens(acts, rows)
-    gradient[0] = jnp.dot(lhs[...], rows[...], preferred_element_type=F32)
+    block = gradient.shape[2]
+    for i in range(gradient.shape[0]):
+        gradient[i] = jnp.dot(lhs[...], rows[:, i * block:(i + 1) * block], preferred_element_type=F32)
 
 
 def left_kernel(count, place, q, error, *refs):
-    cots, acts = refs[:NX], refs[NX:NX + count]
-    left, lhs, cot_rows, rows = refs[NX + count:]
+    cots, acts = refs[:count], refs[count:2 * count]
+    left, lhs, cot_rows, rows = refs[2 * count:]
     z = pl.program_id(0)
     block = acts[0].shape[1]
 
@@ -88,42 +125,48 @@
         left[:, 0] = left[:, 0] + own.reshape(NY * NC, -1, block)
 
 
-def token_specs(activations, cots, pieces):
-    block = activations.shape[1] // (NX * NZ)
-    tokens, width = cots[0].shape
-    specs = [pl.BlockSpec((tokens, width), lambda z, place: (0, 0))] * NX
-    specs.append(pl.BlockSpec((tokens, block), lambda z, place: (0, place[0] * NZ + z)))
-    specs += [pl.BlockSpec((piece.shape[0], block), lambda z, place: (0, z)) for piece in pieces]
+def token_specs(activations, cotangent, pieces, steps):
+    tokens, width = cotangent.shape
+    block = activations.shape[1] // (NX * steps)
+    part = pieces[0].shape[0]
+    last = block * steps // width
+    specs = [pl.BlockSpec((tokens, width), lambda i, place: (0, 0))]
+    specs += [pl.BlockSpec((part, width), lambda i, place: (0, last))] * len(pieces)
+    specs.append(pl.BlockSpec((tokens, block), lambda i, place: (0, place[0] * steps + i)))
+    specs += [pl.BlockSpec((part, block), lambda i, place: (0, i))] * len(pieces)
     return specs
 
 
-def gradient_terms(place, activations, cots, pieces):
-    width = cots[0].shape[1]
-    tokens = NX * cots[0].shape[0]
-    block = activations.shape[1] // (NX * NZ)
+def gradient_terms(place, activations, cotangent, pieces):
+    width = cotangent.shape[1]
+    tokens = NX * cotangent.shape[0]
+    columns = activations.shape[1] // NX
+    steps = 4
     return pl.pallas_call(
         functools.partial(gradient_kernel, 1 + len(pieces)),
-        out_shape=jax.ShapeDtypeStruct((NZ, width, block), F32),
+        out_shape=jax.ShapeDtypeStruct((NZ, width, columns // NZ), F32),
         grid_spec=pltpu.PrefetchScalarGridSpec(
             num_scalar_prefetch=1,
-            grid=(NZ,),
-            in_specs=token_specs(activations, cots, pieces),
-            out_specs=pl.BlockSpec((1, width, block), lambda z, place: (z, 0, 0)),
-            scratch_shapes=[pltpu.VMEM(shape, BF16) for shape in ((width, tokens), (tokens, width), (tokens, block))],
+            grid=(steps,),
+            in_specs=token_specs(activations, cotangent, pieces, steps),
+            out_specs=pl.BlockSpec((NZ // steps, width, columns // NZ), lambda i, place: (i, 0, 0)),
+            scratch_shapes=[
+                pltpu.VMEM(shape, BF16) for shape in ((width, tokens), (tokens, width), (tokens, columns // steps))
+            ],
         ),
         cost_estimate=pl.CostEstimate(
-            flops=2 * width * tokens * block * NZ,
-            bytes_accessed=(2 * tokens + 4 * width) * block * NZ,
+            flops=2 * width * tokens * columns,
+            bytes_accessed=(2 * tokens + 4 * width) * columns,
             transcendentals=0,
         ),
         compiler_params=pltpu.CompilerParams(vmem_limit_bytes=60 * 1024 * 1024),
         name="gradient_terms",
-    )(place, *cots, activations, *pieces)
-
-
-def left_terms(place, q_start, error, activations, cots, pieces):
+    )(place, cotangent, *pieces, activations, *pieces)
+
+
+def left_terms(place, q_start, error, activations, cotangent, pieces):
     rank, width = q_start.shape
-    tokens = NX * cots[0].shape[0]
+    tokens = NX * cotangent.shape[0]
     block = activations.shape[1] // (NX * NZ)
     shares = NY * NC
     return pl.pallas_call(
@@ -136,7 +179,7 @@
                 pl.BlockSpec((rank, width), lambda z, place: (0, 0)),
                 pl.BlockSpec((block, width), lambda z, place: (0, 0)),
             ]
-            + token_specs(activations, cots, pieces),
+            + token_specs(activations, cotangent, pieces, NZ),
             out_specs=pl.BlockSpec((shares, 1, rank // shares, block), lambda z, place: (0, z, 0, 0)),
             scratch_shapes=[pltpu.VMEM(shape, BF16) for shape in ((3 * rank, tokens), (tokens, width), (tokens, block))],
         ),
@@ -147,7 +190,7 @@
         ),
         compiler_params=pltpu.CompilerParams(vmem_limit_bytes=60 * 1024 * 1024),
         name="left_terms",
-    )(place, q_start, error, *cots, activations, *pieces)
+    )(place, q_start, error, cotangent, *pieces, activations, *pieces)
 
 
 def project_kernel(place, cot, own, other, out, rows, arrived):
@@ -280,30 +323,25 @@
 
 def local(activations, cotangent, kv_weight, error_buffer, q_start):
     c, x, z = (lax.axis_index(a) for a in "cxz")
-    place = jnp.stack([x, c, z]).astype(jnp.int32)
+    place = jnp.stack([x, c, z] + [x ^ k for k in PARTNERS]).astype(jnp.int32)
     error = error_buffer[0]
-    tokens = cotangent.shape[0]
-    columns = activations.shape[1] // NX
 
     with jax.named_scope("exchange"):
-        cots, pieces = [cotangent], []
-        for k in (2, 1, 3):
-            cots.append(swap(cotangent, "x", NX, k))
-            for h in range(2):
-                piece = lax.dynamic_slice(activations, (h * (tokens // 2), (x ^ k) * columns), (tokens // 2, columns))
-                pieces.append(swap(piece, "x", NX, k))
         sub = kv_weight.shape[0] // NC
         mine = lax.dynamic_slice_in_dim(kv_weight, c * sub, sub, axis=0)
         column = jnp.stack(swaps(mine, "x", NX))
+        packed = pack(place, activations, cotangent)
+        column, packed = lax.optimization_barrier((column, packed))
         weight = lax.all_gather(column, "z", axis=0)
+        pieces = [swap(packed[i], "x", NX, PARTNERS[i // 2]) for i in (0, 2, 4, 1, 3, 5)]
 
     with jax.named_scope("gradient"):
-        part = gradient_terms(place, activations, cots, pieces)
-        part, cots, pieces = lax.optimization_barrier((part, cots, pieces))
+        part = gradient_terms(place, activations, cotangent, pieces)
+        part, pieces = lax.optimization_barrier((part, pieces))
         gradient = lax.psum_scatter(part, "z", scatter_dimension=0, tiled=True)
 
     with jax.named_scope("left"):
-        left = left_terms(place, q_start, error, activations, cots, pieces)
+        left = left_terms(place, q_start, error, activations, cotangent, pieces)
         left = tree(list(lax.all_to_all(left, ("y", "c"), 0, 0, tiled=True)))
         left = tree(list(lax.all_to_all(left, "z", 0, 0, tiled=True)))
         left = jnp.broadcast_to(left[None], (NY * NC,) + left.shape)

time: 236 us -> 215 us (0.911)
  waiting for transfers between devices: 97.5 us -> 86.9 us
  starting transfers between devices: 44.9 us -> 37.9 us
  Pallas kernels: 36.6 us -> 40.7 us
  local copies, waits for them, and re-layouts: 7.89 us -> 3.98 us
    ppermute x25 -> x22, waiting for transfers between devices: 97.5 us -> 85.1 us  [swap(): return lax.ppermute(value, axis, [(i, i ^ k) for i in range(size)])]
    ppermute x25 -> x22, starting transfers between devices: 39.1 us -> 32.1 us  [swap(): return lax.ppermute(value, axis, [(i, i ^ k) for i in range(size)])]
    pallas_call x0 -> x1, Pallas kernels: none -> 5.94 us  [pack(): pl.pallas_call(pack_kernel, out_shape=(jax.ShapeDtypeStruct(shape, BF16),...]
    dynamic_slice x1 -> x0, local copies, waits for them, and re-layouts: 3.86 us -> none  [local(): lax.dynamic_slice(activations, (h * (tokens // 2), (x ^ k) * columns), (t...]
  transfers between devices with their start and end apart: 28 -> 25, of which waited for: 17 -> 18; matrix products, arithmetic and copies ran while one was open for 3% -> 1% of each run, Pallas kernels for 13% -> 16%
where the time goes in v4:
time: 215 us; the launch traced here: 214 us
  waiting for transfers between devices  86.9 us (40%)
  Pallas kernels  40.7 us (19%)
  starting transfers between devices  37.9 us (18%)
  blocking collectives  29.7 us (14%)
  between operations  14.2 us (7%)
  local copies, waits for them, and re-layouts  3.98 us (2%)
    ppermute x22, waiting for transfers between devices, swap(): return lax.ppermute(value, axis, [(i, i ^ k) for i in range(size)])  85.1 us
    ppermute x22, starting transfers between devices, swap(): return lax.ppermute(value, axis, [(i, i ^ k) for i in range(size)])  32.1 us
    all_to_all x1, blocking collectives, local(): left = tree(list(lax.all_to_all(left, 'z', 0, 0, tiled=True)))  16.1 us
    all_to_all x1, blocking collectives, local(): left = tree(list(lax.all_to_all(left, ('y', 'c'), 0, 0, tiled=True)))  13.6 us
    pallas_call x1, Pallas kernels, left_terms(): pl.pallas_call(functools.partial(left_kernel, 1 + len(pieces)), out_shape...  11.6 us
    pallas_call x1, Pallas kernels, gradient_terms(): pl.pallas_call(functools.partial(gradient_kernel, 1 + len(pieces)), out_s...  8.47 us
    pallas_call x1, Pallas kernels, project(): pl.pallas_call(project_kernel, out_shape=jax.ShapeDtypeStruct((tokens, NX...  8.25 us
    pallas_call x1, Pallas kernels, pack(): pl.pallas_call(pack_kernel, out_shape=(jax.ShapeDtypeStruct(shape, BF16),...  5.94 us
  transfers between devices with their start and end apart: 25, of which 18 were waited for; matrix products, arithmetic and copies ran while one was open for 1% of the time, Pallas kernels for 16%

profile of v4, /device:TPU:1, one launch (start us, length us, event | category | flops | bytes accessed | tf_op | source)
XLA Modules:
  0.0 214.4 jit_solution(2001010016965089895)
XLA Ops:
  8.1 3.7 %collective-permute-start.1 = (bf16[128,512]{1,0:T(8,128)(2,1)S(1)}, bf16[128,512]{1,0:T(8,128)(2,1)S(1)}, u32[]{:S(2)}, u32[]{:S(2)}) collective-permute-start(bf16[128,512]{1,0:T(8,128)(2,1)S(1)} %constant_dynamic-slice_fusion), channel_id=1, source_target_pairs={{0,16},{8,24},{16,0},{24,8},{1,17},{9,25},{17,1},{25,9},{2,18},{10... | collective-permute-start | bytes 393224 | tf_op jit(solution)/shard_map/exchange/ppermute | solution.py:20
  13.3 5.9 %pack.1 = (bf16[160,2560]{1,0:T(8,128)(2,1)}, bf16[160,2560]{1,0:T(8,128)(2,1)}, bf16[160,2560]{1,0:T(8,128)(2,1)}, bf16[160,2560]{1,0:T(8,128)(2,1)}, bf16[160,...) custom-call(s32[6]{0:T(128)} %stack.42.place, bf16[320,8192]{1,0:T(8,128)(2,1)} %refs_7_.3, bf16[320,512]{1,0:T(8,128)(2,1)} %refs_0_.3), custom_call_target="tpu_custom_call" | custom-call | bytes 10485760 | tf_op jit(solution)/shard_map/exchange/pack/pallas_call | solution.py:64
  26.3 13.2 %collective-permute-done.4.refs_1_.refs_8_ = bf16[160,2560]{1,0:T(8,128)(2,1)S(1)} collective-permute-done((bf16[160,2560]{1,0:T(8,128)(2,1)}, bf16[160,2560]{1,0:T(8,128)(2,1)S(1)}, u32[]{:S(2)}, u32[]{:S(2)}) %collective-permute-start.4) | collective-permute-done | bytes 819232 | tf_op jit(solution)/shard_map/exchange/ppermute | solution.py:20
  39.5 2.9 %collective-permute-start.9 = (bf16[160,2560]{1,0:T(8,128)(2,1)}, bf16[160,2560]{1,0:T(8,128)(2,1)}, u32[]{:S(2)}, u32[]{:S(2)}) collective-permute-start(bf16[160,2560]{1,0:T(8,128)(2,1)} %get-tuple-element.42), channel_id=1, source_target_pairs={{0,24},{8,16},{16,8},{24,0},{1,25},{9,17},{17,9},{25,1},{2,26},{10... | collective-permute-start | bytes 2457608 | tf_op jit(solution)/shard_map/exchange/ppermute | solution.py:20
  42.4 15.3 %collective-permute-done.5.refs_2_.refs_9_ = bf16[160,2560]{1,0:T(8,128)(2,1)S(1)} collective-permute-done((bf16[160,2560]{1,0:T(8,128)(2,1)}, bf16[160,2560]{1,0:T(8,128)(2,1)S(1)}, u32[]{:S(2)}, u32[]{:S(2)}) %collective-permute-start.5) | collective-permute-done | bytes 819232 | tf_op jit(solution)/shard_map/exchange/ppermute | solution.py:20
  57.7 5.4 %collective-permute-done.6.refs_3_.refs_10_ = bf16[160,2560]{1,0:T(8,128)(2,1)S(1)} collective-permute-done((bf16[160,2560]{1,0:T(8,128)(2,1)}, bf16[160,2560]{1,0:T(8,128)(2,1)S(1)}, u32[]{:S(2)}, u32[]{:S(2)}) %collective-permute-start.6) | collective-permute-done | bytes 819232 | tf_op jit(solution)/shard_map/exchange/ppermute | solution.py:20
  63.2 11.5 %collective-permute-done.7.refs_4_.refs_11_ = bf16[160,2560]{1,0:T(8,128)(2,1)S(1)} collective-permute-done((bf16[160,2560]{1,0:T(8,128)(2,1)}, bf16[160,2560]{1,0:T(8,128)(2,1)S(1)}, u32[]{:S(2)}, u32[]{:S(2)}) %collective-permute-start.7) | collective-permute-done | bytes 819232 | tf_op jit(solution)/shard_map/exchange/ppermute | solution.py:20
  74.7 18.2 %collective-permute-done.8.refs_5_.refs_12_ = bf16[160,2560]{1,0:T(8,128)(2,1)} collective-permute-done((bf16[160,2560]{1,0:T(8,128)(2,1)}, bf16[160,2560]{1,0:T(8,128)(2,1)}, u32[]{:S(2)}, u32[]{:S(2)}) %collective-permute-start.8) | collective-permute-done | bytes 819232 | tf_op jit(solution)/shard_map/exchange/ppermute | solution.py:20
  92.9 2.4 %collective-permute-done.9.refs_6_.refs_13_ = bf16[160,2560]{1,0:T(8,128)(2,1)} collective-permute-done((bf16[160,2560]{1,0:T(8,128)(2,1)}, bf16[160,2560]{1,0:T(8,128)(2,1)}, u32[]{:S(2)}, u32[]{:S(2)}) %collective-permute-start.9) | collective-permute-done | bytes 819232 | tf_op jit(solution)/shard_map/exchange/ppermute | solution.py:20
  95.3 8.5 %gradient_terms.1 = f32[8,512,256]{2,1,0:T(8,128)} custom-call(s32[6]{0:T(128)} %stack.42.place, bf16[320,512]{1,0:T(8,128)(2,1)} %refs_0_.3, bf16[160,2560]{1,0:T(8,128)(2,1)} %copy-done.4, bf16[160,2560]{1,0:T(8,128)(2,1)} %copy-done.5, bf16[160,2560]{1,0:T(8,128)(2,1)} %copy-done.6, bf16[160,2560]{1,0:T(8,128)(2,1)} %copy-done.7, ...), custom_call_target="tpu_custom_call" | custom-call | flops 2684354560 | bytes 9437184 | tf_op jit(solution)/shard_map/gradient/gradient_terms/pallas_call | solution.py:145
  104.4 11.6 %left_terms.1 = f32[8,8,8,256]{3,2,1,0:T(8,128)} custom-call(s32[6]{0:T(128)} %stack.42.place, f32[64,512]{1,0:T(8,128)} %q.1, f32[256,512]{1,0:T(8,128)} %bitcast.19, bf16[320,512]{1,0:T(8,128)(2,1)} %refs_0_.3, bf16[160,2560]{1,0:T(8,128)(2,1)} %copy-done.4, bf16[160,2560]{1,0:T(8,128)(2,1)} %copy-done.5, bf16[160,2560]{1,0:T(8,128)(2,1)} %copy-done.6, ...), custom_call_target="tpu_custom_call" | custom-call | flops 1006632960 | bytes 5242880 | tf_op jit(solution)/shard_map/left/left_terms/pallas_call | solution.py:172
  116.1 13.6 %all_to_all.15 = f32[8,8,8,256]{3,2,1,0:T(8,128)S(1)} all-to-all(f32[8,8,8,256]{3,2,1,0:T(8,128)} %left_terms.1), channel_id=1, replica_groups=mesh['y'=4,'c'=2,'x'=4,'z'=8] {'y','c'}, dimensions={0} | all-to-all | bytes 1048576 | tf_op jit(solution)/shard_map/left/all_to_all | solution.py:345
  129.7 16.1 %all_to_all.16 = f32[8,8,256]{2,1,0:T(8,128)S(1)} all-to-all(f32[8,8,256]{2,1,0:T(8,128)S(1)} %fusion.2), channel_id=1, replica_groups=mesh['y'=4,'c'=2,'x'=4,'z'=8] {'z'}, dimensions={0} | all-to-all | bytes 131072 | tf_op jit(solution)/shard_map/left/all_to_all | solution.py:346
  146.5 5.7 %all-to-all-start.2 = ((f32[8,8,256]{2,1,0:T(8,128)}), f32[8,8,256]{2,1,0:T(8,128)S(1)}, u32[]{:S(2)}, u32[]{:S(2)}) async-start(f32[8,8,256]{2,1,0:T(8,128)} %broadcast_in_dim.12), calls=%async_computation.3 | async-start | bytes 131072 | tf_op jit(solution)/shard_map/left/all_to_all | solution.py:348
  152.2 8.2 %project.1 = bf16[320,8192]{1,0:T(8,128)(2,1)} custom-call(s32[6]{0:T(128)} %stack.42.place, bf16[320,512]{1,0:T(8,128)(2,1)} %refs_0_.3, bf16[8,4,128,512]{3,2,1,0:T(8,128)(2,1)} %bitcast.24, bf16[8,4,128,512]{3,2,1,0:T(8,128)(2,1)} %collective-permute-done.3.other), custom_call_target="tpu_custom_call" | custom-call | flops 2684354560 | bytes 13631488 | tf_op jit(solution)/shard_map/weight/project/pallas_call | solution.py:227
  166.7 2.5 %collective-permute-start.13 = (f32[32,576]{1,0:T(8,128)S(1)}, f32[32,576]{1,0:T(8,128)S(1)}, u32[]{:S(2)}, u32[]{:S(2)}) collective-permute-start(f32[32,576]{1,0:T(8,128)S(1)} %add.112), channel_id=1, source_target_pairs={{0,192},{64,128},{128,64},{192,0},{1,193},{65,129},{129,65},{193,1... | collective-permute-start | bytes 221192 | tf_op jit(solution)/shard_map/sums/ppermute | solution.py:20
  171.7 2.3 %collective-permute-done.12 = f32[32,576]{1,0:T(8,128)S(1)} collective-permute-done((f32[32,576]{1,0:T(8,128)S(1)}, f32[32,576]{1,0:T(8,128)S(1)}, u32[]{:S(2)}, u32[]{:S(2)}) %collective-permute-start.12) | collective-permute-done | bytes 73760 | tf_op jit(solution)/shard_map/sums/ppermute | solution.py:20
  174.2 2.5 %collective-permute-start.16 = (f32[32,576]{1,0:T(8,128)S(1)}, f32[32,576]{1,0:T(8,128)S(1)}, u32[]{:S(2)}, u32[]{:S(2)}) collective-permute-start(f32[32,576]{1,0:T(8,128)S(1)} %add_add_fusion.2), channel_id=1, source_target_pairs={{0,24},{8,16},{16,8},{24,0},{1,25},{9,17},{17,9},{25,1},{2,26},{10... | collective-permute-start | bytes 221192 | tf_op jit(solution)/shard_map/sums/ppermute | solution.py:20
  179.0 2.6 %collective-permute-done.15 = f32[32,576]{1,0:T(8,128)S(1)} collective-permute-done((f32[32,576]{1,0:T(8,128)S(1)}, f32[32,576]{1,0:T(8,128)S(1)}, u32[]{:S(2)}, u32[]{:S(2)}) %collective-permute-start.15) | collective-permute-done | bytes 73760 | tf_op jit(solution)/shard_map/sums/ppermute | solution.py:20
  181.7 3.3 %collective-permute-done.17 = f32[32,576]{1,0:T(8,128)S(1)} collective-permute-done((f32[32,576]{1,0:T(8,128)S(1)}, f32[32,576]{1,0:T(8,128)S(1)}, u32[]{:S(2)}, u32[]{:S(2)}) %collective-permute-start.17) | collective-permute-done | bytes 73760 | tf_op jit(solution)/shard_map/sums/ppermute | solution.py:20
  187.0 2.9 %collective-permute-start.19 = (f32[32,576]{1,0:T(8,128)S(1)}, f32[32,576]{1,0:T(8,128)S(1)}, u32[]{:S(2)}, u32[]{:S(2)}) collective-permute-start(f32[32,576]{1,0:T(8,128)S(1)} %add.119), channel_id=1, source_target_pairs={{0,4},{1,5},{2,6},{3,7},{4,0},{5,1},{6,2},{7,3},{8,12},{9,13},{10,... | collective-permute-start | bytes 221192 | tf_op jit(solution)/shard_map/sums/ppermute | solution.py:20
  190.8 4.0 %collective-permute-done.19 = f32[32,576]{1,0:T(8,128)S(1)} collective-permute-done((f32[32,576]{1,0:T(8,128)S(1)}, f32[32,576]{1,0:T(8,128)S(1)}, u32[]{:S(2)}, u32[]{:S(2)}) %collective-permute-start.19) | collective-permute-done | bytes 73760 | tf_op jit(solution)/shard_map/sums/ppermute | solution.py:20
  196.2 5.1 %collective-permute-start.21 = (f32[32,576]{1,0:T(8,128)S(1)}, f32[32,576]{1,0:T(8,128)S(1)}, u32[]{:S(2)}, u32[]{:S(2)}) collective-permute-start(f32[32,576]{1,0:T(8,128)S(1)} %add_add_fusion.mine), channel_id=1, source_target_pairs={{0,32},{32,0},{1,33},{33,1},{2,34},{34,2},{3,35},{35,3},{4,36},{36... | collective-permute-start | bytes 221192 | tf_op jit(solution)/shard_map/sums/ppermute | solution.py:20
  202.2 5.3 %finish.1 = (f32[256,512]{1,0:T(8,128)}, f32[256,512]{1,0:T(8,128)}, f32[64,512]{1,0:T(8,128)}) custom-call(s32[6]{0:T(128)S(1)} %copy-done.3, f32[32,576]{1,0:T(8,128)S(1)} %add_add_fusion.mine, f32[32,576]{1,0:T(8,128)S(1)} %collective-permute-done.21.other, f32[64,256]{1,0:T(8,128)S(1)} %bitcast.22, f32[256,512]{1,0:T(8,128)S(1)} %get-tuple-element.52.merged), custom_call_target="tpu_custom_call" | custom-call | tf_op jit(solution)/shard_map/finish/finish/pallas_call | solution.py:311
  (65 shorter events, 27.3 us)
Async XLA Ops:
  7.2 96.6 %all-gather.3.cloned.1.call-start = ((), (), s32[]{:S(2)}) async-start(), calls=%async_computation.5 | async-start | bytes 4718592 | tf_op jit(solution)/shard_map/exchange/all_gather | solution.py:335
  8.1 11.2 %collective-permute-start.1 = (bf16[128,512]{1,0:T(8,128)(2,1)S(1)}, bf16[128,512]{1,0:T(8,128)(2,1)S(1)}, u32[]{:S(2)}, u32[]{:S(2)}) collective-permute-start(bf16[128,512]{1,0:T(8,128)(2,1)S(1)} %constant_dynamic-slice_fusion), channel_id=1, source_target_pairs={{0,16},{8,24},{16,0},{24,8},{1,17},{9,25},{17,1},{25,9},{2,18},{10... | collective-permute-start | bytes 393224 | tf_op jit(solution)/shard_map/exchange/ppermute | solution.py:20
  11.8 7.5 %collective-permute-start = (bf16[128,512]{1,0:T(8,128)(2,1)S(1)}, bf16[128,512]{1,0:T(8,128)(2,1)S(1)}, u32[]{:S(2)}, u32[]{:S(2)}) collective-permute-start(bf16[128,512]{1,0:T(8,128)(2,1)S(1)} %constant_dynamic-slice_fusion), channel_id=1, source_target_pairs={{0,8},{8,0},{16,24},{24,16},{1,9},{9,1},{17,25},{25,17},{2,10},{10... | collective-permute-start | bytes 393224 | tf_op jit(solution)/shard_map/exchange/ppermute | solution.py:20
  12.1 7.5 %collective-permute-start.2 = (bf16[128,512]{1,0:T(8,128)(2,1)S(1)}, bf16[128,512]{1,0:T(8,128)(2,1)S(1)}, u32[]{:S(2)}, u32[]{:S(2)}) collective-permute-start(bf16[128,512]{1,0:T(8,128)(2,1)S(1)} %constant_dynamic-slice_fusion), channel_id=1, source_target_pairs={{0,24},{8,16},{16,8},{24,0},{1,25},{9,17},{17,9},{25,1},{2,26},{10... | collective-permute-start | bytes 393224 | tf_op jit(solution)/shard_map/exchange/ppermute | solution.py:20
  20.5 142.4 %reduce-scatter.2.cloned.1.call-start = ((), (), s32[]{:S(2)}) async-start(), calls=%async_computation.4 | async-start | bytes 4718592 | tf_op jit(solution)/shard_map/gradient/reduce_scatter | solution.py:341
  20.5 19.0 %collective-permute-start.4 = (bf16[160,2560]{1,0:T(8,128)(2,1)}, bf16[160,2560]{1,0:T(8,128)(2,1)S(1)}, u32[]{:S(2)}, u32[]{:S(2)}) collective-permute-start(bf16[160,2560]{1,0:T(8,128)(2,1)} %get-tuple-element.37), channel_id=1, source_target_pairs={{0,16},{8,24},{16,0},{24,8},{1,17},{9,25},{17,1},{25,9},{2,18},{10... | collective-permute-start | bytes 2457608 | tf_op jit(solution)/shard_map/exchange/ppermute | solution.py:20
  22.7 35.0 %collective-permute-start.5 = (bf16[160,2560]{1,0:T(8,128)(2,1)}, bf16[160,2560]{1,0:T(8,128)(2,1)S(1)}, u32[]{:S(2)}, u32[]{:S(2)}) collective-permute-start(bf16[160,2560]{1,0:T(8,128)(2,1)} %get-tuple-element.38), channel_id=1, source_target_pairs={{0,8},{8,0},{16,24},{24,16},{1,9},{9,1},{17,25},{25,17},{2,10},{10... | collective-permute-start | bytes 2457608 | tf_op jit(solution)/shard_map/exchange/ppermute | solution.py:20
  23.0 40.1 %collective-permute-start.6 = (bf16[160,2560]{1,0:T(8,128)(2,1)}, bf16[160,2560]{1,0:T(8,128)(2,1)S(1)}, u32[]{:S(2)}, u32[]{:S(2)}) collective-permute-start(bf16[160,2560]{1,0:T(8,128)(2,1)} %get-tuple-element.39), channel_id=1, source_target_pairs={{0,24},{8,16},{16,8},{24,0},{1,25},{9,17},{17,9},{25,1},{2,26},{10... | collective-permute-start | bytes 2457608 | tf_op jit(solution)/shard_map/exchange/ppermute | solution.py:20
  23.9 50.8 %collective-permute-start.7 = (bf16[160,2560]{1,0:T(8,128)(2,1)}, bf16[160,2560]{1,0:T(8,128)(2,1)S(1)}, u32[]{:S(2)}, u32[]{:S(2)}) collective-permute-start(bf16[160,2560]{1,0:T(8,128)(2,1)} %get-tuple-element.40), channel_id=1, source_target_pairs={{0,16},{8,24},{16,0},{24,8},{1,17},{9,25},{17,1},{25,9},{2,18},{10... | collective-permute-start | bytes 2457608 | tf_op jit(solution)/shard_map/exchange/ppermute | solution.py:20
  26.0 66.9 %collective-permute-start.8 = (bf16[160,2560]{1,0:T(8,128)(2,1)}, bf16[160,2560]{1,0:T(8,128)(2,1)}, u32[]{:S(2)}, u32[]{:S(2)}) collective-permute-start(bf16[160,2560]{1,0:T(8,128)(2,1)} %get-tuple-element.41), channel_id=1, source_target_pairs={{0,8},{8,0},{16,24},{24,16},{1,9},{9,1},{17,25},{25,17},{2,10},{10... | collective-permute-start | bytes 2457608 | tf_op jit(solution)/shard_map/exchange/ppermute | solution.py:20
  39.5 55.8 %collective-permute-start.9 = (bf16[160,2560]{1,0:T(8,128)(2,1)}, bf16[160,2560]{1,0:T(8,128)(2,1)}, u32[]{:S(2)}, u32[]{:S(2)}) collective-permute-start(bf16[160,2560]{1,0:T(8,128)(2,1)} %get-tuple-element.42), channel_id=1, source_target_pairs={{0,24},{8,16},{16,8},{24,0},{1,25},{9,17},{17,9},{25,1},{2,26},{10... | collective-permute-start | bytes 2457608 | tf_op jit(solution)/shard_map/exchange/ppermute | solution.py:20
  103.8 48.4 %collective-permute-start.3 = (bf16[8,4,128,512]{3,2,1,0:T(8,128)(2,1)}, bf16[8,4,128,512]{3,2,1,0:T(8,128)(2,1)}, u32[]{:S(2)}, u32[]{:S(2)}) collective-permute-start(bf16[8,4,128,512]{3,2,1,0:T(8,128)(2,1)} %bitcast.23), channel_id=1, source_target_pairs={{0,32},{32,0},{1,33},{33,1},{2,34},{34,2},{3,35},{35,3},{4,36},{36... | collective-permute-start | bytes 12582920 | tf_op jit(solution)/shard_map/weight/ppermute | solution.py:20
  146.5 14.7 %all-to-all-start.2 = ((f32[8,8,256]{2,1,0:T(8,128)}), f32[8,8,256]{2,1,0:T(8,128)S(1)}, u32[]{:S(2)}, u32[]{:S(2)}) async-start(f32[8,8,256]{2,1,0:T(8,128)} %broadcast_in_dim.12), calls=%async_computation.3 | async-start | bytes 131072 | tf_op jit(solution)/shard_map/left/all_to_all | solution.py:348
  166.7 5.0 %collective-permute-start.13 = (f32[32,576]{1,0:T(8,128)S(1)}, f32[32,576]{1,0:T(8,128)S(1)}, u32[]{:S(2)}, u32[]{:S(2)}) collective-permute-start(f32[32,576]{1,0:T(8,128)S(1)} %add.112), channel_id=1, source_target_pairs={{0,192},{64,128},{128,64},{192,0},{1,193},{65,129},{129,65},{193,1... | collective-permute-start | bytes 221192 | tf_op jit(solution)/shard_map/sums/ppermute | solution.py:20
  169.2 4.8 %collective-permute-start.12 = (f32[32,576]{1,0:T(8,128)S(1)}, f32[32,576]{1,0:T(8,128)S(1)}, u32[]{:S(2)}, u32[]{:S(2)}) collective-permute-start(f32[32,576]{1,0:T(8,128)S(1)} %add.112), channel_id=1, source_target_pairs={{0,128},{64,192},{128,0},{192,64},{1,129},{65,193},{129,1},{193,65... | collective-permute-start | bytes 221192 | tf_op jit(solution)/shard_map/sums/ppermute | solution.py:20
  169.7 4.5 %collective-permute-start.11 = (f32[32,576]{1,0:T(8,128)S(1)}, f32[32,576]{1,0:T(8,128)S(1)}, u32[]{:S(2)}, u32[]{:S(2)}) collective-permute-start(f32[32,576]{1,0:T(8,128)S(1)} %add.112), channel_id=1, source_target_pairs={{0,64},{64,0},{128,192},{192,128},{1,65},{65,1},{129,193},{193,129... | collective-permute-start | bytes 221192 | tf_op jit(solution)/shard_map/sums/ppermute | solution.py:20
  174.2 4.8 %collective-permute-start.16 = (f32[32,576]{1,0:T(8,128)S(1)}, f32[32,576]{1,0:T(8,128)S(1)}, u32[]{:S(2)}, u32[]{:S(2)}) collective-permute-start(f32[32,576]{1,0:T(8,128)S(1)} %add_add_fusion.2), channel_id=1, source_target_pairs={{0,24},{8,16},{16,8},{24,0},{1,25},{9,17},{17,9},{25,1},{2,26},{10... | collective-permute-start | bytes 221192 | tf_op jit(solution)/shard_map/sums/ppermute | solution.py:20
  176.7 4.9 %collective-permute-start.15 = (f32[32,576]{1,0:T(8,128)S(1)}, f32[32,576]{1,0:T(8,128)S(1)}, u32[]{:S(2)}, u32[]{:S(2)}) collective-permute-start(f32[32,576]{1,0:T(8,128)S(1)} %add_add_fusion.2), channel_id=1, source_target_pairs={{0,16},{8,24},{16,0},{24,8},{1,17},{9,25},{17,1},{25,9},{2,18},{10... | collective-permute-start | bytes 221192 | tf_op jit(solution)/shard_map/sums/ppermute | solution.py:20
  177.3 4.3 %collective-permute-start.14 = (f32[32,576]{1,0:T(8,128)S(1)}, f32[32,576]{1,0:T(8,128)S(1)}, u32[]{:S(2)}, u32[]{:S(2)}) collective-permute-start(f32[32,576]{1,0:T(8,128)S(1)} %add_add_fusion.2), channel_id=1, source_target_pairs={{0,8},{8,0},{16,24},{24,16},{1,9},{9,1},{17,25},{25,17},{2,10},{10... | collective-permute-start | bytes 221192 | tf_op jit(solution)/shard_map/sums/ppermute | solution.py:20
  181.6 3.4 %collective-permute-start.17 = (f32[32,576]{1,0:T(8,128)S(1)}, f32[32,576]{1,0:T(8,128)S(1)}, u32[]{:S(2)}, u32[]{:S(2)}) collective-permute-start(f32[32,576]{1,0:T(8,128)S(1)} %add_add_fusion.1), channel_id=1, source_target_pairs={{0,1},{1,0},{2,3},{3,2},{4,5},{5,4},{6,7},{7,6},{8,9},{9,8},{10,11... | collective-permute-start | bytes 221192 | tf_op jit(solution)/shard_map/sums/ppermute | solution.py:20
  185.0 5.8 %collective-permute-start.20 = (f32[32,576]{1,0:T(8,128)S(1)}, f32[32,576]{1,0:T(8,128)S(1)}, u32[]{:S(2)}, u32[]{:S(2)}) collective-permute-start(f32[32,576]{1,0:T(8,128)S(1)} %add.119), channel_id=1, source_target_pairs={{0,6},{1,7},{2,4},{3,5},{4,2},{5,3},{6,0},{7,1},{8,14},{9,15},{10,... | collective-permute-start | bytes 221192 | tf_op jit(solution)/shard_map/sums/ppermute | solution.py:20
  187.0 7.8 %collective-permute-start.19 = (f32[32,576]{1,0:T(8,128)S(1)}, f32[32,576]{1,0:T(8,128)S(1)}, u32[]{:S(2)}, u32[]{:S(2)}) collective-permute-start(f32[32,576]{1,0:T(8,128)S(1)} %add.119), channel_id=1, source_target_pairs={{0,4},{1,5},{2,6},{3,7},{4,0},{5,1},{6,2},{7,3},{8,12},{9,13},{10,... | collective-permute-start | bytes 221192 | tf_op jit(solution)/shard_map/sums/ppermute | solution.py:20
  190.0 6.2 %collective-permute-start.18 = (f32[32,576]{1,0:T(8,128)S(1)}, f32[32,576]{1,0:T(8,128)S(1)}, u32[]{:S(2)}, u32[]{:S(2)}) collective-permute-start(f32[32,576]{1,0:T(8,128)S(1)} %add.119), channel_id=1, source_target_pairs={{0,2},{1,3},{2,0},{3,1},{4,6},{5,7},{6,4},{7,5},{8,10},{9,11},{10,... | collective-permute-start | bytes 221192 | tf_op jit(solution)/shard_map/sums/ppermute | solution.py:20
  196.2 6.0 %collective-permute-start.21 = (f32[32,576]{1,0:T(8,128)S(1)}, f32[32,576]{1,0:T(8,128)S(1)}, u32[]{:S(2)}, u32[]{:S(2)}) collective-permute-start(f32[32,576]{1,0:T(8,128)S(1)} %add_add_fusion.mine), channel_id=1, source_target_pairs={{0,32},{32,0},{1,33},{33,1},{2,34},{34,2},{3,35},{35,3},{4,36},{36... | collective-permute-start | bytes 221192 | tf_op jit(solution)/shard_map/sums/ppermute | solution.py:20
  (9 other events, 171.1 us)
Sparse Core Ops, SparseCore 0:
  20.6 57.9 all-gather.2
  103.9 58.9 reduce-scatter.1

commit v5 on v4

--- a/solution.py
+++ b/solution.py
@@ -47,34 +47,35 @@
 PARTNERS = (2, 1, 3)
 
 
-def pack_kernel(place, act, cot, *outs):
-    rows, columns = outs[0].shape[0], act.shape[1]
-    for j in range(len(PARTNERS)):
-        @pl.when(pl.program_id(0) == j)
-        def _():
-            for h in range(2):
-                outs[2 * j + h][:, :columns] = act[h * rows:(h + 1) * rows, :]
-                outs[2 * j + h][:, columns:] = cot[h * rows:(h + 1) * rows, :]
+def pack_kernel(place, act, cot, *refs):
+    outs, arrived = refs[:-1], refs[-1]
+    rows = outs[0].shape[0]
+    columns = act.shape[1] // NX
+    copies = []
+    for i, out in enumerate(outs):
+        here = pl.ds((i % 2) * rows, rows)
+        start = pl.multiple_of(place[3 + i // 2] * columns, columns)
+        copies.append((act.at[here, pl.ds(start, columns)], out.at[:, pl.ds(0, columns)]))
+        copies.append((cot.at[here, :], out.at[:, pl.ds(columns, cot.shape[1])]))
+    copies = [pltpu.make_async_copy(src, dst, arrived.at[i]) for i, (src, dst) in enumerate(copies)]
+    for copy in copies:
+        copy.start()
+    for copy in copies:
+        copy.wait()
 
 
 def pack(place, activations, cotangent):
     tokens, width = cotangent.shape
-    columns = activations.shape[1] // NX
-    shape = (tokens // 2, columns + width)
+    count = 2 * len(PARTNERS)
+    shape = jax.ShapeDtypeStruct((tokens // 2, activations.shape[1] // NX + width), BF16)
     return pl.pallas_call(
         pack_kernel,
-        out_shape=(jax.ShapeDtypeStruct(shape, BF16),) * (2 * len(PARTNERS)),
-        grid_spec=pltpu.PrefetchScalarGridSpec(
-            num_scalar_prefetch=1,
-            grid=(len(PARTNERS),),
-            in_specs=[
-                pl.BlockSpec((tokens, columns), lambda j, place: (0, place[3 + j])),
-                pl.BlockSpec((tokens, width), lambda j, place: (0, 0)),
-            ],
-            out_specs=[pl.BlockSpec(shape, lambda j, place: (0, 0))] * (2 * len(PARTNERS)),
-        ),
-        cost_estimate=pl.CostEstimate(flops=0, bytes_accessed=8 * tokens * columns * 2, transcendentals=0),
-        compiler_params=pltpu.CompilerParams(vmem_limit_bytes=60 * 1024 * 1024),
+        out_shape=(shape,) * count,
+        in_specs=[pl.BlockSpec(memory_space=pltpu.SMEM)] + [pl.BlockSpec(memory_space=pltpu.HBM)] * 2,
+        out_specs=[pl.BlockSpec(memory_space=pltpu.VMEM)] * count,
+        scratch_shapes=[pltpu.SemaphoreType.DMA((2 * count,))],
+        cost_estimate=pl.CostEstimate(flops=0, bytes_accessed=2 * activations.size, transcendentals=0),
+        compiler_params=pltpu.CompilerParams(vmem_limit_bytes=46 * 1024 * 1024),
         name="pack",
     )(place, activations, cotangent)
 
@@ -159,7 +160,7 @@
             bytes_accessed=(2 * tokens + 4 * width) * columns,
             transcendentals=0,
         ),
-        compiler_params=pltpu.CompilerParams(vmem_limit_bytes=60 * 1024 * 1024),
+        compiler_params=pltpu.CompilerParams(vmem_limit_bytes=52 * 1024 * 1024),
         name="gradient_terms",
     )(place, cotangent, *pieces, activations, *pieces)
 
@@ -188,7 +189,7 @@
             bytes_accessed=2 * tokens * block * NZ,
             transcendentals=0,
         ),
-        compiler_params=pltpu.CompilerParams(vmem_limit_bytes=60 * 1024 * 1024),
+        compiler_params=pltpu.CompilerParams(vmem_limit_bytes=52 * 1024 * 1024),
         name="left_terms",
     )(place, q_start, error, cotangent, *pieces, activations, *pieces)
 
@@ -331,9 +332,8 @@
         mine = lax.dynamic_slice_in_dim(kv_weight, c * sub, sub, axis=0)
         column = jnp.stack(swaps(mine, "x", NX))
         packed = pack(place, activations, cotangent)
-        column, packed = lax.optimization_barrier((column, packed))
         weight = lax.all_gather(column, "z", axis=0)
-        pieces = [swap(packed[i], "x", NX, PARTNERS[i // 2]) for i in (0, 2, 4, 1, 3, 5)]
+        pieces = [swap(packed[i], "x", NX, PARTNERS[i // 2]) for i in (0, 1, 4, 5, 2, 3)]
 
     with jax.named_scope("gradient"):
         part = gradient_terms(place, activations, cotangent, pieces)

time: 215 us -> 222 us (1.033)
  waiting for transfers between devices: 86.9 us -> 97.3 us
  Pallas kernels: 40.7 us -> 35.7 us
  local copies, waits for them, and re-layouts: 3.98 us -> 6.84 us
    ppermute x22, waiting for transfers between devices: 85.1 us -> 96.8 us  [swap(): return lax.ppermute(value, axis, [(i, i ^ k) for i in range(size)])]
    unnamed x16 -> x28, local copies, waits for them, and re-layouts: 1.96 us -> 5.41 us
    pallas_call x1, Pallas kernels: 5.94 us -> 2.75 us  [pack(): pl.pallas_call(pack_kernel, out_shape=(shape,) * count, in_specs=[pl.Bloc...]
  transfers between devices with their start and end apart: 25 -> 25, of which waited for: 18 -> 16; matrix products, arithmetic and copies ran while one was open for 1% -> 1% of each run, Pallas kernels for 16% -> 13%
where the time goes in v5:
time: 222 us; the launch traced here: 221 us
  waiting for transfers between devices  97.3 us (44%)
  starting transfers between devices  35.8 us (16%)
  Pallas kernels  35.7 us (16%)
  blocking collectives  30.3 us (14%)
  between operations  14.2 us (6%)
  local copies, waits for them, and re-layouts  6.84 us (3%)
    ppermute x22, waiting for transfers between devices, swap(): return lax.ppermute(value, axis, [(i, i ^ k) for i in range(size)])  96.8 us
    ppermute x22, starting transfers between devices, swap(): return lax.ppermute(value, axis, [(i, i ^ k) for i in range(size)])  30 us
    all_to_all x1, blocking collectives, local(): left = tree(list(lax.all_to_all(left, 'z', 0, 0, tiled=True)))  16.2 us
    all_to_all x1, blocking collectives, local(): left = tree(list(lax.all_to_all(left, ('y', 'c'), 0, 0, tiled=True)))  14.1 us
    pallas_call x1, Pallas kernels, left_terms(): pl.pallas_call(functools.partial(left_kernel, 1 + len(pieces)), out_shape...  10.5 us
    pallas_call x1, Pallas kernels, project(): pl.pallas_call(project_kernel, out_shape=jax.ShapeDtypeStruct((tokens, NX...  8.26 us
    pallas_call x1, Pallas kernels, gradient_terms(): pl.pallas_call(functools.partial(gradient_kernel, 1 + len(pieces)), out_s...  7.75 us
    all_to_all x1, starting transfers between devices, local(): lax.all_to_all(left, ('y', 'c'), 0, 0, tiled=True)  5.73 us
  transfers between devices with their start and end apart: 25, of which 16 were waited for; matrix products, arithmetic and copies ran while one was open for 1% of the time, Pallas kernels for 13%

profile of v5, /device:TPU:1, one launch (start us, length us, event | category | flops | bytes accessed | tf_op | source)
XLA Modules:
  0.0 221.1 jit_solution(7117711487258798887)
XLA Ops:
  10.3 2.5 %collective-permute-start.1 = (bf16[128,512]{1,0:T(8,128)(2,1)S(1)}, bf16[128,512]{1,0:T(8,128)(2,1)S(1)}, u32[]{:S(2)}, u32[]{:S(2)}) collective-permute-start(bf16[128,512]{1,0:T(8,128)(2,1)S(1)} %constant_dynamic-slice_fusion), channel_id=1, source_target_pairs={{0,16},{8,24},{16,0},{24,8},{1,17},{9,25},{17,1},{25,9},{2,18},{10... | collective-permute-start | bytes 393224 | tf_op jit(solution)/shard_map/exchange/ppermute | solution.py:20
  12.8 5.6 %collective-permute-done.1 = bf16[128,512]{1,0:T(8,128)(2,1)S(1)} collective-permute-done((bf16[128,512]{1,0:T(8,128)(2,1)S(1)}, bf16[128,512]{1,0:T(8,128)(2,1)S(1)}, u32[]{:S(2)}, u32[]{:S(2)}) %collective-permute-start.1) | collective-permute-done | bytes 131104 | tf_op jit(solution)/shard_map/exchange/ppermute | solution.py:20
  18.4 2.5 %collective-permute-done.2 = bf16[128,512]{1,0:T(8,128)(2,1)S(1)} collective-permute-done((bf16[128,512]{1,0:T(8,128)(2,1)S(1)}, bf16[128,512]{1,0:T(8,128)(2,1)S(1)}, u32[]{:S(2)}, u32[]{:S(2)}) %collective-permute-start.2) | collective-permute-done | bytes 131104 | tf_op jit(solution)/shard_map/exchange/ppermute | solution.py:20
  22.9 2.8 %pack.1 = (bf16[160,2560]{1,0:T(8,128)(2,1)S(1)}, bf16[160,2560]{1,0:T(8,128)(2,1)S(1)}, bf16[160,2560]{1,0:T(8,128)(2,1)S(1)}, bf16[160,2560]{1,0:T(8,128)(2,1)...) custom-call(s32[6]{0:T(128)S(1)} %stack.42.place, bf16[320,8192]{1,0:T(8,128)(2,1)} %refs_7_.3, ...), custom_call_target="tpu_custom_call" | custom-call | bytes 5242880 | tf_op jit(solution)/shard_map/exchange/pack/pallas_call | solution.py:71
  25.8 3.0 %collective-permute-start.5 = (bf16[160,2560]{1,0:T(8,128)(2,1)S(1)}, bf16[160,2560]{1,0:T(8,128)(2,1)S(1)}, u32[]{:S(2)}, u32[]{:S(2)}) collective-permute-start(bf16[160,2560]{1,0:T(8,128)(2,1)S(1)} %get-tuple-element.24), channel_id=1, source_target_pairs={{0,16},{8,24},{16,0},{24,8},{1,17},{9,25},{17,1},{25,9},{2,18},{10... | collective-permute-start | bytes 2457608 | tf_op jit(solution)/shard_map/exchange/ppermute | solution.py:20
  28.8 2.7 %collective-permute-start.7 = (bf16[160,2560]{1,0:T(8,128)(2,1)S(1)}, bf16[160,2560]{1,0:T(8,128)(2,1)S(1)}, u32[]{:S(2)}, u32[]{:S(2)}) collective-permute-start(bf16[160,2560]{1,0:T(8,128)(2,1)S(1)} %get-tuple-element.26), channel_id=1, source_target_pairs={{0,24},{8,16},{16,8},{24,0},{1,25},{9,17},{17,9},{25,1},{2,26},{10... | collective-permute-start | bytes 2457608 | tf_op jit(solution)/shard_map/exchange/ppermute | solution.py:20
  31.4 14.4 %collective-permute-done.4.refs_1_.refs_8_ = bf16[160,2560]{1,0:T(8,128)(2,1)S(1)} collective-permute-done((bf16[160,2560]{1,0:T(8,128)(2,1)S(1)}, bf16[160,2560]{1,0:T(8,128)(2,1)S(1)}, u32[]{:S(2)}, u32[]{:S(2)}) %collective-permute-start.4) | collective-permute-done | bytes 819232 | tf_op jit(solution)/shard_map/exchange/ppermute | solution.py:20
  45.9 17.5 %collective-permute-done.5.refs_2_.refs_9_ = bf16[160,2560]{1,0:T(8,128)(2,1)S(1)} collective-permute-done((bf16[160,2560]{1,0:T(8,128)(2,1)S(1)}, bf16[160,2560]{1,0:T(8,128)(2,1)S(1)}, u32[]{:S(2)}, u32[]{:S(2)}) %collective-permute-start.5) | collective-permute-done | bytes 819232 | tf_op jit(solution)/shard_map/exchange/ppermute | solution.py:20
  63.4 19.1 %collective-permute-done.6.refs_3_.refs_10_ = bf16[160,2560]{1,0:T(8,128)(2,1)S(1)} collective-permute-done((bf16[160,2560]{1,0:T(8,128)(2,1)S(1)}, bf16[160,2560]{1,0:T(8,128)(2,1)S(1)}, u32[]{:S(2)}, u32[]{:S(2)}) %collective-permute-start.6) | collective-permute-done | bytes 819232 | tf_op jit(solution)/shard_map/exchange/ppermute | solution.py:20
  82.6 17.6 %collective-permute-done.7.refs_4_.refs_11_ = bf16[160,2560]{1,0:T(8,128)(2,1)S(1)} collective-permute-done((bf16[160,2560]{1,0:T(8,128)(2,1)S(1)}, bf16[160,2560]{1,0:T(8,128)(2,1)S(1)}, u32[]{:S(2)}, u32[]{:S(2)}) %collective-permute-start.7) | collective-permute-done | bytes 819232 | tf_op jit(solution)/shard_map/exchange/ppermute | solution.py:20
  102.2 7.8 %gradient_terms.1 = f32[8,512,256]{2,1,0:T(8,128)} custom-call(s32[6]{0:T(128)S(1)} %stack.42.place, bf16[320,512]{1,0:T(8,128)(2,1)S(1)} %copy-done.4, bf16[160,2560]{1,0:T(8,128)(2,1)S(1)} %collective-permute-done.4.refs_1_.refs_8_, bf16[160,2560]{1,0:T(8,128)(2,1)S(1)} %collective-permute-done.5.refs_2_.refs_9_, bf16[160,2560]{1,0:T(8,128)(2,1)} %copy-done.10, ...), custom_call_target="tpu_custom_call" | custom-call | flops 2684354560 | bytes 9437184 | tf_op jit(solution)/shard_map/gradient/gradient_terms/pallas_call | solution.py:146
  111.0 10.5 %left_terms.1 = f32[8,8,8,256]{3,2,1,0:T(8,128)S(1)} custom-call(s32[6]{0:T(128)S(1)} %stack.42.place, f32[64,512]{1,0:T(8,128)S(1)} %copy-done.7, f32[256,512]{1,0:T(8,128)S(1)} %bitcast.19, bf16[320,512]{1,0:T(8,128)(2,1)S(1)} %copy-done.4, bf16[160,2560]{1,0:T(8,128)(2,1)} %copy-done.1, bf16[160,2560]{1,0:T(8,128)(2,1)} %copy-done.2, ...), custom_call_target="tpu_custom_call" | custom-call | flops 1006632960 | bytes 5242880 | tf_op jit(solution)/shard_map/left/left_terms/pallas_call | solution.py:173
  121.5 14.1 %all_to_all.15 = f32[8,8,8,256]{3,2,1,0:T(8,128)S(1)} all-to-all(f32[8,8,8,256]{3,2,1,0:T(8,128)S(1)} %left_terms.1), channel_id=1, replica_groups=mesh['y'=4,'c'=2,'x'=4,'z'=8] {'y','c'}, dimensions={0} | all-to-all | bytes 1048576 | tf_op jit(solution)/shard_map/left/all_to_all | solution.py:345
  135.7 16.2 %all_to_all.16 = f32[8,8,256]{2,1,0:T(8,128)S(1)} all-to-all(f32[8,8,256]{2,1,0:T(8,128)S(1)} %fusion.2), channel_id=1, replica_groups=mesh['y'=4,'c'=2,'x'=4,'z'=8] {'z'}, dimensions={0} | all-to-all | bytes 131072 | tf_op jit(solution)/shard_map/left/all_to_all | solution.py:346
  152.5 5.7 %all-to-all-start.2 = ((f32[8,8,256]{2,1,0:T(8,128)}), f32[8,8,256]{2,1,0:T(8,128)S(1)}, u32[]{:S(2)}, u32[]{:S(2)}) async-start(f32[8,8,256]{2,1,0:T(8,128)} %broadcast_in_dim.12), calls=%async_computation.3 | async-start | bytes 131072 | tf_op jit(solution)/shard_map/left/all_to_all | solution.py:348
  158.3 8.3 %project.1 = bf16[320,8192]{1,0:T(8,128)(2,1)} custom-call(s32[6]{0:T(128)} %copy-done.8, bf16[320,512]{1,0:T(8,128)(2,1)} %refs_0_.3, bf16[8,4,128,512]{3,2,1,0:T(8,128)(2,1)} %bitcast.24, bf16[8,4,128,512]{3,2,1,0:T(8,128)(2,1)} %collective-permute-done.3.other), custom_call_target="tpu_custom_call" | custom-call | flops 2684354560 | bytes 13631488 | tf_op jit(solution)/shard_map/weight/project/pallas_call | solution.py:228
  172.8 2.5 %collective-permute-start.12 = (f32[32,576]{1,0:T(8,128)S(1)}, f32[32,576]{1,0:T(8,128)S(1)}, u32[]{:S(2)}, u32[]{:S(2)}) collective-permute-start(f32[32,576]{1,0:T(8,128)S(1)} %add.112), channel_id=1, source_target_pairs={{0,128},{64,192},{128,0},{192,64},{1,129},{65,193},{129,1},{193,65... | collective-permute-start | bytes 221192 | tf_op jit(solution)/shard_map/sums/ppermute | solution.py:20
  175.4 3.8 %collective-permute-done.12 = f32[32,576]{1,0:T(8,128)S(1)} collective-permute-done((f32[32,576]{1,0:T(8,128)S(1)}, f32[32,576]{1,0:T(8,128)S(1)}, u32[]{:S(2)}, u32[]{:S(2)}) %collective-permute-start.12) | collective-permute-done | bytes 73760 | tf_op jit(solution)/shard_map/sums/ppermute | solution.py:20
  182.4 2.5 %collective-permute-start.15 = (f32[32,576]{1,0:T(8,128)S(1)}, f32[32,576]{1,0:T(8,128)S(1)}, u32[]{:S(2)}, u32[]{:S(2)}) collective-permute-start(f32[32,576]{1,0:T(8,128)S(1)} %add_add_fusion.2), channel_id=1, source_target_pairs={{0,16},{8,24},{16,0},{24,8},{1,17},{9,25},{17,1},{25,9},{2,18},{10... | collective-permute-start | bytes 221192 | tf_op jit(solution)/shard_map/sums/ppermute | solution.py:20
  185.1 2.7 %collective-permute-done.15 = f32[32,576]{1,0:T(8,128)S(1)} collective-permute-done((f32[32,576]{1,0:T(8,128)S(1)}, f32[32,576]{1,0:T(8,128)S(1)}, u32[]{:S(2)}, u32[]{:S(2)}) %collective-permute-start.15) | collective-permute-done | bytes 73760 | tf_op jit(solution)/shard_map/sums/ppermute | solution.py:20
  190.3 3.3 %collective-permute-done.17 = f32[32,576]{1,0:T(8,128)S(1)} collective-permute-done((f32[32,576]{1,0:T(8,128)S(1)}, f32[32,576]{1,0:T(8,128)S(1)}, u32[]{:S(2)}, u32[]{:S(2)}) %collective-permute-start.17) | collective-permute-done | bytes 73760 | tf_op jit(solution)/shard_map/sums/ppermute | solution.py:20
  199.4 3.5 %collective-permute-done.19 = f32[32,576]{1,0:T(8,128)S(1)} collective-permute-done((f32[32,576]{1,0:T(8,128)S(1)}, f32[32,576]{1,0:T(8,128)S(1)}, u32[]{:S(2)}, u32[]{:S(2)}) %collective-permute-start.19) | collective-permute-done | bytes 73760 | tf_op jit(solution)/shard_map/sums/ppermute | solution.py:20
  203.4 4.6 %collective-permute-start.21 = (f32[32,576]{1,0:T(8,128)S(1)}, f32[32,576]{1,0:T(8,128)S(1)}, u32[]{:S(2)}, u32[]{:S(2)}) collective-permute-start(f32[32,576]{1,0:T(8,128)S(1)} %add_add_fusion.mine), channel_id=1, source_target_pairs={{0,32},{32,0},{1,33},{33,1},{2,34},{34,2},{3,35},{35,3},{4,36},{36... | collective-permute-start | bytes 221192 | tf_op jit(solution)/shard_map/sums/ppermute | solution.py:20
  208.9 5.3 %finish.1 = (f32[256,512]{1,0:T(8,128)}, f32[256,512]{1,0:T(8,128)}, f32[64,512]{1,0:T(8,128)}) custom-call(s32[6]{0:T(128)S(1)} %copy-done.9, f32[32,576]{1,0:T(8,128)S(1)} %add_add_fusion.mine, f32[32,576]{1,0:T(8,128)S(1)} %collective-permute-done.21.other, f32[64,256]{1,0:T(8,128)S(1)} %bitcast.22, f32[256,512]{1,0:T(8,128)S(1)} %get-tuple-element.38.merged), custom_call_target="tpu_custom_call" | custom-call | tf_op jit(solution)/shard_map/finish/finish/pallas_call | solution.py:312
  (77 shorter events, 28.6 us)
Async XLA Ops:
  7.2 102.9 %all-gather.3.cloned.1.call-start = ((), (), s32[]{:S(2)}) async-start(), calls=%async_computation.5 | async-start | bytes 4718592 | tf_op jit(solution)/shard_map/exchange/all_gather | solution.py:335
  8.1 4.6 %collective-permute-start = (bf16[128,512]{1,0:T(8,128)(2,1)S(1)}, bf16[128,512]{1,0:T(8,128)(2,1)S(1)}, u32[]{:S(2)}, u32[]{:S(2)}) collective-permute-start(bf16[128,512]{1,0:T(8,128)(2,1)S(1)} %constant_dynamic-slice_fusion), channel_id=1, source_target_pairs={{0,8},{8,0},{16,24},{24,16},{1,9},{9,1},{17,25},{25,17},{2,10},{10... | collective-permute-start | bytes 393224 | tf_op jit(solution)/shard_map/exchange/ppermute | solution.py:20
  10.3 8.2 %collective-permute-start.1 = (bf16[128,512]{1,0:T(8,128)(2,1)S(1)}, bf16[128,512]{1,0:T(8,128)(2,1)S(1)}, u32[]{:S(2)}, u32[]{:S(2)}) collective-permute-start(bf16[128,512]{1,0:T(8,128)(2,1)S(1)} %constant_dynamic-slice_fusion), channel_id=1, source_target_pairs={{0,16},{8,24},{16,0},{24,8},{1,17},{9,25},{17,1},{25,9},{2,18},{10... | collective-permute-start | bytes 393224 | tf_op jit(solution)/shard_map/exchange/ppermute | solution.py:20
  12.7 8.2 %collective-permute-start.2 = (bf16[128,512]{1,0:T(8,128)(2,1)S(1)}, bf16[128,512]{1,0:T(8,128)(2,1)S(1)}, u32[]{:S(2)}, u32[]{:S(2)}) collective-permute-start(bf16[128,512]{1,0:T(8,128)(2,1)S(1)} %constant_dynamic-slice_fusion), channel_id=1, source_target_pairs={{0,24},{8,16},{16,8},{24,0},{1,25},{9,17},{17,9},{25,1},{2,26},{10... | collective-permute-start | bytes 393224 | tf_op jit(solution)/shard_map/exchange/ppermute | solution.py:20
  21.8 145.9 %reduce-scatter.2.cloned.1.call-start = ((), (), s32[]{:S(2)}) async-start(), calls=%async_computation.4 | async-start | bytes 4718592 | tf_op jit(solution)/shard_map/gradient/reduce_scatter | solution.py:341
  25.7 20.2 %collective-permute-start.4 = (bf16[160,2560]{1,0:T(8,128)(2,1)S(1)}, bf16[160,2560]{1,0:T(8,128)(2,1)S(1)}, u32[]{:S(2)}, u32[]{:S(2)}) collective-permute-start(bf16[160,2560]{1,0:T(8,128)(2,1)S(1)} %get-tuple-element.23), channel_id=1, source_target_pairs={{0,16},{8,24},{16,0},{24,8},{1,17},{9,25},{17,1},{25,9},{2,18},{10... | collective-permute-start | bytes 2457608 | tf_op jit(solution)/shard_map/exchange/ppermute | solution.py:20
  25.8 37.6 %collective-permute-start.5 = (bf16[160,2560]{1,0:T(8,128)(2,1)S(1)}, bf16[160,2560]{1,0:T(8,128)(2,1)S(1)}, u32[]{:S(2)}, u32[]{:S(2)}) collective-permute-start(bf16[160,2560]{1,0:T(8,128)(2,1)S(1)} %get-tuple-element.24), channel_id=1, source_target_pairs={{0,16},{8,24},{16,0},{24,8},{1,17},{9,25},{17,1},{25,9},{2,18},{10... | collective-permute-start | bytes 2457608 | tf_op jit(solution)/shard_map/exchange/ppermute | solution.py:20
  28.8 53.8 %collective-permute-start.6 = (bf16[160,2560]{1,0:T(8,128)(2,1)S(1)}, bf16[160,2560]{1,0:T(8,128)(2,1)S(1)}, u32[]{:S(2)}, u32[]{:S(2)}) collective-permute-start(bf16[160,2560]{1,0:T(8,128)(2,1)S(1)} %get-tuple-element.25), channel_id=1, source_target_pairs={{0,24},{8,16},{16,8},{24,0},{1,25},{9,17},{17,9},{25,1},{2,26},{10... | collective-permute-start | bytes 2457608 | tf_op jit(solution)/shard_map/exchange/ppermute | solution.py:20
  28.8 71.4 %collective-permute-start.7 = (bf16[160,2560]{1,0:T(8,128)(2,1)S(1)}, bf16[160,2560]{1,0:T(8,128)(2,1)S(1)}, u32[]{:S(2)}, u32[]{:S(2)}) collective-permute-start(bf16[160,2560]{1,0:T(8,128)(2,1)S(1)} %get-tuple-element.26), channel_id=1, source_target_pairs={{0,24},{8,16},{16,8},{24,0},{1,25},{9,17},{17,9},{25,1},{2,26},{10... | collective-permute-start | bytes 2457608 | tf_op jit(solution)/shard_map/exchange/ppermute | solution.py:20
  31.4 68.7 %collective-permute-start.8 = (bf16[160,2560]{1,0:T(8,128)(2,1)S(1)}, bf16[160,2560]{1,0:T(8,128)(2,1)S(1)}, u32[]{:S(2)}, u32[]{:S(2)}) collective-permute-start(bf16[160,2560]{1,0:T(8,128)(2,1)S(1)} %get-tuple-element.27), channel_id=1, source_target_pairs={{0,8},{8,0},{16,24},{24,16},{1,9},{9,1},{17,25},{25,17},{2,10},{10... | collective-permute-start | bytes 2457608 | tf_op jit(solution)/shard_map/exchange/ppermute | solution.py:20
  45.9 54.3 %collective-permute-start.9 = (bf16[160,2560]{1,0:T(8,128)(2,1)S(1)}, bf16[160,2560]{1,0:T(8,128)(2,1)S(1)}, u32[]{:S(2)}, u32[]{:S(2)}) collective-permute-start(bf16[160,2560]{1,0:T(8,128)(2,1)S(1)} %get-tuple-element.28), channel_id=1, source_target_pairs={{0,8},{8,0},{16,24},{24,16},{1,9},{9,1},{17,25},{25,17},{2,10},{10... | collective-permute-start | bytes 2457608 | tf_op jit(solution)/shard_map/exchange/ppermute | solution.py:20
  110.1 48.2 %collective-permute-start.3 = (bf16[8,4,128,512]{3,2,1,0:T(8,128)(2,1)}, bf16[8,4,128,512]{3,2,1,0:T(8,128)(2,1)}, u32[]{:S(2)}, u32[]{:S(2)}) collective-permute-start(bf16[8,4,128,512]{3,2,1,0:T(8,128)(2,1)} %bitcast.23), channel_id=1, source_target_pairs={{0,32},{32,0},{1,33},{33,1},{2,34},{34,2},{3,35},{35,3},{4,36},{36... | collective-permute-start | bytes 12582920 | tf_op jit(solution)/shard_map/weight/ppermute | solution.py:20
  152.5 14.7 %all-to-all-start.2 = ((f32[8,8,256]{2,1,0:T(8,128)}), f32[8,8,256]{2,1,0:T(8,128)S(1)}, u32[]{:S(2)}, u32[]{:S(2)}) async-start(f32[8,8,256]{2,1,0:T(8,128)} %broadcast_in_dim.12), calls=%async_computation.3 | async-start | bytes 131072 | tf_op jit(solution)/shard_map/left/all_to_all | solution.py:348
  171.5 3.9 %collective-permute-start.11 = (f32[32,576]{1,0:T(8,128)S(1)}, f32[32,576]{1,0:T(8,128)S(1)}, u32[]{:S(2)}, u32[]{:S(2)}) collective-permute-start(f32[32,576]{1,0:T(8,128)S(1)} %add.112), channel_id=1, source_target_pairs={{0,64},{64,0},{128,192},{192,128},{1,65},{65,1},{129,193},{193,129... | collective-permute-start | bytes 221192 | tf_op jit(solution)/shard_map/sums/ppermute | solution.py:20
  172.8 6.4 %collective-permute-start.12 = (f32[32,576]{1,0:T(8,128)S(1)}, f32[32,576]{1,0:T(8,128)S(1)}, u32[]{:S(2)}, u32[]{:S(2)}) collective-permute-start(f32[32,576]{1,0:T(8,128)S(1)} %add.112), channel_id=1, source_target_pairs={{0,128},{64,192},{128,0},{192,64},{1,129},{65,193},{129,1},{193,65... | collective-permute-start | bytes 221192 | tf_op jit(solution)/shard_map/sums/ppermute | solution.py:20
  175.2 5.9 %collective-permute-start.13 = (f32[32,576]{1,0:T(8,128)S(1)}, f32[32,576]{1,0:T(8,128)S(1)}, u32[]{:S(2)}, u32[]{:S(2)}) collective-permute-start(f32[32,576]{1,0:T(8,128)S(1)} %add.112), channel_id=1, source_target_pairs={{0,192},{64,128},{128,64},{192,0},{1,193},{65,129},{129,65},{193,1... | collective-permute-start | bytes 221192 | tf_op jit(solution)/shard_map/sums/ppermute | solution.py:20
  181.2 3.9 %collective-permute-start.14 = (f32[32,576]{1,0:T(8,128)S(1)}, f32[32,576]{1,0:T(8,128)S(1)}, u32[]{:S(2)}, u32[]{:S(2)}) collective-permute-start(f32[32,576]{1,0:T(8,128)S(1)} %add_add_fusion.2), channel_id=1, source_target_pairs={{0,8},{8,0},{16,24},{24,16},{1,9},{9,1},{17,25},{25,17},{2,10},{10... | collective-permute-start | bytes 221192 | tf_op jit(solution)/shard_map/sums/ppermute | solution.py:20
  182.4 5.4 %collective-permute-start.15 = (f32[32,576]{1,0:T(8,128)S(1)}, f32[32,576]{1,0:T(8,128)S(1)}, u32[]{:S(2)}, u32[]{:S(2)}) collective-permute-start(f32[32,576]{1,0:T(8,128)S(1)} %add_add_fusion.2), channel_id=1, source_target_pairs={{0,16},{8,24},{16,0},{24,8},{1,17},{9,25},{17,1},{25,9},{2,18},{10... | collective-permute-start | bytes 221192 | tf_op jit(solution)/shard_map/sums/ppermute | solution.py:20
  184.9 5.3 %collective-permute-start.16 = (f32[32,576]{1,0:T(8,128)S(1)}, f32[32,576]{1,0:T(8,128)S(1)}, u32[]{:S(2)}, u32[]{:S(2)}) collective-permute-start(f32[32,576]{1,0:T(8,128)S(1)} %add_add_fusion.2), channel_id=1, source_target_pairs={{0,24},{8,16},{16,8},{24,0},{1,25},{9,17},{17,9},{25,1},{2,26},{10... | collective-permute-start | bytes 221192 | tf_op jit(solution)/shard_map/sums/ppermute | solution.py:20
  190.2 3.4 %collective-permute-start.17 = (f32[32,576]{1,0:T(8,128)S(1)}, f32[32,576]{1,0:T(8,128)S(1)}, u32[]{:S(2)}, u32[]{:S(2)}) collective-permute-start(f32[32,576]{1,0:T(8,128)S(1)} %add_add_fusion.1), channel_id=1, source_target_pairs={{0,1},{1,0},{2,3},{3,2},{4,5},{5,4},{6,7},{7,6},{8,9},{9,8},{10,11... | collective-permute-start | bytes 221192 | tf_op jit(solution)/shard_map/sums/ppermute | solution.py:20
  193.6 5.7 %collective-permute-start.18 = (f32[32,576]{1,0:T(8,128)S(1)}, f32[32,576]{1,0:T(8,128)S(1)}, u32[]{:S(2)}, u32[]{:S(2)}) collective-permute-start(f32[32,576]{1,0:T(8,128)S(1)} %add.119), channel_id=1, source_target_pairs={{0,2},{1,3},{2,0},{3,1},{4,6},{5,7},{6,4},{7,5},{8,10},{9,11},{10,... | collective-permute-start | bytes 221192 | tf_op jit(solution)/shard_map/sums/ppermute | solution.py:20
  195.2 7.7 %collective-permute-start.19 = (f32[32,576]{1,0:T(8,128)S(1)}, f32[32,576]{1,0:T(8,128)S(1)}, u32[]{:S(2)}, u32[]{:S(2)}) collective-permute-start(f32[32,576]{1,0:T(8,128)S(1)} %add.119), channel_id=1, source_target_pairs={{0,4},{1,5},{2,6},{3,7},{4,0},{5,1},{6,2},{7,3},{8,12},{9,13},{10,... | collective-permute-start | bytes 221192 | tf_op jit(solution)/shard_map/sums/ppermute | solution.py:20
  197.6 5.7 %collective-permute-start.20 = (f32[32,576]{1,0:T(8,128)S(1)}, f32[32,576]{1,0:T(8,128)S(1)}, u32[]{:S(2)}, u32[]{:S(2)}) collective-permute-start(f32[32,576]{1,0:T(8,128)S(1)} %add.119), channel_id=1, source_target_pairs={{0,6},{1,7},{2,4},{3,5},{4,2},{5,3},{6,0},{7,1},{8,14},{9,15},{10,... | collective-permute-start | bytes 221192 | tf_op jit(solution)/shard_map/sums/ppermute | solution.py:20
  203.4 5.5 %collective-permute-start.21 = (f32[32,576]{1,0:T(8,128)S(1)}, f32[32,576]{1,0:T(8,128)S(1)}, u32[]{:S(2)}, u32[]{:S(2)}) collective-permute-start(f32[32,576]{1,0:T(8,128)S(1)} %add_add_fusion.mine), channel_id=1, source_target_pairs={{0,32},{32,0},{1,33},{33,1},{2,34},{34,2},{3,35},{35,3},{4,36},{36... | collective-permute-start | bytes 221192 | tf_op jit(solution)/shard_map/sums/ppermute | solution.py:20
  (15 other events, 330.1 us)
Sparse Core Ops, SparseCore 0:
  21.9 55.9 all-gather.2
  110.1 57.4 reduce-scatter.1

commit v6 on v5

--- a/solution.py
+++ b/solution.py
@@ -194,14 +194,15 @@
     )(place, q_start, error, cotangent, *pieces, activations, *pieces)
 
 
-def project_kernel(place, cot, own, other, out, rows, arrived):
-    sub = own.shape[2]
+def project_kernel(place, cot, *rest):
+    pieces, out, rows, arrived = rest[:NC * NX], rest[NC * NX], rest[NC * NX + 1], rest[NC * NX + 2]
+    sub = pieces[0].shape[1]
     block = NC * sub
 
     def fetch(k, c):
         start = pl.multiple_of((place[1] ^ c) * sub, sub)
         return pltpu.make_async_copy(
-            (own, other)[c].at[:, k], rows.at[k, :, pl.ds(start, sub), :], arrived.at[NC * k + c]
+            pieces[NC * k + c], rows.at[k, :, pl.ds(start, sub), :], arrived.at[NC * k + c]
         )
 
     @pl.when(pl.program_id(0) == 0)
@@ -221,9 +222,9 @@
                 ).astype(BF16)
 
 
-def project(place, cot, own, other):
+def project(place, cot, pieces):
     tokens, width = cot.shape
-    sub = own.shape[2]
+    sub = pieces[0].shape[1]
     columns = NZ * NC * sub
     return pl.pallas_call(
         project_kernel,
@@ -232,7 +233,7 @@
             num_scalar_prefetch=1,
             grid=(NX,),
             in_specs=[pl.BlockSpec((tokens, width), lambda k, place: (0, 0))]
-            + [pl.BlockSpec(memory_space=pltpu.HBM)] * 2,
+            + [pl.BlockSpec(memory_space=pltpu.HBM)] * (NC * NX),
             out_specs=pl.BlockSpec((tokens, columns), lambda k, place: (0, k ^ place[0])),
             scratch_shapes=[pltpu.VMEM((NX, NZ, NC * sub, width), BF16), pltpu.SemaphoreType.DMA((NC * NX,))],
         ),
@@ -243,7 +244,7 @@
         ),
         compiler_params=pltpu.CompilerParams(vmem_limit_bytes=62_000_000),
         name="project",
-    )(place, cot, own, other)
+    )(place, cot, *pieces)
 
 
 def right_kernel(place, _, gradient, error, p_total, merged_out, keep, give):
@@ -329,26 +330,31 @@
 
     with jax.named_scope("exchange"):
         sub = kv_weight.shape[0] // NC
-        mine = lax.dynamic_slice_in_dim(kv_weight, c * sub, sub, axis=0)
-        column = jnp.stack(swaps(mine, "x", NX))
+        line = lax.all_gather(kv_weight, "z", axis=0)
         packed = pack(place, activations, cotangent)
-        weight = lax.all_gather(column, "z", axis=0)
         pieces = [swap(packed[i], "x", NX, PARTNERS[i // 2]) for i in (0, 1, 4, 5, 2, 3)]
 
     with jax.named_scope("gradient"):
         part = gradient_terms(place, activations, cotangent, pieces)
-        part, pieces = lax.optimization_barrier((part, pieces))
+        part, pieces, line = lax.optimization_barrier((part, pieces, line))
         gradient = lax.psum_scatter(part, "z", scatter_dimension=0, tiled=True)
+
+    with jax.named_scope("weight"):
+        halves = swaps(lax.dynamic_slice_in_dim(line, c * sub, sub, axis=1), "x", NX)
 
     with jax.named_scope("left"):
         left = left_terms(place, q_start, error, activations, cotangent, pieces)
         left = tree(list(lax.all_to_all(left, ("y", "c"), 0, 0, tiled=True)))
         left = tree(list(lax.all_to_all(left, "z", 0, 0, tiled=True)))
+        left, halves = lax.optimization_barrier((left, halves))
         left = jnp.broadcast_to(left[None], (NY * NC,) + left.shape)
         p_total = lax.all_to_all(left, ("y", "c"), 0, 0, tiled=True).reshape(q_start.shape[0], -1)
 
     with jax.named_scope("weight"):
-        input_grad = project(place, cotangent, weight, swap(weight, "c", NC, 1))
+        weights = []
+        for half in halves:
+            weights += [half, swap(half, "c", NC, 1)]
+        input_grad = project(place, cotangent, weights)
 
     with jax.named_scope("sums"):
         merged, keep, give = right_terms(place, input_grad[:16, :128], gradient, error, p_total)

time: 222 us -> 221 us (level)
  waiting for transfers between devices: 97.3 us -> 88.4 us
  starting transfers between devices: 35.8 us -> 43 us
    ppermute x22 -> x25, waiting for transfers between devices: 96.8 us -> 87.7 us  [swap(): return lax.ppermute(value, axis, [(i, i ^ k) for i in range(size)])]
    ppermute x22 -> x25, starting transfers between devices: 30 us -> 37.9 us  [swap(): return lax.ppermute(value, axis, [(i, i ^ k) for i in range(size)])]
    unnamed x28 -> x30, local copies, waits for them, and re-layouts: 5.41 us -> 4.19 us
  transfers between devices with their start and end apart: 25 -> 28, of which waited for: 16 -> 16; matrix products, arithmetic and copies ran while one was open for 1% -> 1% of each run, Pallas kernels for 13% -> 13%
where the time goes in v6:
time: 221 us; the launch traced here: 220 us
  waiting for transfers between devices  88.4 us (40%)
  starting transfers between devices  43 us (19%)
  Pallas kernels  35.5 us (16%)
  blocking collectives  31.8 us (14%)
  between operations  14.2 us (6%)
  local copies, waits for them, and re-layouts  6.95 us (3%)
    ppermute x25, waiting for transfers between devices, swap(): return lax.ppermute(value, axis, [(i, i ^ k) for i in range(size)])  87.7 us
    ppermute x25, starting transfers between devices, swap(): return lax.ppermute(value, axis, [(i, i ^ k) for i in range(size)])  37.9 us
    all_to_all x1, blocking collectives, local(): left = tree(list(lax.all_to_all(left, 'z', 0, 0, tiled=True)))  16.3 us
    all_to_all x1, blocking collectives, local(): left = tree(list(lax.all_to_all(left, ('y', 'c'), 0, 0, tiled=True)))  15.4 us
    pallas_call x1, Pallas kernels, left_terms(): pl.pallas_call(functools.partial(left_kernel, 1 + len(pieces)), out_shape...  10.6 us
    pallas_call x1, Pallas kernels, project(): pl.pallas_call(project_kernel, out_shape=jax.ShapeDtypeStruct((tokens, NX...  8.09 us
    pallas_call x1, Pallas kernels, gradient_terms(): pl.pallas_call(functools.partial(gradient_kernel, 1 + len(pieces)), out_s...  7.67 us
    pallas_call x1, Pallas kernels, finish(): pl.pallas_call(finish_kernel, out_shape=(jax.ShapeDtypeStruct(merged.shap...  5.29 us
  transfers between devices with their start and end apart: 28, of which 16 were waited for; matrix products, arithmetic and copies ran while one was open for 1% of the time, Pallas kernels for 13%

profile of v6, /device:TPU:1, one launch (start us, length us, event | category | flops | bytes accessed | tf_op | source)
XLA Modules:
  0.0 220.1 jit_solution(7111812920656943233)
XLA Ops:
  9.0 2.8 %pack.1 = (bf16[160,2560]{1,0:T(8,128)(2,1)S(1)}, bf16[160,2560]{1,0:T(8,128)(2,1)S(1)}, bf16[160,2560]{1,0:T(8,128)(2,1)S(1)}, bf16[160,2560]{1,0:T(8,128)(2,1)...) custom-call(s32[6]{0:T(128)S(1)} %stack.27.place, bf16[320,8192]{1,0:T(8,128)(2,1)} %refs_7_.3, ...), custom_call_target="tpu_custom_call" | custom-call | bytes 5242880 | tf_op jit(solution)/shard_map/exchange/pack/pallas_call | solution.py:71
  11.8 3.7 %collective-permute-start = (bf16[160,2560]{1,0:T(8,128)(2,1)S(1)}, bf16[160,2560]{1,0:T(8,128)(2,1)S(1)}, u32[]{:S(2)}, u32[]{:S(2)}) collective-permute-start(bf16[160,2560]{1,0:T(8,128)(2,1)S(1)} %get-tuple-element.29), channel_id=1, source_target_pairs={{0,16},{8,24},{16,0},{24,8},{1,17},{9,25},{17,1},{25,9},{2,18},{10... | collective-permute-start | bytes 2457608 | tf_op jit(solution)/shard_map/exchange/ppermute | solution.py:20
  15.5 2.6 %collective-permute-start.2 = (bf16[160,2560]{1,0:T(8,128)(2,1)S(1)}, bf16[160,2560]{1,0:T(8,128)(2,1)S(1)}, u32[]{:S(2)}, u32[]{:S(2)}) collective-permute-start(bf16[160,2560]{1,0:T(8,128)(2,1)S(1)} %get-tuple-element.31), channel_id=1, source_target_pairs={{0,24},{8,16},{16,8},{24,0},{1,25},{9,17},{17,9},{25,1},{2,26},{10... | collective-permute-start | bytes 2457608 | tf_op jit(solution)/shard_map/exchange/ppermute | solution.py:20
  18.3 14.0 %collective-permute-done.refs_1_.refs_8_ = bf16[160,2560]{1,0:T(8,128)(2,1)S(1)} collective-permute-done((bf16[160,2560]{1,0:T(8,128)(2,1)S(1)}, bf16[160,2560]{1,0:T(8,128)(2,1)S(1)}, u32[]{:S(2)}, u32[]{:S(2)}) %collective-permute-start) | collective-permute-done | bytes 819232 | tf_op jit(solution)/shard_map/exchange/ppermute | solution.py:20
  32.4 2.3 %collective-permute-start.5 = (bf16[160,2560]{1,0:T(8,128)(2,1)S(1)}, bf16[160,2560]{1,0:T(8,128)(2,1)S(1)}, u32[]{:S(2)}, u32[]{:S(2)}) collective-permute-start(bf16[160,2560]{1,0:T(8,128)(2,1)S(1)} %get-tuple-element.34), channel_id=1, source_target_pairs={{0,8},{8,0},{16,24},{24,16},{1,9},{9,1},{17,25},{25,17},{2,10},{10... | collective-permute-start | bytes 2457608 | tf_op jit(solution)/shard_map/exchange/ppermute | solution.py:20
  34.7 15.3 %collective-permute-done.1.refs_2_.refs_9_ = bf16[160,2560]{1,0:T(8,128)(2,1)S(1)} collective-permute-done((bf16[160,2560]{1,0:T(8,128)(2,1)S(1)}, bf16[160,2560]{1,0:T(8,128)(2,1)S(1)}, u32[]{:S(2)}, u32[]{:S(2)}) %collective-permute-start.1) | collective-permute-done | bytes 819232 | tf_op jit(solution)/shard_map/exchange/ppermute | solution.py:20
  49.9 19.3 %collective-permute-done.2.refs_3_.refs_10_ = bf16[160,2560]{1,0:T(8,128)(2,1)S(1)} collective-permute-done((bf16[160,2560]{1,0:T(8,128)(2,1)S(1)}, bf16[160,2560]{1,0:T(8,128)(2,1)S(1)}, u32[]{:S(2)}, u32[]{:S(2)}) %collective-permute-start.2) | collective-permute-done | bytes 819232 | tf_op jit(solution)/shard_map/exchange/ppermute | solution.py:20
  69.3 17.6 %collective-permute-done.3.refs_4_.refs_11_ = bf16[160,2560]{1,0:T(8,128)(2,1)S(1)} collective-permute-done((bf16[160,2560]{1,0:T(8,128)(2,1)S(1)}, bf16[160,2560]{1,0:T(8,128)(2,1)S(1)}, u32[]{:S(2)}, u32[]{:S(2)}) %collective-permute-start.3) | collective-permute-done | bytes 819232 | tf_op jit(solution)/shard_map/exchange/ppermute | solution.py:20
  89.0 7.7 %gradient_terms.1 = f32[8,512,256]{2,1,0:T(8,128)} custom-call(s32[6]{0:T(128)S(1)} %stack.27.place, bf16[320,512]{1,0:T(8,128)(2,1)S(1)} %copy-done.3, bf16[160,2560]{1,0:T(8,128)(2,1)S(1)} %collective-permute-done.refs_1_.refs_8_, bf16[160,2560]{1,0:T(8,128)(2,1)S(1)} %collective-permute-done.1.refs_2_.refs_9_, bf16[160,2560]{1,0:T(8,128)(2,1)} %copy-done.9, ...), custom_call_target="tpu_custom_call" | custom-call | flops 2684354560 | bytes 9437184 | tf_op jit(solution)/shard_map/gradient/gradient_terms/pallas_call | solution.py:146
  98.1 2.8 %collective-permute-start.8 = (bf16[8,128,512]{2,1,0:T(8,128)(2,1)S(1)}, bf16[8,128,512]{2,1,0:T(8,128)(2,1)S(1)}, u32[]{:S(2)}, u32[]{:S(2)}) collective-permute-start(bf16[8,128,512]{2,1,0:T(8,128)(2,1)S(1)} %constant_dynamic-slice_fusion.rest_0_), channel_id=1, source_target_pairs={{0,24},{8,16},{16,8},{24,0},{1,25},{9,17},{17,9},{25,1},{2,26},{10... | collective-permute-start | bytes 3145736 | tf_op jit(solution)/shard_map/weight/ppermute | solution.py:20
  101.6 10.6 %left_terms.1 = f32[8,8,8,256]{3,2,1,0:T(8,128)S(1)} custom-call(s32[6]{0:T(128)S(1)} %stack.27.place, f32[64,512]{1,0:T(8,128)S(1)} %copy-done.6, f32[256,512]{1,0:T(8,128)S(1)} %bitcast.14, bf16[320,512]{1,0:T(8,128)(2,1)S(1)} %copy-done.3, bf16[160,2560]{1,0:T(8,128)(2,1)} %copy-done, bf16[160,2560]{1,0:T(8,128)(2,1)} %copy-done.1, ...), custom_call_target="tpu_custom_call" | custom-call | flops 1006632960 | bytes 5242880 | tf_op jit(solution)/shard_map/left/left_terms/pallas_call | solution.py:173
  112.2 15.4 %all_to_all.15 = f32[8,8,8,256]{3,2,1,0:T(8,128)S(1)} all-to-all(f32[8,8,8,256]{3,2,1,0:T(8,128)S(1)} %left_terms.1), channel_id=1, replica_groups=mesh['y'=4,'c'=2,'x'=4,'z'=8] {'y','c'}, dimensions={0} | all-to-all | bytes 1048576 | tf_op jit(solution)/shard_map/left/all_to_all | solution.py:347
  127.6 16.3 %all_to_all.16 = f32[8,8,256]{2,1,0:T(8,128)S(1)} all-to-all(f32[8,8,256]{2,1,0:T(8,128)S(1)} %fusion.2), channel_id=1, replica_groups=mesh['y'=4,'c'=2,'x'=4,'z'=8] {'z'}, dimensions={0} | all-to-all | bytes 131072 | tf_op jit(solution)/shard_map/left/all_to_all | solution.py:348
  144.0 2.3 %collective-permute-done.8.rest_6_ = bf16[8,128,512]{2,1,0:T(8,128)(2,1)S(1)} collective-permute-done((bf16[8,128,512]{2,1,0:T(8,128)(2,1)S(1)}, bf16[8,128,512]{2,1,0:T(8,128)(2,1)S(1)}, u32[]{:S(2)}, u32[]{:S(2)}) %collective-permute-start.8) | collective-permute-done | bytes 1048608 | tf_op jit(solution)/shard_map/weight/ppermute | solution.py:20
  149.4 5.1 %all-to-all-start.2 = ((f32[8,8,256]{2,1,0:T(8,128)}), f32[8,8,256]{2,1,0:T(8,128)S(1)}, u32[]{:S(2)}, u32[]{:S(2)}) async-start(f32[8,8,256]{2,1,0:T(8,128)} %broadcast_in_dim.4), calls=%async_computation.3 | async-start | bytes 131072 | tf_op jit(solution)/shard_map/left/all_to_all | solution.py:351
  155.4 8.1 %project.1 = bf16[320,8192]{1,0:T(8,128)(2,1)} custom-call(s32[6]{0:T(128)} %copy-done.7, bf16[320,512]{1,0:T(8,128)(2,1)} %cot.3, bf16[8,128,512]{2,1,0:T(8,128)(2,1)} %copy-done.13, bf16[8,128,512]{2,1,0:T(8,128)(2,1)} %collective-permute-done.9.rest_1_, bf16[8,128,512]{2,1,0:T(8,128)(2,1)} %collective-permute-done.6.rest_2_, ...), custom_call_target="tpu_custom_call" | custom-call | flops 2684354560 | bytes 13631488 | tf_op jit(solution)/shard_map/weight/project/pallas_call | solution.py:229
  167.8 2.9 %collective-permute-start.16 = (f32[32,576]{1,0:T(8,128)S(1)}, f32[32,576]{1,0:T(8,128)S(1)}, u32[]{:S(2)}, u32[]{:S(2)}) collective-permute-start(f32[32,576]{1,0:T(8,128)S(1)} %add.115), channel_id=1, source_target_pairs={{0,192},{64,128},{128,64},{192,0},{1,193},{65,129},{129,65},{193,1... | collective-permute-start | bytes 221192 | tf_op jit(solution)/shard_map/sums/ppermute | solution.py:20
  171.4 2.6 %collective-permute-done.16 = f32[32,576]{1,0:T(8,128)S(1)} collective-permute-done((f32[32,576]{1,0:T(8,128)S(1)}, f32[32,576]{1,0:T(8,128)S(1)}, u32[]{:S(2)}, u32[]{:S(2)}) %collective-permute-start.16) | collective-permute-done | bytes 73760 | tf_op jit(solution)/shard_map/sums/ppermute | solution.py:20
  175.5 2.6 %collective-permute-start.19 = (f32[32,576]{1,0:T(8,128)S(1)}, f32[32,576]{1,0:T(8,128)S(1)}, u32[]{:S(2)}, u32[]{:S(2)}) collective-permute-start(f32[32,576]{1,0:T(8,128)S(1)} %add_add_fusion.2), channel_id=1, source_target_pairs={{0,24},{8,16},{16,8},{24,0},{1,25},{9,17},{17,9},{25,1},{2,26},{10... | collective-permute-start | bytes 221192 | tf_op jit(solution)/shard_map/sums/ppermute | solution.py:20
  180.4 2.6 %collective-permute-done.18 = f32[32,576]{1,0:T(8,128)S(1)} collective-permute-done((f32[32,576]{1,0:T(8,128)S(1)}, f32[32,576]{1,0:T(8,128)S(1)}, u32[]{:S(2)}, u32[]{:S(2)}) %collective-permute-start.18) | collective-permute-done | bytes 73760 | tf_op jit(solution)/shard_map/sums/ppermute | solution.py:20
  186.6 5.9 %collective-permute-start.23 = (f32[32,576]{1,0:T(8,128)S(1)}, f32[32,576]{1,0:T(8,128)S(1)}, u32[]{:S(2)}, u32[]{:S(2)}) collective-permute-start(f32[32,576]{1,0:T(8,128)S(1)} %add.122), channel_id=1, source_target_pairs={{0,6},{1,7},{2,4},{3,5},{4,2},{5,3},{6,0},{7,1},{8,14},{9,15},{10,... | collective-permute-start | bytes 221192 | tf_op jit(solution)/shard_map/sums/ppermute | solution.py:20
  194.8 5.8 %collective-permute-done.22 = f32[32,576]{1,0:T(8,128)S(1)} collective-permute-done((f32[32,576]{1,0:T(8,128)S(1)}, f32[32,576]{1,0:T(8,128)S(1)}, u32[]{:S(2)}, u32[]{:S(2)}) %collective-permute-start.22) | collective-permute-done | bytes 73760 | tf_op jit(solution)/shard_map/sums/ppermute | solution.py:20
  200.6 6.4 %collective-permute-start.24 = (f32[32,576]{1,0:T(8,128)S(1)}, f32[32,576]{1,0:T(8,128)S(1)}, u32[]{:S(2)}, u32[]{:S(2)}) collective-permute-start(f32[32,576]{1,0:T(8,128)S(1)} %add_add_fusion.mine), channel_id=1, source_target_pairs={{0,32},{32,0},{1,33},{33,1},{2,34},{34,2},{3,35},{35,3},{4,36},{36... | collective-permute-start | bytes 221192 | tf_op jit(solution)/shard_map/sums/ppermute | solution.py:20
  207.9 5.3 %finish.1 = (f32[256,512]{1,0:T(8,128)}, f32[256,512]{1,0:T(8,128)}, f32[64,512]{1,0:T(8,128)}) custom-call(s32[6]{0:T(128)S(1)} %copy-done.8, f32[32,576]{1,0:T(8,128)S(1)} %add_add_fusion.mine, f32[32,576]{1,0:T(8,128)S(1)} %collective-permute-done.24.other, f32[64,256]{1,0:T(8,128)S(1)} %bitcast.17, f32[256,512]{1,0:T(8,128)S(1)} %get-tuple-element.50.merged), custom_call_target="tpu_custom_call" | custom-call | tf_op jit(solution)/shard_map/finish/finish/pallas_call | solution.py:313
  (83 shorter events, 26.0 us)
Async XLA Ops:
  7.2 89.5 %all-gather.3.cloned.1.call-start = ((), (), s32[]{:S(2)}) async-start(), calls=%async_computation.5 | async-start | bytes 2359296 | tf_op jit(solution)/shard_map/exchange/all_gather | solution.py:333
  7.9 156.3 %reduce-scatter.2.cloned.1.call-start = ((), (), s32[]{:S(2)}) async-start(), calls=%async_computation.4 | async-start | bytes 4718592 | tf_op jit(solution)/shard_map/gradient/reduce_scatter | solution.py:340
  11.8 20.6 %collective-permute-start = (bf16[160,2560]{1,0:T(8,128)(2,1)S(1)}, bf16[160,2560]{1,0:T(8,128)(2,1)S(1)}, u32[]{:S(2)}, u32[]{:S(2)}) collective-permute-start(bf16[160,2560]{1,0:T(8,128)(2,1)S(1)} %get-tuple-element.29), channel_id=1, source_target_pairs={{0,16},{8,24},{16,0},{24,8},{1,17},{9,25},{17,1},{25,9},{2,18},{10... | collective-permute-start | bytes 2457608 | tf_op jit(solution)/shard_map/exchange/ppermute | solution.py:20
  15.4 34.5 %collective-permute-start.1 = (bf16[160,2560]{1,0:T(8,128)(2,1)S(1)}, bf16[160,2560]{1,0:T(8,128)(2,1)S(1)}, u32[]{:S(2)}, u32[]{:S(2)}) collective-permute-start(bf16[160,2560]{1,0:T(8,128)(2,1)S(1)} %get-tuple-element.30), channel_id=1, source_target_pairs={{0,16},{8,24},{16,0},{24,8},{1,17},{9,25},{17,1},{25,9},{2,18},{10... | collective-permute-start | bytes 2457608 | tf_op jit(solution)/shard_map/exchange/ppermute | solution.py:20
  15.5 53.7 %collective-permute-start.2 = (bf16[160,2560]{1,0:T(8,128)(2,1)S(1)}, bf16[160,2560]{1,0:T(8,128)(2,1)S(1)}, u32[]{:S(2)}, u32[]{:S(2)}) collective-permute-start(bf16[160,2560]{1,0:T(8,128)(2,1)S(1)} %get-tuple-element.31), channel_id=1, source_target_pairs={{0,24},{8,16},{16,8},{24,0},{1,25},{9,17},{17,9},{25,1},{2,26},{10... | collective-permute-start | bytes 2457608 | tf_op jit(solution)/shard_map/exchange/ppermute | solution.py:20
  18.1 68.7 %collective-permute-start.3 = (bf16[160,2560]{1,0:T(8,128)(2,1)S(1)}, bf16[160,2560]{1,0:T(8,128)(2,1)S(1)}, u32[]{:S(2)}, u32[]{:S(2)}) collective-permute-start(bf16[160,2560]{1,0:T(8,128)(2,1)S(1)} %get-tuple-element.32), channel_id=1, source_target_pairs={{0,24},{8,16},{16,8},{24,0},{1,25},{9,17},{17,9},{25,1},{2,26},{10... | collective-permute-start | bytes 2457608 | tf_op jit(solution)/shard_map/exchange/ppermute | solution.py:20
  18.2 68.6 %collective-permute-start.4 = (bf16[160,2560]{1,0:T(8,128)(2,1)S(1)}, bf16[160,2560]{1,0:T(8,128)(2,1)S(1)}, u32[]{:S(2)}, u32[]{:S(2)}) collective-permute-start(bf16[160,2560]{1,0:T(8,128)(2,1)S(1)} %get-tuple-element.33), channel_id=1, source_target_pairs={{0,8},{8,0},{16,24},{24,16},{1,9},{9,1},{17,25},{25,17},{2,10},{10... | collective-permute-start | bytes 2457608 | tf_op jit(solution)/shard_map/exchange/ppermute | solution.py:20
  32.4 54.4 %collective-permute-start.5 = (bf16[160,2560]{1,0:T(8,128)(2,1)S(1)}, bf16[160,2560]{1,0:T(8,128)(2,1)S(1)}, u32[]{:S(2)}, u32[]{:S(2)}) collective-permute-start(bf16[160,2560]{1,0:T(8,128)(2,1)S(1)} %get-tuple-element.34), channel_id=1, source_target_pairs={{0,8},{8,0},{16,24},{24,16},{1,9},{9,1},{17,25},{25,17},{2,10},{10... | collective-permute-start | bytes 2457608 | tf_op jit(solution)/shard_map/exchange/ppermute | solution.py:20
  98.1 48.2 %collective-permute-start.8 = (bf16[8,128,512]{2,1,0:T(8,128)(2,1)S(1)}, bf16[8,128,512]{2,1,0:T(8,128)(2,1)S(1)}, u32[]{:S(2)}, u32[]{:S(2)}) collective-permute-start(bf16[8,128,512]{2,1,0:T(8,128)(2,1)S(1)} %constant_dynamic-slice_fusion.rest_0_), channel_id=1, source_target_pairs={{0,24},{8,16},{16,8},{24,0},{1,25},{9,17},{17,9},{25,1},{2,26},{10... | collective-permute-start | bytes 3145736 | tf_op jit(solution)/shard_map/weight/ppermute | solution.py:20
  100.9 45.4 %collective-permute-start.7 = (bf16[8,128,512]{2,1,0:T(8,128)(2,1)S(1)}, bf16[8,128,512]{2,1,0:T(8,128)(2,1)}, u32[]{:S(2)}, u32[]{:S(2)}) collective-permute-start(bf16[8,128,512]{2,1,0:T(8,128)(2,1)S(1)} %constant_dynamic-slice_fusion.rest_0_), channel_id=1, source_target_pairs={{0,16},{8,24},{16,0},{24,8},{1,17},{9,25},{17,1},{25,9},{2,18},{10... | collective-permute-start | bytes 3145736 | tf_op jit(solution)/shard_map/weight/ppermute | solution.py:20
  101.4 45.4 %collective-permute-start.6 = (bf16[8,128,512]{2,1,0:T(8,128)(2,1)S(1)}, bf16[8,128,512]{2,1,0:T(8,128)(2,1)}, u32[]{:S(2)}, u32[]{:S(2)}) collective-permute-start(bf16[8,128,512]{2,1,0:T(8,128)(2,1)S(1)} %constant_dynamic-slice_fusion.rest_0_), channel_id=1, source_target_pairs={{0,8},{8,0},{16,24},{24,16},{1,9},{9,1},{17,25},{25,17},{2,10},{10... | collective-permute-start | bytes 3145736 | tf_op jit(solution)/shard_map/weight/ppermute | solution.py:20
  146.8 7.7 %collective-permute-start.9 = (bf16[8,128,512]{2,1,0:T(8,128)(2,1)S(1)}, bf16[8,128,512]{2,1,0:T(8,128)(2,1)}, u32[]{:S(2)}, u32[]{:S(2)}) collective-permute-start(bf16[8,128,512]{2,1,0:T(8,128)(2,1)S(1)} %constant_dynamic-slice_fusion.rest_0_), channel_id=1, source_target_pairs={{0,32},{32,0},{1,33},{33,1},{2,34},{34,2},{3,35},{35,3},{4,36},{36... | collective-permute-start | bytes 3145736 | tf_op jit(solution)/shard_map/weight/ppermute | solution.py:20
  148.3 6.2 %collective-permute-start.10 = (bf16[8,128,512]{2,1,0:T(8,128)(2,1)}, bf16[8,128,512]{2,1,0:T(8,128)(2,1)}, u32[]{:S(2)}, u32[]{:S(2)}) collective-permute-start(bf16[8,128,512]{2,1,0:T(8,128)(2,1)} %collective-permute-done.6.rest_2_), channel_id=1, source_target_pairs={{0,32},{32,0},{1,33},{33,1},{2,34},{34,2},{3,35},{35,3},{4,36},{36... | collective-permute-start | bytes 3145736 | tf_op jit(solution)/shard_map/weight/ppermute | solution.py:20
  148.3 7.1 %collective-permute-start.11 = (bf16[8,128,512]{2,1,0:T(8,128)(2,1)}, bf16[8,128,512]{2,1,0:T(8,128)(2,1)}, u32[]{:S(2)}, u32[]{:S(2)}) collective-permute-start(bf16[8,128,512]{2,1,0:T(8,128)(2,1)} %collective-permute-done.7.rest_4_), channel_id=1, source_target_pairs={{0,32},{32,0},{1,33},{33,1},{2,34},{34,2},{3,35},{35,3},{4,36},{36... | collective-permute-start | bytes 3145736 | tf_op jit(solution)/shard_map/weight/ppermute | solution.py:20
  148.8 6.6 %collective-permute-start.12 = (bf16[8,128,512]{2,1,0:T(8,128)(2,1)S(1)}, bf16[8,128,512]{2,1,0:T(8,128)(2,1)}, u32[]{:S(2)}, u32[]{:S(2)}) collective-permute-start(bf16[8,128,512]{2,1,0:T(8,128)(2,1)S(1)} %collective-permute-done.8.rest_6_), channel_id=1, source_target_pairs={{0,32},{32,0},{1,33},{33,1},{2,34},{34,2},{3,35},{35,3},{4,36},{36... | collective-permute-start | bytes 3145736 | tf_op jit(solution)/shard_map/weight/ppermute | solution.py:20
  149.4 14.8 %all-to-all-start.2 = ((f32[8,8,256]{2,1,0:T(8,128)}), f32[8,8,256]{2,1,0:T(8,128)S(1)}, u32[]{:S(2)}, u32[]{:S(2)}) async-start(f32[8,8,256]{2,1,0:T(8,128)} %broadcast_in_dim.4), calls=%async_computation.3 | async-start | bytes 131072 | tf_op jit(solution)/shard_map/left/all_to_all | solution.py:351
  167.8 6.2 %collective-permute-start.16 = (f32[32,576]{1,0:T(8,128)S(1)}, f32[32,576]{1,0:T(8,128)S(1)}, u32[]{:S(2)}, u32[]{:S(2)}) collective-permute-start(f32[32,576]{1,0:T(8,128)S(1)} %add.115), channel_id=1, source_target_pairs={{0,192},{64,128},{128,64},{192,0},{1,193},{65,129},{129,65},{193,1... | collective-permute-start | bytes 221192 | tf_op jit(solution)/shard_map/sums/ppermute | solution.py:20
  170.7 4.8 %collective-permute-start.15 = (f32[32,576]{1,0:T(8,128)S(1)}, f32[32,576]{1,0:T(8,128)S(1)}, u32[]{:S(2)}, u32[]{:S(2)}) collective-permute-start(f32[32,576]{1,0:T(8,128)S(1)} %add.115), channel_id=1, source_target_pairs={{0,128},{64,192},{128,0},{192,64},{1,129},{65,193},{129,1},{193,65... | collective-permute-start | bytes 221192 | tf_op jit(solution)/shard_map/sums/ppermute | solution.py:20
  175.5 4.8 %collective-permute-start.19 = (f32[32,576]{1,0:T(8,128)S(1)}, f32[32,576]{1,0:T(8,128)S(1)}, u32[]{:S(2)}, u32[]{:S(2)}) collective-permute-start(f32[32,576]{1,0:T(8,128)S(1)} %add_add_fusion.2), channel_id=1, source_target_pairs={{0,24},{8,16},{16,8},{24,0},{1,25},{9,17},{17,9},{25,1},{2,26},{10... | collective-permute-start | bytes 221192 | tf_op jit(solution)/shard_map/sums/ppermute | solution.py:20
  178.1 4.9 %collective-permute-start.18 = (f32[32,576]{1,0:T(8,128)S(1)}, f32[32,576]{1,0:T(8,128)S(1)}, u32[]{:S(2)}, u32[]{:S(2)}) collective-permute-start(f32[32,576]{1,0:T(8,128)S(1)} %add_add_fusion.2), channel_id=1, source_target_pairs={{0,16},{8,24},{16,0},{24,8},{1,17},{9,25},{17,1},{25,9},{2,18},{10... | collective-permute-start | bytes 221192 | tf_op jit(solution)/shard_map/sums/ppermute | solution.py:20
  186.6 8.2 %collective-permute-start.23 = (f32[32,576]{1,0:T(8,128)S(1)}, f32[32,576]{1,0:T(8,128)S(1)}, u32[]{:S(2)}, u32[]{:S(2)}) collective-permute-start(f32[32,576]{1,0:T(8,128)S(1)} %add.122), channel_id=1, source_target_pairs={{0,6},{1,7},{2,4},{3,5},{4,2},{5,3},{6,0},{7,1},{8,14},{9,15},{10,... | collective-permute-start | bytes 221192 | tf_op jit(solution)/shard_map/sums/ppermute | solution.py:20
  192.5 8.1 %collective-permute-start.22 = (f32[32,576]{1,0:T(8,128)S(1)}, f32[32,576]{1,0:T(8,128)S(1)}, u32[]{:S(2)}, u32[]{:S(2)}) collective-permute-start(f32[32,576]{1,0:T(8,128)S(1)} %add.122), channel_id=1, source_target_pairs={{0,4},{1,5},{2,6},{3,7},{4,0},{5,1},{6,2},{7,3},{8,12},{9,13},{10,... | collective-permute-start | bytes 221192 | tf_op jit(solution)/shard_map/sums/ppermute | solution.py:20
  193.5 7.1 %collective-permute-start.21 = (f32[32,576]{1,0:T(8,128)S(1)}, f32[32,576]{1,0:T(8,128)S(1)}, u32[]{:S(2)}, u32[]{:S(2)}) collective-permute-start(f32[32,576]{1,0:T(8,128)S(1)} %add.122), channel_id=1, source_target_pairs={{0,2},{1,3},{2,0},{3,1},{4,6},{5,7},{6,4},{7,5},{8,10},{9,11},{10,... | collective-permute-start | bytes 221192 | tf_op jit(solution)/shard_map/sums/ppermute | solution.py:20
  200.6 7.3 %collective-permute-start.24 = (f32[32,576]{1,0:T(8,128)S(1)}, f32[32,576]{1,0:T(8,128)S(1)}, u32[]{:S(2)}, u32[]{:S(2)}) collective-permute-start(f32[32,576]{1,0:T(8,128)S(1)} %add_add_fusion.mine), channel_id=1, source_target_pairs={{0,32},{32,0},{1,33},{33,1},{2,34},{34,2},{3,35},{35,3},{4,36},{36... | collective-permute-start | bytes 221192 | tf_op jit(solution)/shard_map/sums/ppermute | solution.py:20
  (19 other events, 397.4 us)
Sparse Core Ops, SparseCore 0:
  9.8 41.1 all-gather.2
  96.9 59.7 reduce-scatter.1

commit v7 on v6

--- a/solution.py
+++ b/solution.py
@@ -271,6 +271,19 @@
         compiler_params=pltpu.CompilerParams(vmem_limit_bytes=32 * 1024 * 1024),
         name="right_terms",
     )(place, after, gradient, error, p_total)
+
+
+def add_kernel(_, *refs):
+    refs[-1][...] = tree([ref[...] for ref in refs[:-1]])
+
+
+def add_after(after, parts):
+    return pl.pallas_call(
+        add_kernel,
+        out_shape=jax.ShapeDtypeStruct(parts[0].shape, F32),
+        compiler_params=pltpu.CompilerParams(vmem_limit_bytes=4 * 1024 * 1024),
+        name="add_after",
+    )(after, *parts)
 
 
 def eliminate(gram):
@@ -355,12 +368,13 @@
         for half in halves:
             weights += [half, swap(half, "c", NC, 1)]
         input_grad = project(place, cotangent, weights)
+        swapped = tree([half[0, :16, :128] for half in weights[1::2]])
 
     with jax.named_scope("sums"):
-        merged, keep, give = right_terms(place, input_grad[:16, :128], gradient, error, p_total)
+        merged, keep, give = right_terms(place, swapped, gradient, error, p_total)
         keep = keep + swap(give, "c", NC, 1)
         keep = tree(swaps(keep, "y", NY))
-        keep = tree(swaps(keep, "x", NX))
+        keep = add_after(input_grad[:16, :128], swaps(keep, "x", NX))
         keep = keep + swap(keep, "z", NZ, 1)
         keep = tree([keep] + [swap(keep, "z", NZ, k) for k in (2, 4, 6)])
         other = swap(keep, "c", NC, 1)

time: 221 us -> 219 us (level)
    ppermute x25, waiting for transfers between devices: 87.7 us -> 83.1 us  [swap(): return lax.ppermute(value, axis, [(i, i ^ k) for i in range(size)])]
    all_to_all x1, waiting for transfers between devices: 0.01 us -> 3.22 us  [local(): lax.all_to_all(left, ('y', 'c'), 0, 0, tiled=True)]
  transfers between devices with their start and end apart: 28 -> 28, of which waited for: 16 -> 16; matrix products, arithmetic and copies ran while one was open for 1% -> 2% of each run, Pallas kernels for 13% -> 13%
where the time goes in v7:
time: 219 us; the launch traced here: 218 us
  waiting for transfers between devices  87 us (40%)
  starting transfers between devices  42.1 us (19%)
  Pallas kernels  35.5 us (16%)
  blocking collectives  31.8 us (15%)
  between operations  14.2 us (6%)
  local copies, waits for them, and re-layouts  6.9 us (3%)
    ppermute x25, waiting for transfers between devices, swap(): return lax.ppermute(value, axis, [(i, i ^ k) for i in range(size)])  83.1 us
    ppermute x25, starting transfers between devices, swap(): return lax.ppermute(value, axis, [(i, i ^ k) for i in range(size)])  37 us
    all_to_all x1, blocking collectives, local(): left = tree(list(lax.all_to_all(left, 'z', 0, 0, tiled=True)))  16.4 us
    all_to_all x1, blocking collectives, local(): left = tree(list(lax.all_to_all(left, ('y', 'c'), 0, 0, tiled=True)))  15.4 us
    pallas_call x1, Pallas kernels, left_terms(): pl.pallas_call(functools.partial(left_kernel, 1 + len(pieces)), out_shape...  10.6 us
    pallas_call x1, Pallas kernels, project(): pl.pallas_call(project_kernel, out_shape=jax.ShapeDtypeStruct((tokens, NX...  8.08 us
    pallas_call x1, Pallas kernels, gradient_terms(): pl.pallas_call(functools.partial(gradient_kernel, 1 + len(pieces)), out_s...  7.67 us
    pallas_call x1, Pallas kernels, finish(): pl.pallas_call(finish_kernel, out_shape=(jax.ShapeDtypeStruct(merged.shap...  5.29 us
  transfers between devices with their start and end apart: 28, of which 16 were waited for; matrix products, arithmetic and copies ran while one was open for 2% of the time, Pallas kernels for 13%

profile of v7, /device:TPU:1, one launch (start us, length us, event | category | flops | bytes accessed | tf_op | source)
XLA Modules:
  0.0 218.4 jit_solution(5336026816026814616)
XLA Ops:
  9.0 2.8 %pack.1 = (bf16[160,2560]{1,0:T(8,128)(2,1)S(1)}, bf16[160,2560]{1,0:T(8,128)(2,1)S(1)}, bf16[160,2560]{1,0:T(8,128)(2,1)S(1)}, bf16[160,2560]{1,0:T(8,128)(2,1)...) custom-call(s32[6]{0:T(128)S(1)} %stack.27.place, bf16[320,8192]{1,0:T(8,128)(2,1)} %refs_7_.3, ...), custom_call_target="tpu_custom_call" | custom-call | bytes 5242880 | tf_op jit(solution)/shard_map/exchange/pack/pallas_call | solution.py:71
  11.8 3.7 %collective-permute-start = (bf16[160,2560]{1,0:T(8,128)(2,1)S(1)}, bf16[160,2560]{1,0:T(8,128)(2,1)S(1)}, u32[]{:S(2)}, u32[]{:S(2)}) collective-permute-start(bf16[160,2560]{1,0:T(8,128)(2,1)S(1)} %get-tuple-element.29), channel_id=1, source_target_pairs={{0,16},{8,24},{16,0},{24,8},{1,17},{9,25},{17,1},{25,9},{2,18},{10... | collective-permute-start | bytes 2457608 | tf_op jit(solution)/shard_map/exchange/ppermute | solution.py:20
  15.5 2.6 %collective-permute-start.2 = (bf16[160,2560]{1,0:T(8,128)(2,1)S(1)}, bf16[160,2560]{1,0:T(8,128)(2,1)S(1)}, u32[]{:S(2)}, u32[]{:S(2)}) collective-permute-start(bf16[160,2560]{1,0:T(8,128)(2,1)S(1)} %get-tuple-element.31), channel_id=1, source_target_pairs={{0,24},{8,16},{16,8},{24,0},{1,25},{9,17},{17,9},{25,1},{2,26},{10... | collective-permute-start | bytes 2457608 | tf_op jit(solution)/shard_map/exchange/ppermute | solution.py:20
  18.3 14.0 %collective-permute-done.refs_1_.refs_8_ = bf16[160,2560]{1,0:T(8,128)(2,1)S(1)} collective-permute-done((bf16[160,2560]{1,0:T(8,128)(2,1)S(1)}, bf16[160,2560]{1,0:T(8,128)(2,1)S(1)}, u32[]{:S(2)}, u32[]{:S(2)}) %collective-permute-start) | collective-permute-done | bytes 819232 | tf_op jit(solution)/shard_map/exchange/ppermute | solution.py:20
  32.4 2.3 %collective-permute-start.5 = (bf16[160,2560]{1,0:T(8,128)(2,1)S(1)}, bf16[160,2560]{1,0:T(8,128)(2,1)S(1)}, u32[]{:S(2)}, u32[]{:S(2)}) collective-permute-start(bf16[160,2560]{1,0:T(8,128)(2,1)S(1)} %get-tuple-element.34), channel_id=1, source_target_pairs={{0,8},{8,0},{16,24},{24,16},{1,9},{9,1},{17,25},{25,17},{2,10},{10... | collective-permute-start | bytes 2457608 | tf_op jit(solution)/shard_map/exchange/ppermute | solution.py:20
  34.7 15.3 %collective-permute-done.1.refs_2_.refs_9_ = bf16[160,2560]{1,0:T(8,128)(2,1)S(1)} collective-permute-done((bf16[160,2560]{1,0:T(8,128)(2,1)S(1)}, bf16[160,2560]{1,0:T(8,128)(2,1)S(1)}, u32[]{:S(2)}, u32[]{:S(2)}) %collective-permute-start.1) | collective-permute-done | bytes 819232 | tf_op jit(solution)/shard_map/exchange/ppermute | solution.py:20
  49.9 19.3 %collective-permute-done.2.refs_3_.refs_10_ = bf16[160,2560]{1,0:T(8,128)(2,1)S(1)} collective-permute-done((bf16[160,2560]{1,0:T(8,128)(2,1)S(1)}, bf16[160,2560]{1,0:T(8,128)(2,1)S(1)}, u32[]{:S(2)}, u32[]{:S(2)}) %collective-permute-start.2) | collective-permute-done | bytes 819232 | tf_op jit(solution)/shard_map/exchange/ppermute | solution.py:20
  69.3 17.6 %collective-permute-done.3.refs_4_.refs_11_ = bf16[160,2560]{1,0:T(8,128)(2,1)S(1)} collective-permute-done((bf16[160,2560]{1,0:T(8,128)(2,1)S(1)}, bf16[160,2560]{1,0:T(8,128)(2,1)S(1)}, u32[]{:S(2)}, u32[]{:S(2)}) %collective-permute-start.3) | collective-permute-done | bytes 819232 | tf_op jit(solution)/shard_map/exchange/ppermute | solution.py:20
  88.9 7.7 %gradient_terms.1 = f32[8,512,256]{2,1,0:T(8,128)} custom-call(s32[6]{0:T(128)S(1)} %stack.27.place, bf16[320,512]{1,0:T(8,128)(2,1)S(1)} %copy-done.3, bf16[160,2560]{1,0:T(8,128)(2,1)S(1)} %collective-permute-done.refs_1_.refs_8_, bf16[160,2560]{1,0:T(8,128)(2,1)S(1)} %collective-permute-done.1.refs_2_.refs_9_, bf16[160,2560]{1,0:T(8,128)(2,1)} %copy-done.9, ...), custom_call_target="tpu_custom_call" | custom-call | flops 2684354560 | bytes 9437184 | tf_op jit(solution)/shard_map/gradient/gradient_terms/pallas_call | solution.py:146
  98.0 2.8 %collective-permute-start.8 = (bf16[8,128,512]{2,1,0:T(8,128)(2,1)S(1)}, bf16[8,128,512]{2,1,0:T(8,128)(2,1)}, u32[]{:S(2)}, u32[]{:S(2)}) collective-permute-start(bf16[8,128,512]{2,1,0:T(8,128)(2,1)S(1)} %constant_dynamic-slice_fusion.rest_0_), channel_id=1, source_target_pairs={{0,24},{8,16},{16,8},{24,0},{1,25},{9,17},{17,9},{25,1},{2,26},{10... | collective-permute-start | bytes 3145736 | tf_op jit(solution)/shard_map/weight/ppermute | solution.py:20
  101.5 10.6 %left_terms.1 = f32[8,8,8,256]{3,2,1,0:T(8,128)S(1)} custom-call(s32[6]{0:T(128)S(1)} %stack.27.place, f32[64,512]{1,0:T(8,128)S(1)} %copy-done.6, f32[256,512]{1,0:T(8,128)S(1)} %bitcast.16, bf16[320,512]{1,0:T(8,128)(2,1)S(1)} %copy-done.3, bf16[160,2560]{1,0:T(8,128)(2,1)} %copy-done, bf16[160,2560]{1,0:T(8,128)(2,1)} %copy-done.1, ...), custom_call_target="tpu_custom_call" | custom-call | flops 1006632960 | bytes 5242880 | tf_op jit(solution)/shard_map/left/left_terms/pallas_call | solution.py:173
  112.1 15.4 %all_to_all.15 = f32[8,8,8,256]{3,2,1,0:T(8,128)S(1)} all-to-all(f32[8,8,8,256]{3,2,1,0:T(8,128)S(1)} %left_terms.1), channel_id=1, replica_groups=mesh['y'=4,'c'=2,'x'=4,'z'=8] {'y','c'}, dimensions={0} | all-to-all | bytes 1048576 | tf_op jit(solution)/shard_map/left/all_to_all | solution.py:360
  127.6 16.4 %all_to_all.16 = f32[8,8,256]{2,1,0:T(8,128)S(1)} all-to-all(f32[8,8,256]{2,1,0:T(8,128)S(1)} %fusion.2), channel_id=1, replica_groups=mesh['y'=4,'c'=2,'x'=4,'z'=8] {'z'}, dimensions={0} | all-to-all | bytes 131072 | tf_op jit(solution)/shard_map/left/all_to_all | solution.py:361
  143.9 2.3 %collective-permute-done.8.rest_6_ = bf16[8,128,512]{2,1,0:T(8,128)(2,1)} collective-permute-done((bf16[8,128,512]{2,1,0:T(8,128)(2,1)S(1)}, bf16[8,128,512]{2,1,0:T(8,128)(2,1)}, u32[]{:S(2)}, u32[]{:S(2)}) %collective-permute-start.8) | collective-permute-done | bytes 1048608 | tf_op jit(solution)/shard_map/weight/ppermute | solution.py:20
  149.4 5.1 %all-to-all-start.2 = ((f32[8,8,256]{2,1,0:T(8,128)}), f32[8,8,256]{2,1,0:T(8,128)S(1)}, u32[]{:S(2)}, u32[]{:S(2)}) async-start(f32[8,8,256]{2,1,0:T(8,128)} %broadcast_in_dim.4), calls=%async_computation.3 | async-start | bytes 131072 | tf_op jit(solution)/shard_map/left/all_to_all | solution.py:364
  156.1 3.2 %all-to-all-done.2 = f32[8,8,256]{2,1,0:T(8,128)S(1)} async-done(((f32[8,8,256]{2,1,0:T(8,128)}), f32[8,8,256]{2,1,0:T(8,128)S(1)}, u32[]{:S(2)}, u32[]{:S(2)}) %all-to-all-start.2) | async-done | bytes 65568 | tf_op jit(solution)/shard_map/left/all_to_all | solution.py:364
  170.5 2.6 %collective-permute-start.19 = (f32[32,576]{1,0:T(8,128)S(1)}, f32[32,576]{1,0:T(8,128)S(1)}, u32[]{:S(2)}, u32[]{:S(2)}) collective-permute-start(f32[32,576]{1,0:T(8,128)S(1)} %add_add_fusion.1.refs_0_), channel_id=1, source_target_pairs={{0,24},{8,16},{16,8},{24,0},{1,25},{9,17},{17,9},{25,1},{2,26},{10... | collective-permute-start | bytes 221192 | tf_op jit(solution)/shard_map/sums/ppermute | solution.py:20
  173.8 8.1 %project.1 = bf16[320,8192]{1,0:T(8,128)(2,1)} custom-call(s32[6]{0:T(128)} %copy-done.7, bf16[320,512]{1,0:T(8,128)(2,1)} %cot.3, bf16[8,128,512]{2,1,0:T(8,128)(2,1)} %copy-done.13, bf16[8,128,512]{2,1,0:T(8,128)(2,1)} %copy-done.14, bf16[8,128,512]{2,1,0:T(8,128)(2,1)} %collective-permute-done.6.rest_2_, ...), custom_call_target="tpu_custom_call" | custom-call | flops 2684354560 | bytes 13631488 | tf_op jit(solution)/shard_map/weight/project/pallas_call | solution.py:229
  182.6 1.7 collective-permute-start.20
  184.4 1.8 collective-permute-done.20
  186.2 5.9 %collective-permute-start.23 = (f32[32,576]{1,0:T(8,128)S(1)}, f32[32,576]{1,0:T(8,128)S(1)}, u32[]{:S(2)}, u32[]{:S(2)}) collective-permute-start(f32[32,576]{1,0:T(8,128)S(1)} %add.127), channel_id=1, source_target_pairs={{0,6},{1,7},{2,4},{3,5},{4,2},{5,3},{6,0},{7,1},{8,14},{9,15},{10,... | collective-permute-start | bytes 221192 | tf_op jit(solution)/shard_map/sums/ppermute | solution.py:20
  194.7 5.4 %collective-permute-done.22 = f32[32,576]{1,0:T(8,128)S(1)} collective-permute-done((f32[32,576]{1,0:T(8,128)S(1)}, f32[32,576]{1,0:T(8,128)S(1)}, u32[]{:S(2)}, u32[]{:S(2)}) %collective-permute-start.22) | collective-permute-done | bytes 73760 | tf_op jit(solution)/shard_map/sums/ppermute | solution.py:20
  200.2 5.2 %collective-permute-start.24 = (f32[32,576]{1,0:T(8,128)S(1)}, f32[32,576]{1,0:T(8,128)S(1)}, u32[]{:S(2)}, u32[]{:S(2)}) collective-permute-start(f32[32,576]{1,0:T(8,128)S(1)} %add_add_fusion.mine), channel_id=1, source_target_pairs={{0,32},{32,0},{1,33},{33,1},{2,34},{34,2},{3,35},{35,3},{4,36},{36... | collective-permute-start | bytes 221192 | tf_op jit(solution)/shard_map/sums/ppermute | solution.py:20
  206.3 5.3 %finish.1 = (f32[256,512]{1,0:T(8,128)}, f32[256,512]{1,0:T(8,128)}, f32[64,512]{1,0:T(8,128)}) custom-call(s32[6]{0:T(128)S(1)} %copy-done.8, f32[32,576]{1,0:T(8,128)S(1)} %add_add_fusion.mine, f32[32,576]{1,0:T(8,128)S(1)} %collective-permute-done.24.other, f32[64,256]{1,0:T(8,128)S(1)} %bitcast.19, f32[256,512]{1,0:T(8,128)S(1)} %get-tuple-element.50.merged), custom_call_target="tpu_custom_call" | custom-call | tf_op jit(solution)/shard_map/finish/finish/pallas_call | solution.py:326
  (84 shorter events, 27.3 us)
Async XLA Ops:
  7.2 89.5 %all-gather.3.cloned.1.call-start = ((), (), s32[]{:S(2)}) async-start(), calls=%async_computation.5 | async-start | bytes 2359296 | tf_op jit(solution)/shard_map/exchange/all_gather | solution.py:346
  7.9 151.4 %reduce-scatter.2.cloned.1.call-start = ((), (), s32[]{:S(2)}) async-start(), calls=%async_computation.4 | async-start | bytes 4718592 | tf_op jit(solution)/shard_map/gradient/reduce_scatter | solution.py:353
  11.8 20.6 %collective-permute-start = (bf16[160,2560]{1,0:T(8,128)(2,1)S(1)}, bf16[160,2560]{1,0:T(8,128)(2,1)S(1)}, u32[]{:S(2)}, u32[]{:S(2)}) collective-permute-start(bf16[160,2560]{1,0:T(8,128)(2,1)S(1)} %get-tuple-element.29), channel_id=1, source_target_pairs={{0,16},{8,24},{16,0},{24,8},{1,17},{9,25},{17,1},{25,9},{2,18},{10... | collective-permute-start | bytes 2457608 | tf_op jit(solution)/shard_map/exchange/ppermute | solution.py:20
  15.4 34.5 %collective-permute-start.1 = (bf16[160,2560]{1,0:T(8,128)(2,1)S(1)}, bf16[160,2560]{1,0:T(8,128)(2,1)S(1)}, u32[]{:S(2)}, u32[]{:S(2)}) collective-permute-start(bf16[160,2560]{1,0:T(8,128)(2,1)S(1)} %get-tuple-element.30), channel_id=1, source_target_pairs={{0,16},{8,24},{16,0},{24,8},{1,17},{9,25},{17,1},{25,9},{2,18},{10... | collective-permute-start | bytes 2457608 | tf_op jit(solution)/shard_map/exchange/ppermute | solution.py:20
  15.5 53.7 %collective-permute-start.2 = (bf16[160,2560]{1,0:T(8,128)(2,1)S(1)}, bf16[160,2560]{1,0:T(8,128)(2,1)S(1)}, u32[]{:S(2)}, u32[]{:S(2)}) collective-permute-start(bf16[160,2560]{1,0:T(8,128)(2,1)S(1)} %get-tuple-element.31), channel_id=1, source_target_pairs={{0,24},{8,16},{16,8},{24,0},{1,25},{9,17},{17,9},{25,1},{2,26},{10... | collective-permute-start | bytes 2457608 | tf_op jit(solution)/shard_map/exchange/ppermute | solution.py:20
  18.1 68.7 %collective-permute-start.3 = (bf16[160,2560]{1,0:T(8,128)(2,1)S(1)}, bf16[160,2560]{1,0:T(8,128)(2,1)S(1)}, u32[]{:S(2)}, u32[]{:S(2)}) collective-permute-start(bf16[160,2560]{1,0:T(8,128)(2,1)S(1)} %get-tuple-element.32), channel_id=1, source_target_pairs={{0,24},{8,16},{16,8},{24,0},{1,25},{9,17},{17,9},{25,1},{2,26},{10... | collective-permute-start | bytes 2457608 | tf_op jit(solution)/shard_map/exchange/ppermute | solution.py:20
  18.2 68.6 %collective-permute-start.4 = (bf16[160,2560]{1,0:T(8,128)(2,1)S(1)}, bf16[160,2560]{1,0:T(8,128)(2,1)S(1)}, u32[]{:S(2)}, u32[]{:S(2)}) collective-permute-start(bf16[160,2560]{1,0:T(8,128)(2,1)S(1)} %get-tuple-element.33), channel_id=1, source_target_pairs={{0,8},{8,0},{16,24},{24,16},{1,9},{9,1},{17,25},{25,17},{2,10},{10... | collective-permute-start | bytes 2457608 | tf_op jit(solution)/shard_map/exchange/ppermute | solution.py:20
  32.4 54.4 %collective-permute-start.5 = (bf16[160,2560]{1,0:T(8,128)(2,1)S(1)}, bf16[160,2560]{1,0:T(8,128)(2,1)S(1)}, u32[]{:S(2)}, u32[]{:S(2)}) collective-permute-start(bf16[160,2560]{1,0:T(8,128)(2,1)S(1)} %get-tuple-element.34), channel_id=1, source_target_pairs={{0,8},{8,0},{16,24},{24,16},{1,9},{9,1},{17,25},{25,17},{2,10},{10... | collective-permute-start | bytes 2457608 | tf_op jit(solution)/shard_map/exchange/ppermute | solution.py:20
  98.0 48.2 %collective-permute-start.8 = (bf16[8,128,512]{2,1,0:T(8,128)(2,1)S(1)}, bf16[8,128,512]{2,1,0:T(8,128)(2,1)}, u32[]{:S(2)}, u32[]{:S(2)}) collective-permute-start(bf16[8,128,512]{2,1,0:T(8,128)(2,1)S(1)} %constant_dynamic-slice_fusion.rest_0_), channel_id=1, source_target_pairs={{0,24},{8,16},{16,8},{24,0},{1,25},{9,17},{17,9},{25,1},{2,26},{10... | collective-permute-start | bytes 3145736 | tf_op jit(solution)/shard_map/weight/ppermute | solution.py:20
  100.8 45.4 %collective-permute-start.7 = (bf16[8,128,512]{2,1,0:T(8,128)(2,1)S(1)}, bf16[8,128,512]{2,1,0:T(8,128)(2,1)}, u32[]{:S(2)}, u32[]{:S(2)}) collective-permute-start(bf16[8,128,512]{2,1,0:T(8,128)(2,1)S(1)} %constant_dynamic-slice_fusion.rest_0_), channel_id=1, source_target_pairs={{0,16},{8,24},{16,0},{24,8},{1,17},{9,25},{17,1},{25,9},{2,18},{10... | collective-permute-start | bytes 3145736 | tf_op jit(solution)/shard_map/weight/ppermute | solution.py:20
  101.3 45.4 %collective-permute-start.6 = (bf16[8,128,512]{2,1,0:T(8,128)(2,1)S(1)}, bf16[8,128,512]{2,1,0:T(8,128)(2,1)}, u32[]{:S(2)}, u32[]{:S(2)}) collective-permute-start(bf16[8,128,512]{2,1,0:T(8,128)(2,1)S(1)} %constant_dynamic-slice_fusion.rest_0_), channel_id=1, source_target_pairs={{0,8},{8,0},{16,24},{24,16},{1,9},{9,1},{17,25},{25,17},{2,10},{10... | collective-permute-start | bytes 3145736 | tf_op jit(solution)/shard_map/weight/ppermute | solution.py:20
  146.8 7.7 %collective-permute-start.9 = (bf16[8,128,512]{2,1,0:T(8,128)(2,1)S(1)}, bf16[8,128,512]{2,1,0:T(8,128)(2,1)S(1)}, u32[]{:S(2)}, u32[]{:S(2)}) collective-permute-start(bf16[8,128,512]{2,1,0:T(8,128)(2,1)S(1)} %constant_dynamic-slice_fusion.rest_0_), channel_id=1, source_target_pairs={{0,32},{32,0},{1,33},{33,1},{2,34},{34,2},{3,35},{35,3},{4,36},{36... | collective-permute-start | bytes 3145736 | tf_op jit(solution)/shard_map/weight/ppermute | solution.py:20
  148.2 6.2 %collective-permute-start.10 = (bf16[8,128,512]{2,1,0:T(8,128)(2,1)}, bf16[8,128,512]{2,1,0:T(8,128)(2,1)}, u32[]{:S(2)}, u32[]{:S(2)}) collective-permute-start(bf16[8,128,512]{2,1,0:T(8,128)(2,1)} %collective-permute-done.6.rest_2_), channel_id=1, source_target_pairs={{0,32},{32,0},{1,33},{33,1},{2,34},{34,2},{3,35},{35,3},{4,36},{36... | collective-permute-start | bytes 3145736 | tf_op jit(solution)/shard_map/weight/ppermute | solution.py:20
  148.2 6.2 %collective-permute-start.11 = (bf16[8,128,512]{2,1,0:T(8,128)(2,1)}, bf16[8,128,512]{2,1,0:T(8,128)(2,1)}, u32[]{:S(2)}, u32[]{:S(2)}) collective-permute-start(bf16[8,128,512]{2,1,0:T(8,128)(2,1)} %collective-permute-done.7.rest_4_), channel_id=1, source_target_pairs={{0,32},{32,0},{1,33},{33,1},{2,34},{34,2},{3,35},{35,3},{4,36},{36... | collective-permute-start | bytes 3145736 | tf_op jit(solution)/shard_map/weight/ppermute | solution.py:20
  148.7 6.6 %collective-permute-start.12 = (bf16[8,128,512]{2,1,0:T(8,128)(2,1)}, bf16[8,128,512]{2,1,0:T(8,128)(2,1)}, u32[]{:S(2)}, u32[]{:S(2)}) collective-permute-start(bf16[8,128,512]{2,1,0:T(8,128)(2,1)} %collective-permute-done.8.rest_6_), channel_id=1, source_target_pairs={{0,32},{32,0},{1,33},{33,1},{2,34},{34,2},{3,35},{35,3},{4,36},{36... | collective-permute-start | bytes 3145736 | tf_op jit(solution)/shard_map/weight/ppermute | solution.py:20
  149.4 9.9 %all-to-all-start.2 = ((f32[8,8,256]{2,1,0:T(8,128)}), f32[8,8,256]{2,1,0:T(8,128)S(1)}, u32[]{:S(2)}, u32[]{:S(2)}) async-start(f32[8,8,256]{2,1,0:T(8,128)} %broadcast_in_dim.4), calls=%async_computation.3 | async-start | bytes 131072 | tf_op jit(solution)/shard_map/left/all_to_all | solution.py:364
  163.5 5.0 %collective-permute-start.16 = (f32[32,576]{1,0:T(8,128)S(1)}, f32[32,576]{1,0:T(8,128)S(1)}, u32[]{:S(2)}, u32[]{:S(2)}) collective-permute-start(f32[32,576]{1,0:T(8,128)S(1)} %add.123), channel_id=1, source_target_pairs={{0,192},{64,128},{128,64},{192,0},{1,193},{65,129},{129,65},{193,1... | collective-permute-start | bytes 221192 | tf_op jit(solution)/shard_map/sums/ppermute | solution.py:20
  170.5 12.1 %collective-permute-start.19 = (f32[32,576]{1,0:T(8,128)S(1)}, f32[32,576]{1,0:T(8,128)S(1)}, u32[]{:S(2)}, u32[]{:S(2)}) collective-permute-start(f32[32,576]{1,0:T(8,128)S(1)} %add_add_fusion.1.refs_0_), channel_id=1, source_target_pairs={{0,24},{8,16},{16,8},{24,0},{1,25},{9,17},{17,9},{25,1},{2,26},{10... | collective-permute-start | bytes 221192 | tf_op jit(solution)/shard_map/sums/ppermute | solution.py:20
  173.0 9.6 %collective-permute-start.18 = (f32[32,576]{1,0:T(8,128)S(1)}, f32[32,576]{1,0:T(8,128)S(1)}, u32[]{:S(2)}, u32[]{:S(2)}) collective-permute-start(f32[32,576]{1,0:T(8,128)S(1)} %add_add_fusion.1.refs_0_), channel_id=1, source_target_pairs={{0,16},{8,24},{16,0},{24,8},{1,17},{9,25},{17,1},{25,9},{2,18},{10... | collective-permute-start | bytes 221192 | tf_op jit(solution)/shard_map/sums/ppermute | solution.py:20
  173.6 9.1 %collective-permute-start.17 = (f32[32,576]{1,0:T(8,128)S(1)}, f32[32,576]{1,0:T(8,128)S(1)}, u32[]{:S(2)}, u32[]{:S(2)}) collective-permute-start(f32[32,576]{1,0:T(8,128)S(1)} %add_add_fusion.1.refs_0_), channel_id=1, source_target_pairs={{0,8},{8,0},{16,24},{24,16},{1,9},{9,1},{17,25},{25,17},{2,10},{10... | collective-permute-start | bytes 221192 | tf_op jit(solution)/shard_map/sums/ppermute | solution.py:20
  186.2 8.5 %collective-permute-start.23 = (f32[32,576]{1,0:T(8,128)S(1)}, f32[32,576]{1,0:T(8,128)S(1)}, u32[]{:S(2)}, u32[]{:S(2)}) collective-permute-start(f32[32,576]{1,0:T(8,128)S(1)} %add.127), channel_id=1, source_target_pairs={{0,6},{1,7},{2,4},{3,5},{4,2},{5,3},{6,0},{7,1},{8,14},{9,15},{10,... | collective-permute-start | bytes 221192 | tf_op jit(solution)/shard_map/sums/ppermute | solution.py:20
  192.1 8.0 %collective-permute-start.22 = (f32[32,576]{1,0:T(8,128)S(1)}, f32[32,576]{1,0:T(8,128)S(1)}, u32[]{:S(2)}, u32[]{:S(2)}) collective-permute-start(f32[32,576]{1,0:T(8,128)S(1)} %add.127), channel_id=1, source_target_pairs={{0,4},{1,5},{2,6},{3,7},{4,0},{5,1},{6,2},{7,3},{8,12},{9,13},{10,... | collective-permute-start | bytes 221192 | tf_op jit(solution)/shard_map/sums/ppermute | solution.py:20
  193.1 7.0 %collective-permute-start.21 = (f32[32,576]{1,0:T(8,128)S(1)}, f32[32,576]{1,0:T(8,128)S(1)}, u32[]{:S(2)}, u32[]{:S(2)}) collective-permute-start(f32[32,576]{1,0:T(8,128)S(1)} %add.127), channel_id=1, source_target_pairs={{0,2},{1,3},{2,0},{3,1},{4,6},{5,7},{6,4},{7,5},{8,10},{9,11},{10,... | collective-permute-start | bytes 221192 | tf_op jit(solution)/shard_map/sums/ppermute | solution.py:20
  200.2 6.1 %collective-permute-start.24 = (f32[32,576]{1,0:T(8,128)S(1)}, f32[32,576]{1,0:T(8,128)S(1)}, u32[]{:S(2)}, u32[]{:S(2)}) collective-permute-start(f32[32,576]{1,0:T(8,128)S(1)} %add_add_fusion.mine), channel_id=1, source_target_pairs={{0,32},{32,0},{1,33},{33,1},{2,34},{34,2},{3,35},{35,3},{4,36},{36... | collective-permute-start | bytes 221192 | tf_op jit(solution)/shard_map/sums/ppermute | solution.py:20
  (19 other events, 492.6 us)
Sparse Core Ops, SparseCore 0:
  9.8 41.1 all-gather.2
  96.8 59.7 reduce-scatter.1

commit v8 on v7

--- a/solution.py
+++ b/solution.py
@@ -194,8 +194,10 @@
     )(place, q_start, error, cotangent, *pieces, activations, *pieces)
 
 
-def project_kernel(place, cot, *rest):
-    pieces, out, rows, arrived = rest[:NC * NX], rest[NC * NX], rest[NC * NX + 1], rest[NC * NX + 2]
+def project_kernel(first, place, cot, *rest):
+    count = NX // 2
+    pieces, refs = rest[:NC * count], rest[NC * count:]
+    out, flag, rows, arrived = refs[-4:]
     sub = pieces[0].shape[1]
     block = NC * sub
 
@@ -207,11 +209,12 @@
 
     @pl.when(pl.program_id(0) == 0)
     def _():
-        for k in range(NX):
+        flag[...] = jnp.zeros_like(flag)
+        for k in range(count):
             for c in range(NC):
                 fetch(k, c).start()
 
-    for k in range(NX):
+    for k in range(count):
         @pl.when(pl.program_id(0) == k)
         def _():
             for c in range(NC):
@@ -222,29 +225,37 @@
                 ).astype(BF16)
 
 
-def project(place, cot, pieces):
+def project(place, cot, pieces, first, earlier):
     tokens, width = cot.shape
     sub = pieces[0].shape[1]
+    count = NX // 2
     columns = NZ * NC * sub
     return pl.pallas_call(
-        project_kernel,
-        out_shape=jax.ShapeDtypeStruct((tokens, NX * columns), BF16),
+        functools.partial(project_kernel, first),
+        out_shape=(jax.ShapeDtypeStruct((tokens, NX * columns), BF16), jax.ShapeDtypeStruct((8, 128), F32)),
         grid_spec=pltpu.PrefetchScalarGridSpec(
             num_scalar_prefetch=1,
-            grid=(NX,),
+            grid=(count,),
             in_specs=[pl.BlockSpec((tokens, width), lambda k, place: (0, 0))]
-            + [pl.BlockSpec(memory_space=pltpu.HBM)] * (NC * NX),
-            out_specs=pl.BlockSpec((tokens, columns), lambda k, place: (0, k ^ place[0])),
-            scratch_shapes=[pltpu.VMEM((NX, NZ, NC * sub, width), BF16), pltpu.SemaphoreType.DMA((NC * NX,))],
-        ),
+            + [pl.BlockSpec(memory_space=pltpu.HBM)] * (NC * count + len(earlier)),
+            out_specs=(
+                pl.BlockSpec((tokens, columns), lambda k, place: (0, (first + k) ^ place[0])),
+                pl.BlockSpec((8, 128), lambda k, place: (0, 0)),
+            ),
+            scratch_shapes=[
+                pltpu.VMEM((count, NZ, NC * sub, width), BF16),
+                pltpu.SemaphoreType.DMA((NC * count,)),
+            ],
+        ),
+        input_output_aliases={2 + NC * count: 0} if earlier else {},
         cost_estimate=pl.CostEstimate(
-            flops=2 * tokens * width * NX * columns,
-            bytes_accessed=2 * (tokens + width) * NX * columns,
+            flops=2 * tokens * width * count * columns,
+            bytes_accessed=2 * (tokens + width) * count * columns,
             transcendentals=0,
         ),
         compiler_params=pltpu.CompilerParams(vmem_limit_bytes=62_000_000),
         name="project",
-    )(place, cot, *pieces)
+    )(place, cot, *pieces, *earlier)
 
 
 def right_kernel(place, _, gradient, error, p_total, merged_out, keep, give):
@@ -359,24 +370,25 @@
         left = left_terms(place, q_start, error, activations, cotangent, pieces)
         left = tree(list(lax.all_to_all(left, ("y", "c"), 0, 0, tiled=True)))
         left = tree(list(lax.all_to_all(left, "z", 0, 0, tiled=True)))
-        left, halves = lax.optimization_barrier((left, halves))
         left = jnp.broadcast_to(left[None], (NY * NC,) + left.shape)
         p_total = lax.all_to_all(left, ("y", "c"), 0, 0, tiled=True).reshape(q_start.shape[0], -1)
+        p_total, halves = lax.optimization_barrier((p_total, halves))
 
     with jax.named_scope("weight"):
         weights = []
         for half in halves:
             weights += [half, swap(half, "c", NC, 1)]
-        input_grad = project(place, cotangent, weights)
+        input_grad, flag = project(place, cotangent, weights[:NX], 0, ())
+        input_grad, last_flag = project(place, cotangent, weights[NX:], NX // 2, (input_grad,))
         swapped = tree([half[0, :16, :128] for half in weights[1::2]])
 
     with jax.named_scope("sums"):
         merged, keep, give = right_terms(place, swapped, gradient, error, p_total)
         keep = keep + swap(give, "c", NC, 1)
         keep = tree(swaps(keep, "y", NY))
-        keep = add_after(input_grad[:16, :128], swaps(keep, "x", NX))
+        keep = add_after(flag, swaps(keep, "x", NX))
         keep = keep + swap(keep, "z", NZ, 1)
-        keep = tree([keep] + [swap(keep, "z", NZ, k) for k in (2, 4, 6)])
+        keep = add_after(last_flag, [keep] + [swap(keep, "z", NZ, k) for k in (2, 4, 6)])
         other = swap(keep, "c", NC, 1)
 
     with jax.named_scope("finish"):

time: 219 us -> 232 us (1.059)
  waiting for transfers between devices: 87 us -> 102 us
  blocking collectives: 31.8 us -> 25.4 us
  Pallas kernels: 35.5 us -> 40.3 us
    ppermute x25, waiting for transfers between devices: 83.1 us -> 95.7 us  [swap(): return lax.ppermute(value, axis, [(i, i ^ k) for i in range(size)])]
    all_to_all x1, blocking collectives: 15.4 us -> 9.24 us  [local(): lax.all_to_all(left, ('y', 'c'), 0, 0, tiled=True)]
    pallas_call x1 -> x2, Pallas kernels: 8.08 us -> 12.2 us  [project(): pl.pallas_call(functools.partial(project_kernel, first), out_shape=(jax.S...]
    unnamed x30 -> x42, local copies, waits for them, and re-layouts: 4.14 us -> 6.59 us
  transfers between devices with their start and end apart: 28 -> 28, of which waited for: 16 -> 16; matrix products, arithmetic and copies ran while one was open for 2% -> 1% of each run, Pallas kernels for 13% -> 15%
where the time goes in v8:
time: 232 us; the launch traced here: 231 us
  waiting for transfers between devices  102 us (44%)
  starting transfers between devices  41.7 us (18%)
  Pallas kernels  40.3 us (17%)
  blocking collectives  25.4 us (11%)
  between operations  14.3 us (6%)
  local copies, waits for them, and re-layouts  7.75 us (3%)
    ppermute x25, waiting for transfers between devices, swap(): return lax.ppermute(value, axis, [(i, i ^ k) for i in range(size)])  95.7 us
    ppermute x25, starting transfers between devices, swap(): return lax.ppermute(value, axis, [(i, i ^ k) for i in range(size)])  36.4 us
    all_to_all x1, blocking collectives, local(): left = tree(list(lax.all_to_all(left, 'z', 0, 0, tiled=True)))  16.2 us
    pallas_call x2, Pallas kernels, project(): pl.pallas_call(functools.partial(project_kernel, first), out_shape=(jax.S...  12.2 us
    pallas_call x1, Pallas kernels, left_terms(): pl.pallas_call(functools.partial(left_kernel, 1 + len(pieces)), out_shape...  11.2 us
    all_to_all x1, blocking collectives, local(): lax.all_to_all(left, ('y', 'c'), 0, 0, tiled=True)  9.24 us
    pallas_call x1, Pallas kernels, gradient_terms(): pl.pallas_call(functools.partial(gradient_kernel, 1 + len(pieces)), out_s...  7.67 us
    unnamed x42, local copies, waits for them, and re-layouts  6.59 us
  transfers between devices with their start and end apart: 28, of which 16 were waited for; matrix products, arithmetic and copies ran while one was open for 1% of the time, Pallas kernels for 15%

profile of v8, /device:TPU:1, one launch (start us, length us, event | category | flops | bytes accessed | tf_op | source)
XLA Modules:
  0.0 231.1 jit_solution(16081222244980124653)
XLA Ops:
  9.0 2.8 %pack.1 = (bf16[160,2560]{1,0:T(8,128)(2,1)S(1)}, bf16[160,2560]{1,0:T(8,128)(2,1)S(1)}, bf16[160,2560]{1,0:T(8,128)(2,1)S(1)}, bf16[160,2560]{1,0:T(8,128)(2,1)...) custom-call(s32[6]{0:T(128)S(1)} %stack.27.place, bf16[320,8192]{1,0:T(8,128)(2,1)} %refs_7_.3, ...), custom_call_target="tpu_custom_call" | custom-call | bytes 5242880 | tf_op jit(solution)/shard_map/exchange/pack/pallas_call | solution.py:71
  11.8 3.7 %collective-permute-start = (bf16[160,2560]{1,0:T(8,128)(2,1)S(1)}, bf16[160,2560]{1,0:T(8,128)(2,1)S(1)}, u32[]{:S(2)}, u32[]{:S(2)}) collective-permute-start(bf16[160,2560]{1,0:T(8,128)(2,1)S(1)} %get-tuple-element.33), channel_id=1, source_target_pairs={{0,16},{8,24},{16,0},{24,8},{1,17},{9,25},{17,1},{25,9},{2,18},{10... | collective-permute-start | bytes 2457608 | tf_op jit(solution)/shard_map/exchange/ppermute | solution.py:20
  15.5 2.6 %collective-permute-start.2 = (bf16[160,2560]{1,0:T(8,128)(2,1)S(1)}, bf16[160,2560]{1,0:T(8,128)(2,1)S(1)}, u32[]{:S(2)}, u32[]{:S(2)}) collective-permute-start(bf16[160,2560]{1,0:T(8,128)(2,1)S(1)} %get-tuple-element.35), channel_id=1, source_target_pairs={{0,24},{8,16},{16,8},{24,0},{1,25},{9,17},{17,9},{25,1},{2,26},{10... | collective-permute-start | bytes 2457608 | tf_op jit(solution)/shard_map/exchange/ppermute | solution.py:20
  18.3 14.0 %collective-permute-done.refs_1_.refs_8_ = bf16[160,2560]{1,0:T(8,128)(2,1)S(1)} collective-permute-done((bf16[160,2560]{1,0:T(8,128)(2,1)S(1)}, bf16[160,2560]{1,0:T(8,128)(2,1)S(1)}, u32[]{:S(2)}, u32[]{:S(2)}) %collective-permute-start) | collective-permute-done | bytes 819232 | tf_op jit(solution)/shard_map/exchange/ppermute | solution.py:20
  34.7 15.3 %collective-permute-done.1.refs_2_.refs_9_ = bf16[160,2560]{1,0:T(8,128)(2,1)S(1)} collective-permute-done((bf16[160,2560]{1,0:T(8,128)(2,1)S(1)}, bf16[160,2560]{1,0:T(8,128)(2,1)S(1)}, u32[]{:S(2)}, u32[]{:S(2)}) %collective-permute-start.1) | collective-permute-done | bytes 819232 | tf_op jit(solution)/shard_map/exchange/ppermute | solution.py:20
  49.9 19.3 %collective-permute-done.2.refs_3_.refs_10_ = bf16[160,2560]{1,0:T(8,128)(2,1)S(1)} collective-permute-done((bf16[160,2560]{1,0:T(8,128)(2,1)S(1)}, bf16[160,2560]{1,0:T(8,128)(2,1)S(1)}, u32[]{:S(2)}, u32[]{:S(2)}) %collective-permute-start.2) | collective-permute-done | bytes 819232 | tf_op jit(solution)/shard_map/exchange/ppermute | solution.py:20
  69.3 17.6 %collective-permute-done.3.refs_4_.refs_11_ = bf16[160,2560]{1,0:T(8,128)(2,1)S(1)} collective-permute-done((bf16[160,2560]{1,0:T(8,128)(2,1)S(1)}, bf16[160,2560]{1,0:T(8,128)(2,1)S(1)}, u32[]{:S(2)}, u32[]{:S(2)}) %collective-permute-start.3) | collective-permute-done | bytes 819232 | tf_op jit(solution)/shard_map/exchange/ppermute | solution.py:20
  88.9 7.7 %gradient_terms.1 = f32[8,512,256]{2,1,0:T(8,128)} custom-call(s32[6]{0:T(128)S(1)} %stack.27.place, bf16[320,512]{1,0:T(8,128)(2,1)S(1)} %copy-done.3, bf16[160,2560]{1,0:T(8,128)(2,1)S(1)} %collective-permute-done.refs_1_.refs_8_, bf16[160,2560]{1,0:T(8,128)(2,1)S(1)} %collective-permute-done.1.refs_2_.refs_9_, bf16[160,2560]{1,0:T(8,128)(2,1)} %copy-done.11, ...), custom_call_target="tpu_custom_call" | custom-call | flops 2684354560 | bytes 9437184 | tf_op jit(solution)/shard_map/gradient/gradient_terms/pallas_call | solution.py:146
  96.7 11.2 %left_terms.1 = f32[8,8,8,256]{3,2,1,0:T(8,128)} custom-call(s32[6]{0:T(128)S(1)} %stack.27.place, f32[64,512]{1,0:T(8,128)S(1)} %copy-done.6, f32[256,512]{1,0:T(8,128)S(1)} %bitcast.16, bf16[320,512]{1,0:T(8,128)(2,1)S(1)} %copy-done.3, bf16[160,2560]{1,0:T(8,128)(2,1)} %copy-done, bf16[160,2560]{1,0:T(8,128)(2,1)} %copy-done.1, ...), custom_call_target="tpu_custom_call" | custom-call | flops 1006632960 | bytes 5242880 | tf_op jit(solution)/shard_map/left/left_terms/pallas_call | solution.py:173
  108.0 5.2 %all-to-all-start = ((f32[8,8,8,256]{3,2,1,0:T(8,128)}), f32[8,8,8,256]{3,2,1,0:T(8,128)S(1)}, u32[]{:S(2)}, u32[]{:S(2)}) async-start(f32[8,8,8,256]{3,2,1,0:T(8,128)} %left_terms.1), calls=%async_computation | async-start | bytes 1048576 | tf_op jit(solution)/shard_map/left/all_to_all | solution.py:371
  114.2 2.5 %collective-permute-start.8 = (bf16[8,128,512]{2,1,0:T(8,128)(2,1)}, bf16[8,128,512]{2,1,0:T(8,128)(2,1)S(1)}, u32[]{:S(2)}, u32[]{:S(2)}) collective-permute-start(bf16[8,128,512]{2,1,0:T(8,128)(2,1)} %constant_dynamic-slice_fusion.rest_0_), channel_id=1, source_target_pairs={{0,24},{8,16},{16,8},{24,0},{1,25},{9,17},{17,9},{25,1},{2,26},{10... | collective-permute-start | bytes 3145736 | tf_op jit(solution)/shard_map/weight/ppermute | solution.py:20
  117.5 5.3 %all-to-all-done = f32[8,8,8,256]{3,2,1,0:T(8,128)S(1)} async-done(((f32[8,8,8,256]{3,2,1,0:T(8,128)}), f32[8,8,8,256]{3,2,1,0:T(8,128)S(1)}, u32[]{:S(2)}, u32[]{:S(2)}) %all-to-all-start) | async-done | bytes 524320 | tf_op jit(solution)/shard_map/left/all_to_all | solution.py:371
  122.8 16.2 %all_to_all.15 = f32[8,8,256]{2,1,0:T(8,128)S(1)} all-to-all(f32[8,8,256]{2,1,0:T(8,128)S(1)} %fusion.2), channel_id=1, replica_groups=mesh['y'=4,'c'=2,'x'=4,'z'=8] {'z'}, dimensions={0} | all-to-all | bytes 131072 | tf_op jit(solution)/shard_map/left/all_to_all | solution.py:372
  138.9 9.2 %all_to_all.16 = f32[8,8,256]{2,1,0:T(8,128)S(1)} all-to-all(f32[8,8,256]{2,1,0:T(8,128)S(1)} %broadcast_in_dim.12), channel_id=1, replica_groups=mesh['y'=4,'c'=2,'x'=4,'z'=8] {'y','c'}, dimensions={0} | all-to-all | bytes 131072 | tf_op jit(solution)/shard_map/left/all_to_all | solution.py:374
  148.2 14.7 %collective-permute-done.8.rest_2_ = bf16[8,128,512]{2,1,0:T(8,128)(2,1)S(1)} collective-permute-done((bf16[8,128,512]{2,1,0:T(8,128)(2,1)}, bf16[8,128,512]{2,1,0:T(8,128)(2,1)S(1)}, u32[]{:S(2)}, u32[]{:S(2)}) %collective-permute-start.8) | collective-permute-done | bytes 1048608 | tf_op jit(solution)/shard_map/weight/ppermute | solution.py:20
  164.9 3.4 %collective-permute-done.9.rest_1_ = bf16[8,128,512]{2,1,0:T(8,128)(2,1)S(1)} collective-permute-done((bf16[8,128,512]{2,1,0:T(8,128)(2,1)}, bf16[8,128,512]{2,1,0:T(8,128)(2,1)S(1)}, u32[]{:S(2)}, u32[]{:S(2)}) %collective-permute-start.9) | collective-permute-done | bytes 1048608 | tf_op jit(solution)/shard_map/weight/ppermute | solution.py:20
  176.2 2.7 %collective-permute-start.16 = (f32[32,576]{1,0:T(8,128)S(1)}, f32[32,576]{1,0:T(8,128)S(1)}, u32[]{:S(2)}, u32[]{:S(2)}) collective-permute-start(f32[32,576]{1,0:T(8,128)S(1)} %add.111), channel_id=1, source_target_pairs={{0,192},{64,128},{128,64},{192,0},{1,193},{65,129},{129,65},{193,1... | collective-permute-start | bytes 221192 | tf_op jit(solution)/shard_map/sums/ppermute | solution.py:20
  179.6 2.5 %collective-permute-done.16 = f32[32,576]{1,0:T(8,128)S(1)} collective-permute-done((f32[32,576]{1,0:T(8,128)S(1)}, f32[32,576]{1,0:T(8,128)S(1)}, u32[]{:S(2)}, u32[]{:S(2)}) %collective-permute-start.16) | collective-permute-done | bytes 73760 | tf_op jit(solution)/shard_map/sums/ppermute | solution.py:20
  183.7 2.6 %collective-permute-start.19 = (f32[32,576]{1,0:T(8,128)S(1)}, f32[32,576]{1,0:T(8,128)S(1)}, u32[]{:S(2)}, u32[]{:S(2)}) collective-permute-start(f32[32,576]{1,0:T(8,128)S(1)} %add_add_fusion.refs_0_), channel_id=1, source_target_pairs={{0,24},{8,16},{16,8},{24,0},{1,25},{9,17},{17,9},{25,1},{2,26},{10... | collective-permute-start | bytes 221192 | tf_op jit(solution)/shard_map/sums/ppermute | solution.py:20
  187.1 6.1 %project.2 = (bf16[320,8192]{1,0:T(8,128)(2,1)}, f32[8,128]{1,0:T(8,128)}) custom-call(s32[6]{0:T(128)} %copy-done.7, bf16[320,512]{1,0:T(8,128)(2,1)} %cot.5, bf16[8,128,512]{2,1,0:T(8,128)(2,1)} %constant_dynamic-slice_fusion.rest_0_, bf16[8,128,512]{2,1,0:T(8,128)(2,1)} %copy-done.19, bf16[8,128,512]{2,1,0:T(8,128)(2,1)} %collective-permute-done.6.rest_2_, ...), custom_call_target="tpu_custom_call" | custom-call | flops 1342177280 | bytes 6815744 | tf_op jit(solution)/shard_map/weight/project/pallas_call | solution.py:233
  197.3 5.9 %collective-permute-start.23 = (f32[32,576]{1,0:T(8,128)S(1)}, f32[32,576]{1,0:T(8,128)S(1)}, u32[]{:S(2)}, u32[]{:S(2)}) collective-permute-start(f32[32,576]{1,0:T(8,128)S(1)} %add.115.refs_0_), channel_id=1, source_target_pairs={{0,6},{1,7},{2,4},{3,5},{4,2},{5,3},{6,0},{7,1},{8,14},{9,15},{10,... | collective-permute-start | bytes 221192 | tf_op jit(solution)/shard_map/sums/ppermute | solution.py:20
  205.4 6.1 %project.3 = (bf16[320,8192]{1,0:T(8,128)(2,1)}, f32[8,128]{1,0:T(8,128)}) custom-call(s32[6]{0:T(128)} %copy-done.7, bf16[320,512]{1,0:T(8,128)(2,1)} %cot.5, bf16[8,128,512]{2,1,0:T(8,128)(2,1)} %collective-permute-done.7.rest_0_, bf16[8,128,512]{2,1,0:T(8,128)(2,1)} %copy-done.15, ...), custom_call_target="tpu_custom_call", output_to_operand_aliasing={{0}: (6, {})} | custom-call | flops 1342177280 | bytes 6815744 | tf_op jit(solution)/shard_map/weight/project/pallas_call | solution.py:233
  212.3 5.8 %collective-permute-start.24 = (f32[32,576]{1,0:T(8,128)S(1)}, f32[32,576]{1,0:T(8,128)S(1)}, u32[]{:S(2)}, u32[]{:S(2)}) collective-permute-start(f32[32,576]{1,0:T(8,128)S(1)} %add_after.3.mine), channel_id=1, source_target_pairs={{0,32},{32,0},{1,33},{33,1},{2,34},{34,2},{3,35},{35,3},{4,36},{36... | collective-permute-start | bytes 221192 | tf_op jit(solution)/shard_map/sums/ppermute | solution.py:20
  219.0 5.3 %finish.1 = (f32[256,512]{1,0:T(8,128)}, f32[256,512]{1,0:T(8,128)}, f32[64,512]{1,0:T(8,128)}) custom-call(s32[6]{0:T(128)S(1)} %copy-done.8, f32[32,576]{1,0:T(8,128)S(1)} %add_after.3.mine, f32[32,576]{1,0:T(8,128)S(1)} %collective-permute-done.24.other, f32[64,256]{1,0:T(8,128)S(1)} %bitcast.19, f32[256,512]{1,0:T(8,128)S(1)} %get-tuple-element.58.merged), custom_call_target="tpu_custom_call" | custom-call | tf_op jit(solution)/shard_map/finish/finish/pallas_call | solution.py:337
  (96 shorter events, 29.4 us)
Async XLA Ops:
  7.2 89.5 %all-gather.3.cloned.1.call-start = ((), (), s32[]{:S(2)}) async-start(), calls=%async_computation.5 | async-start | bytes 2359296 | tf_op jit(solution)/shard_map/exchange/all_gather | solution.py:357
  7.9 164.6 %reduce-scatter.2.cloned.1.call-start = ((), (), s32[]{:S(2)}) async-start(), calls=%async_computation.4 | async-start | bytes 4718592 | tf_op jit(solution)/shard_map/gradient/reduce_scatter | solution.py:364
  11.8 20.6 %collective-permute-start = (bf16[160,2560]{1,0:T(8,128)(2,1)S(1)}, bf16[160,2560]{1,0:T(8,128)(2,1)S(1)}, u32[]{:S(2)}, u32[]{:S(2)}) collective-permute-start(bf16[160,2560]{1,0:T(8,128)(2,1)S(1)} %get-tuple-element.33), channel_id=1, source_target_pairs={{0,16},{8,24},{16,0},{24,8},{1,17},{9,25},{17,1},{25,9},{2,18},{10... | collective-permute-start | bytes 2457608 | tf_op jit(solution)/shard_map/exchange/ppermute | solution.py:20
  15.4 34.5 %collective-permute-start.1 = (bf16[160,2560]{1,0:T(8,128)(2,1)S(1)}, bf16[160,2560]{1,0:T(8,128)(2,1)S(1)}, u32[]{:S(2)}, u32[]{:S(2)}) collective-permute-start(bf16[160,2560]{1,0:T(8,128)(2,1)S(1)} %get-tuple-element.34), channel_id=1, source_target_pairs={{0,16},{8,24},{16,0},{24,8},{1,17},{9,25},{17,1},{25,9},{2,18},{10... | collective-permute-start | bytes 2457608 | tf_op jit(solution)/shard_map/exchange/ppermute | solution.py:20
  15.5 53.7 %collective-permute-start.2 = (bf16[160,2560]{1,0:T(8,128)(2,1)S(1)}, bf16[160,2560]{1,0:T(8,128)(2,1)S(1)}, u32[]{:S(2)}, u32[]{:S(2)}) collective-permute-start(bf16[160,2560]{1,0:T(8,128)(2,1)S(1)} %get-tuple-element.35), channel_id=1, source_target_pairs={{0,24},{8,16},{16,8},{24,0},{1,25},{9,17},{17,9},{25,1},{2,26},{10... | collective-permute-start | bytes 2457608 | tf_op jit(solution)/shard_map/exchange/ppermute | solution.py:20
  18.1 68.7 %collective-permute-start.3 = (bf16[160,2560]{1,0:T(8,128)(2,1)S(1)}, bf16[160,2560]{1,0:T(8,128)(2,1)S(1)}, u32[]{:S(2)}, u32[]{:S(2)}) collective-permute-start(bf16[160,2560]{1,0:T(8,128)(2,1)S(1)} %get-tuple-element.36), channel_id=1, source_target_pairs={{0,24},{8,16},{16,8},{24,0},{1,25},{9,17},{17,9},{25,1},{2,26},{10... | collective-permute-start | bytes 2457608 | tf_op jit(solution)/shard_map/exchange/ppermute | solution.py:20
  18.2 68.6 %collective-permute-start.4 = (bf16[160,2560]{1,0:T(8,128)(2,1)S(1)}, bf16[160,2560]{1,0:T(8,128)(2,1)S(1)}, u32[]{:S(2)}, u32[]{:S(2)}) collective-permute-start(bf16[160,2560]{1,0:T(8,128)(2,1)S(1)} %get-tuple-element.37), channel_id=1, source_target_pairs={{0,8},{8,0},{16,24},{24,16},{1,9},{9,1},{17,25},{25,17},{2,10},{10... | collective-permute-start | bytes 2457608 | tf_op jit(solution)/shard_map/exchange/ppermute | solution.py:20
  32.4 54.4 %collective-permute-start.5 = (bf16[160,2560]{1,0:T(8,128)(2,1)S(1)}, bf16[160,2560]{1,0:T(8,128)(2,1)S(1)}, u32[]{:S(2)}, u32[]{:S(2)}) collective-permute-start(bf16[160,2560]{1,0:T(8,128)(2,1)S(1)} %get-tuple-element.38), channel_id=1, source_target_pairs={{0,8},{8,0},{16,24},{24,16},{1,9},{9,1},{17,25},{25,17},{2,10},{10... | collective-permute-start | bytes 2457608 | tf_op jit(solution)/shard_map/exchange/ppermute | solution.py:20
  108.0 14.8 %all-to-all-start = ((f32[8,8,8,256]{3,2,1,0:T(8,128)}), f32[8,8,8,256]{3,2,1,0:T(8,128)S(1)}, u32[]{:S(2)}, u32[]{:S(2)}) async-start(f32[8,8,8,256]{3,2,1,0:T(8,128)} %left_terms.1), calls=%async_computation | async-start | bytes 1048576 | tf_op jit(solution)/shard_map/left/all_to_all | solution.py:371
  114.2 48.7 %collective-permute-start.8 = (bf16[8,128,512]{2,1,0:T(8,128)(2,1)}, bf16[8,128,512]{2,1,0:T(8,128)(2,1)S(1)}, u32[]{:S(2)}, u32[]{:S(2)}) collective-permute-start(bf16[8,128,512]{2,1,0:T(8,128)(2,1)} %constant_dynamic-slice_fusion.rest_0_), channel_id=1, source_target_pairs={{0,24},{8,16},{16,8},{24,0},{1,25},{9,17},{17,9},{25,1},{2,26},{10... | collective-permute-start | bytes 3145736 | tf_op jit(solution)/shard_map/weight/ppermute | solution.py:20
  116.7 46.2 %collective-permute-start.7 = (bf16[8,128,512]{2,1,0:T(8,128)(2,1)}, bf16[8,128,512]{2,1,0:T(8,128)(2,1)}, u32[]{:S(2)}, u32[]{:S(2)}) collective-permute-start(bf16[8,128,512]{2,1,0:T(8,128)(2,1)} %constant_dynamic-slice_fusion.rest_0_), channel_id=1, source_target_pairs={{0,16},{8,24},{16,0},{24,8},{1,17},{9,25},{17,1},{25,9},{2,18},{10... | collective-permute-start | bytes 3145736 | tf_op jit(solution)/shard_map/weight/ppermute | solution.py:20
  117.2 46.1 %collective-permute-start.6 = (bf16[8,128,512]{2,1,0:T(8,128)(2,1)}, bf16[8,128,512]{2,1,0:T(8,128)(2,1)}, u32[]{:S(2)}, u32[]{:S(2)}) collective-permute-start(bf16[8,128,512]{2,1,0:T(8,128)(2,1)} %constant_dynamic-slice_fusion.rest_0_), channel_id=1, source_target_pairs={{0,8},{8,0},{16,24},{24,16},{1,9},{9,1},{17,25},{25,17},{2,10},{10... | collective-permute-start | bytes 3145736 | tf_op jit(solution)/shard_map/weight/ppermute | solution.py:20
  163.3 5.1 %collective-permute-start.9 = (bf16[8,128,512]{2,1,0:T(8,128)(2,1)}, bf16[8,128,512]{2,1,0:T(8,128)(2,1)S(1)}, u32[]{:S(2)}, u32[]{:S(2)}) collective-permute-start(bf16[8,128,512]{2,1,0:T(8,128)(2,1)} %collective-permute-done.7.rest_0_), channel_id=1, source_target_pairs={{0,32},{32,0},{1,33},{33,1},{2,34},{34,2},{3,35},{35,3},{4,36},{36... | collective-permute-start | bytes 3145736 | tf_op jit(solution)/shard_map/weight/ppermute | solution.py:20
  164.4 5.2 %collective-permute-start.10 = (bf16[8,128,512]{2,1,0:T(8,128)(2,1)S(1)}, bf16[8,128,512]{2,1,0:T(8,128)(2,1)S(1)}, u32[]{:S(2)}, u32[]{:S(2)}) collective-permute-start(bf16[8,128,512]{2,1,0:T(8,128)(2,1)S(1)} %collective-permute-done.8.rest_2_), channel_id=1, source_target_pairs={{0,32},{32,0},{1,33},{33,1},{2,34},{34,2},{3,35},{35,3},{4,36},{36... | collective-permute-start | bytes 3145736 | tf_op jit(solution)/shard_map/weight/ppermute | solution.py:20
  164.4 5.5 %collective-permute-start.11 = (bf16[8,128,512]{2,1,0:T(8,128)(2,1)}, bf16[8,128,512]{2,1,0:T(8,128)(2,1)S(1)}, u32[]{:S(2)}, u32[]{:S(2)}) collective-permute-start(bf16[8,128,512]{2,1,0:T(8,128)(2,1)} %constant_dynamic-slice_fusion.rest_0_), channel_id=1, source_target_pairs={{0,32},{32,0},{1,33},{33,1},{2,34},{34,2},{3,35},{35,3},{4,36},{36... | collective-permute-start | bytes 3145736 | tf_op jit(solution)/shard_map/weight/ppermute | solution.py:20
  164.9 6.5 %collective-permute-start.12 = (bf16[8,128,512]{2,1,0:T(8,128)(2,1)}, bf16[8,128,512]{2,1,0:T(8,128)(2,1)S(1)}, u32[]{:S(2)}, u32[]{:S(2)}) collective-permute-start(bf16[8,128,512]{2,1,0:T(8,128)(2,1)} %collective-permute-done.6.rest_2_), channel_id=1, source_target_pairs={{0,32},{32,0},{1,33},{33,1},{2,34},{34,2},{3,35},{35,3},{4,36},{36... | collective-permute-start | bytes 3145736 | tf_op jit(solution)/shard_map/weight/ppermute | solution.py:20
  176.2 5.9 %collective-permute-start.16 = (f32[32,576]{1,0:T(8,128)S(1)}, f32[32,576]{1,0:T(8,128)S(1)}, u32[]{:S(2)}, u32[]{:S(2)}) collective-permute-start(f32[32,576]{1,0:T(8,128)S(1)} %add.111), channel_id=1, source_target_pairs={{0,192},{64,128},{128,64},{192,0},{1,193},{65,129},{129,65},{193,1... | collective-permute-start | bytes 221192 | tf_op jit(solution)/shard_map/sums/ppermute | solution.py:20
  183.7 9.5 %collective-permute-start.19 = (f32[32,576]{1,0:T(8,128)S(1)}, f32[32,576]{1,0:T(8,128)S(1)}, u32[]{:S(2)}, u32[]{:S(2)}) collective-permute-start(f32[32,576]{1,0:T(8,128)S(1)} %add_add_fusion.refs_0_), channel_id=1, source_target_pairs={{0,24},{8,16},{16,8},{24,0},{1,25},{9,17},{17,9},{25,1},{2,26},{10... | collective-permute-start | bytes 221192 | tf_op jit(solution)/shard_map/sums/ppermute | solution.py:20
  186.3 6.9 %collective-permute-start.18 = (f32[32,576]{1,0:T(8,128)S(1)}, f32[32,576]{1,0:T(8,128)S(1)}, u32[]{:S(2)}, u32[]{:S(2)}) collective-permute-start(f32[32,576]{1,0:T(8,128)S(1)} %add_add_fusion.refs_0_), channel_id=1, source_target_pairs={{0,16},{8,24},{16,0},{24,8},{1,17},{9,25},{17,1},{25,9},{2,18},{10... | collective-permute-start | bytes 221192 | tf_op jit(solution)/shard_map/sums/ppermute | solution.py:20
  186.8 6.4 %collective-permute-start.17 = (f32[32,576]{1,0:T(8,128)S(1)}, f32[32,576]{1,0:T(8,128)S(1)}, u32[]{:S(2)}, u32[]{:S(2)}) collective-permute-start(f32[32,576]{1,0:T(8,128)S(1)} %add_add_fusion.refs_0_), channel_id=1, source_target_pairs={{0,8},{8,0},{16,24},{24,16},{1,9},{9,1},{17,25},{25,17},{2,10},{10... | collective-permute-start | bytes 221192 | tf_op jit(solution)/shard_map/sums/ppermute | solution.py:20
  197.3 14.2 %collective-permute-start.23 = (f32[32,576]{1,0:T(8,128)S(1)}, f32[32,576]{1,0:T(8,128)S(1)}, u32[]{:S(2)}, u32[]{:S(2)}) collective-permute-start(f32[32,576]{1,0:T(8,128)S(1)} %add.115.refs_0_), channel_id=1, source_target_pairs={{0,6},{1,7},{2,4},{3,5},{4,2},{5,3},{6,0},{7,1},{8,14},{9,15},{10,... | collective-permute-start | bytes 221192 | tf_op jit(solution)/shard_map/sums/ppermute | solution.py:20
  203.2 8.3 %collective-permute-start.22 = (f32[32,576]{1,0:T(8,128)S(1)}, f32[32,576]{1,0:T(8,128)S(1)}, u32[]{:S(2)}, u32[]{:S(2)}) collective-permute-start(f32[32,576]{1,0:T(8,128)S(1)} %add.115.refs_0_), channel_id=1, source_target_pairs={{0,4},{1,5},{2,6},{3,7},{4,0},{5,1},{6,2},{7,3},{8,12},{9,13},{10,... | collective-permute-start | bytes 221192 | tf_op jit(solution)/shard_map/sums/ppermute | solution.py:20
  204.4 7.1 %collective-permute-start.21 = (f32[32,576]{1,0:T(8,128)S(1)}, f32[32,576]{1,0:T(8,128)S(1)}, u32[]{:S(2)}, u32[]{:S(2)}) collective-permute-start(f32[32,576]{1,0:T(8,128)S(1)} %add.115.refs_0_), channel_id=1, source_target_pairs={{0,2},{1,3},{2,0},{3,1},{4,6},{5,7},{6,4},{7,5},{8,10},{9,11},{10,... | collective-permute-start | bytes 221192 | tf_op jit(solution)/shard_map/sums/ppermute | solution.py:20
  212.3 6.7 %collective-permute-start.24 = (f32[32,576]{1,0:T(8,128)S(1)}, f32[32,576]{1,0:T(8,128)S(1)}, u32[]{:S(2)}, u32[]{:S(2)}) collective-permute-start(f32[32,576]{1,0:T(8,128)S(1)} %add_after.3.mine), channel_id=1, source_target_pairs={{0,32},{32,0},{1,33},{33,1},{2,34},{34,2},{3,35},{35,3},{4,36},{36... | collective-permute-start | bytes 221192 | tf_op jit(solution)/shard_map/sums/ppermute | solution.py:20
  (25 other events, 646.2 us)
Sparse Core Ops, SparseCore 0:
  9.8 41.1 all-gather.2
  96.8 59.7 reduce-scatter.1
